TPU v7x, 512 devices: a whole 4x8x8 slice. The times are simulated.
512 devices in a mesh: replica: 64 (over x, y, core), tensor: 8 (over z).
Axes of the slice: x: 4, y: 8, z: 8, core: 2. Of those that a mesh axis runs over, the one named last changes fastest.
Arguments:
- tokens: bfloat16 [32768, 1024], P('replica'), may hold values from -6 to 6
- w_in: bfloat16 [1024, 8, 512], P(None, 'tensor'), may hold values from -0.1875 to 0.1875
- w_out: bfloat16 [8, 128, 1024], P('tensor'), may hold values from -0.1875 to 0.1875
- cache_keys: bfloat16 [64, 1024, 8, 128], P('replica', None, 'tensor'), may hold values from -6 to 6
- cache_values: bfloat16 [64, 1024, 8, 128], P('replica', None, 'tensor'), may hold values from -6 to 6
- session_slot: int32 [64], replicated, may hold values from 0 to 63, as said below
- request_session: int32 [4096], P('replica'), may hold values from 0 to 63, as said below
- cand_count: int32 [4096], P('replica'), may hold values from 1 to 8
- hist_len: int32 [64], replicated, may hold values from 256 to 1024
Outputs:
- mixed: bfloat16 [32768, 1024], P(('replica', 'tensor'))
Inputs may be any that keep to these rules, and one draw needn't show every extreme that they name: `session_slot`: a permutation of the cache rows; cache row p lies on replica index p. `request_session`: the 64 requests of one replica index name sessions on at most 2 requests per owning replica index; some owning replica index holds the sessions of exactly 2 requests of every replica index.
All inputs are finite; a program needn't handle non-finite values.
Results may differ from a plain program's by a relative error of at most 0.01.
Values may be sent and summed in bfloat16 or wider, within the bound.
No kernel may reach another device: no remote copies, remote signals or barrier semaphores. Data moves between devices by JAX's collectives and lax.ppermute only.
A program may use at most 64 MiB of HBM per device.

v0:
```python
import jax
import jax.numpy as jnp
from jax import lax
from jax.sharding import PartitionSpec as P

epsilon = 1e-05


def layer_norm(values):
    average = jnp.mean(values, -1, keepdims=True)
    centred = values - average
    return centred * lax.rsqrt(jnp.mean(centred * centred, -1, keepdims=True) + epsilon)


def on_device(
    tokens,
    w_in,
    w_out,
    cache_keys,
    cache_values,
    session_slot,
    request_session,
    cand_count,
    hist_len,
):
    replicas = lax.axis_size("replica")
    my_index = lax.axis_index("replica")
    tok_rows, model_width = tokens.shape
    local_heads = w_in.shape[1]
    head_dim = w_in.shape[2] // 4
    requests = request_session.shape[0]
    cands = tok_rows // requests
    sess_local = cache_keys.shape[0]
    history = cache_keys.shape[1]
    capacity = max(2, (2 * requests + replicas - 1) // replicas)
    slot_total = replicas * capacity
    score_scale = head_dim ** (-0.5)
    inputs = tokens.astype(jnp.float32)
    normed = layer_norm(inputs).astype(jnp.bfloat16)
    projected = jax.nn.silu(
        jnp.dot(normed, w_in.reshape(model_width, -1), preferred_element_type=jnp.float32)
    ).astype(jnp.bfloat16)
    projected = projected.reshape(requests, cands, local_heads, 4 * head_dim)
    gate_units = projected[..., :head_dim]
    cand_values = projected[..., head_dim : 2 * head_dim]
    queries = projected[..., 2 * head_dim : 3 * head_dim]
    cand_keys = projected[..., 3 * head_dim :]
    owner_row = jnp.take(session_slot, request_session)
    target = owner_row // sess_local
    lengths = jnp.take(hist_len, request_session)
    positions = jnp.arange(requests, dtype=jnp.int32)
    earlier = (target[:, None] == target[None, :]) & (positions[None, :] < positions[:, None])
    within_rank = jnp.sum(earlier.astype(jnp.int32), 1)
    slot_index = target * capacity + within_rank
    chosen = jnp.arange(slot_total, dtype=jnp.int32)[:, None] == slot_index[None, :]
    chosen_bf = chosen.astype(jnp.bfloat16)
    chosen_int = chosen.astype(jnp.int32)
    sent_queries = jnp.dot(
        chosen_bf, queries.reshape(requests, -1), preferred_element_type=jnp.float32
    )
    sent_queries = sent_queries.astype(jnp.bfloat16).reshape(
        replicas, capacity, cands, local_heads * head_dim
    )
    sent_session = jnp.sum(chosen_int * request_session[None, :], 1).reshape(replicas, capacity)
    sent_count = jnp.sum(chosen_int * cand_count[None, :], 1).reshape(replicas, capacity)
    got_queries = lax.all_to_all(sent_queries, "replica", split_axis=0, concat_axis=0, tiled=True)
    got_session = lax.all_to_all(sent_session, "replica", split_axis=0, concat_axis=0, tiled=True)
    got_count = lax.all_to_all(sent_count, "replica", split_axis=0, concat_axis=0, tiled=True)
    sources, held = got_session.shape
    row_total = sources * held * cands
    query_rows = got_queries.reshape(row_total, local_heads, head_dim)
    row_session = jnp.repeat(got_session.reshape(-1), cands, total_repeat_length=row_total)
    row_limit = jnp.repeat(got_count.reshape(-1), cands, total_repeat_length=row_total)
    row_place = jnp.tile(jnp.arange(cands, dtype=jnp.int32), sources * held)
    row_local = jnp.take(session_slot, row_session) - my_index * sess_local
    row_length = jnp.take(hist_len, row_session)
    key_block = min(512, history)
    history_sum = jnp.zeros((row_total, local_heads, head_dim), jnp.float32)
    row_match = row_local == 0
    key_rows = cache_keys[0]
    value_rows = cache_values[0]

    def add_block(block_step, running):
        key_piece = lax.dynamic_slice_in_dim(key_rows, block_step * key_block, key_block, 0)
        value_piece = lax.dynamic_slice_in_dim(value_rows, block_step * key_block, key_block, 0)
        scores = (
            jnp.einsum("rhd,jhd->hrj", query_rows, key_piece, preferred_element_type=jnp.float32)
            * score_scale
        )
        key_place = block_step * key_block + jnp.arange(key_block, dtype=jnp.int32)
        visible = row_match[None, :, None] & (key_place[None, None, :] < row_length[None, :, None])
        weights = (jax.nn.silu(scores) * visible.astype(jnp.float32)).astype(jnp.bfloat16)
        return running + jnp.einsum(
            "hrj,jhd->rhd", weights, value_piece, preferred_element_type=jnp.float32
        )

    history_sum = lax.fori_loop(0, history // key_block, add_block, history_sum)
    keep_rows = (row_place < row_limit).astype(jnp.float32)
    scaled = history_sum / (row_length + 1).astype(jnp.float32)[:, None, None]
    answers = (scaled * keep_rows[:, None, None]).astype(jnp.bfloat16)
    answers = answers.reshape(sources, held, cands, local_heads * head_dim)
    returned = lax.all_to_all(answers, "replica", split_axis=0, concat_axis=0, tiled=True)
    hist_part = jnp.dot(
        chosen_bf.T, returned.reshape(slot_total, -1), preferred_element_type=jnp.float32
    )
    hist_part = hist_part.reshape(requests, cands, local_heads, head_dim)
    own_scores = (
        jnp.sum(queries.astype(jnp.float32) * cand_keys.astype(jnp.float32), -1, keepdims=True)
        * score_scale
    )
    own_term = (
        jax.nn.silu(own_scores)
        * cand_values.astype(jnp.float32)
        / (lengths + 1).astype(jnp.float32)[:, None, None, None]
    )
    alive_rows = (jnp.arange(cands, dtype=jnp.int32)[None, :] < cand_count[:, None]).astype(
        jnp.float32
    )
    attended = (hist_part + own_term) * alive_rows[:, :, None, None]
    gated = (layer_norm(attended) * gate_units.astype(jnp.float32)).astype(jnp.bfloat16)
    gated = gated.reshape(tok_rows, local_heads * head_dim)
    groups = lax.axis_size("tensor")
    group_index = lax.axis_index("tensor")
    row_share = tok_rows // groups
    my_tokens = lax.dynamic_slice_in_dim(inputs, group_index * row_share, row_share, 0)
    out_flat = w_out.reshape(local_heads * head_dim, model_width)
    summed = lax.psum_scatter(
        jnp.dot(gated, out_flat, preferred_element_type=jnp.float32).astype(jnp.bfloat16),
        "tensor",
        scatter_dimension=0,
        tiled=True,
    ).astype(jnp.float32)
    return (my_tokens + summed).astype(jnp.bfloat16)


def solution(mesh):
    in_specs = (
        P("replica", None),
        P(None, "tensor", None),
        P("tensor", None, None),
        P("replica", None, "tensor", None),
        P("replica", None, "tensor", None),
        P(),
        P("replica"),
        P("replica"),
        P(),
    )
    out_specs = P(("replica", "tensor"), None)
    return jax.shard_map(
        on_device, mesh=mesh, in_specs=in_specs, out_specs=out_specs, check_vma=False
    )
```

profile of v0, /device:TPU:6, one launch (start us, length us, event | category | flops | bytes accessed | tf_op | source)
XLA Modules:
  0.0 247.1 jit_solution(4662050947131647567)
XLA Ops:
  6.5 0.8 compare_select_fusion.2
  7.4 1.4 gather_fusion.3
  8.8 1.4 gather_fusion
  10.2 1.2 fusion.56
  11.6 0.8 select_reduce_fusion
  12.4 0.8 all_to_all.21
  13.1 10.8 %all-to-all-start.2 = ((s32[64,1,2]{2,1,0:T(1,128)}), s32[64,1,2]{2,1,0:T(1,128)S(1)}, u32[]{:S(2)}, u32[]{:S(2)}) async-start(s32[64,1,2]{2,1,0:T(1,128)} %bitcast.136), calls=%async_computation.2 | async-start | bytes 65536 | tf_op jit(solution)/shard_map/all_to_all | solution.py:68
  24.0 2.1 fusion.60
  26.0 2.1 fusion.59
  28.1 2.1 fusion.58
  30.2 2.1 fusion.64
  32.3 2.1 fusion.63
  34.3 2.1 fusion.62
  36.4 1.4 convert_reduce_fusion
  37.9 0.4 multiply_reduce_fusion
  38.3 0.9 fusion.36
  39.2 0.7 fusion.57
  40.0 0.3 fusion.27
  40.4 0.7 fusion.61
  41.1 0.7 all_to_all.18
  41.8 10.5 %all-to-all-start = ((s32[64,1,2]{2,1,0:T(1,128)}), s32[64,1,2]{2,1,0:T(1,128)}, u32[]{:S(2)}, u32[]{:S(2)}) async-start(s32[64,1,2]{2,1,0:T(1,128)} %bitcast.3), calls=%async_computation | async-start | bytes 65536 | tf_op jit(solution)/shard_map/all_to_all | solution.py:67
  52.4 0.7 fusion.65
  53.1 0.6 tile.4
  53.7 0.9 tile.10
  54.6 0.7 copy.45
  55.3 0.5 broadcast.961
  55.9 1.4 reduce.13
  57.4 6.6 %gather_fusion.2 = s32[1024]{0:T(1024)S(1)} fusion(s32[128]{0:T(128)S(1)} %reshape.257, s32[1024]{0:T(1024)S(1)} %fusion.50), kind=kCustom, calls=%fused_computation.3.clone | custom fusion | bytes 12288 | tf_op jit(solution)/shard_map/jit(_take)/gather | solution.py:73
  64.0 10.5 %all-to-all-start.1 = ((bf16[64,2,8,128]{3,2,1,0:T(8,128)(2,1)}), bf16[64,2,8,128]{3,2,1,0:T(8,128)(2,1)}, u32[]{:S(2)}, u32[]{:S(2)}) async-start(bf16[64,2,8,128]{3,2,1,0:T(8,128)(2,1)} %bitcast.156), calls=%async_computation.1 | async-start | bytes 524288 | tf_op jit(solution)/shard_map/all_to_all | solution.py:66
  74.6 1.4 reduce.12
  76.2 6.6 %gather_fusion.1 = s32[1024]{0:T(1024)S(1)} fusion(s32[128]{0:T(128)S(1)} %reshape.251, s32[1024]{0:T(1024)S(1)} %fusion.50), kind=kCustom, calls=%fused_computation.1.clone | custom fusion | bytes 12288 | tf_op jit(solution)/shard_map/jit(_take)/gather | solution.py:72
  82.8 40.9 %add_convert_fusion.1 = (f32[1024]{0:T(1024)S(1)}, s32[1024]{0:T(1024)}, pred[1024]{0:T(1024)(128)(4,1)S(1)}, pred[1024]{0:T(1024)(128)(4,1)S(1)}, pred[1024]{0:...) fusion(s32[]{:T(128)} %bitcast.131, ...), kind=kLoop, calls=%fused_computation.75 | loop fusion | flops 147456 | bytes 82208 | tf_op jit(solution)/shard_map/convert_element_type | solution.py:99
  123.7 39.9 %fusion.49 = pred[1024]{0:T(1024)(128)(4,1)S(1)} fusion(pred[1024]{0:T(1024)(128)(4,1)S(1)} %get-tuple-element.258, pred[1024]{0:T(1024)(128)(4,1)S(1)} %get-tuple-element.257, pred[1024]{0:T(1024)(128)(4,1)S(1)} %get-tuple-element.256, pred[1024]{0:T(1024)(128)(4,1)S(1)} %get-tuple-element.255, pred[1024]{0:T(1024)(128)(4,1)S(1)} %get-tuple-element.254, ...), kind=kLoop, calls=%fused_computation.71 | loop fusion | flops 67584 | bytes 66820 | tf_op jit(solution)/shard_map/eq | solution.py:79
  163.6 4.7 %while.16 = (s32[]{:T(128)}, f32[1024,1,128]{0,2,1:T(8,128)S(1)}, bf16[1024,1,128]{2,0,1:T(8,128)(2,1)}, pred[1024]{0:T(1024)(128)(4,1)S(1)}, s32[1024]{0:T(1024...) while((s32[]{:T(128)}, f32[1024,1,128]{0,2,1:T(8,128)S(1)}, ...), condition=%wide.region_5.9_spmd.clone, body=%wide.region_4.8_spmd.clone.sunk | while | flops 273416704 | bytes 1583792 | solution.py:97
  163.6 2.3 fusion.75
  166.0 2.3 fusion.75
  168.3 0.8 copy-done.4
  169.1 1.3 copy.35
  170.4 1.0 multiply_convert_fusion.7
  171.4 10.5 %all-to-all-start.3 = ((bf16[64,2,8,128]{3,2,1,0:T(8,128)(2,1)}), bf16[64,2,8,128]{3,2,1,0:T(8,128)(2,1)S(1)}, u32[]{:S(2)}, u32[]{:S(2)}) async-start(bf16[64,2,8,128]{3,2,1,0:T(8,128)(2,1)} %bitcast.137), calls=%async_computation.3 | async-start | bytes 524288 | tf_op jit(solution)/shard_map/all_to_all | solution.py:102
  182.2 11.3 %all-to-all-done.3 = bf16[64,2,8,128]{3,2,1,0:T(8,128)(2,1)S(1)} async-done(((bf16[64,2,8,128]{3,2,1,0:T(8,128)(2,1)}), bf16[64,2,8,128]{3,2,1,0:T(8,128)(2,1)S(1)}, u32[]{:S(2)}, u32[]{:S(2)}) %all-to-all-start.3) | async-done | bytes 262176 | tf_op jit(solution)/shard_map/all_to_all | solution.py:102
  193.7 0.4 fusion.66
  194.1 0.3 multiply_reduce_fusion.1
  194.3 0.2 multiply_convert_fusion.8
  194.6 1.4 convolution_convert_fusion
  196.0 1.6 convert_element_type.71
  197.6 40.9 %reduce-scatter.2.cloned.1.call-done = bf16[64,1024]{1,0:T(8,128)(2,1)} async-done(((bf16[512,1024]{1,0:T(8,128)(2,1)}), bf16[64,1024]{1,0:T(8,128)(2,1)}) %reduce-scatter.2.cloned.1.call-update) | async-done | bytes 131088 | tf_op jit(solution)/shard_map/reduce_scatter | solution.py:127
  238.5 1.7 add_convert_fusion
  (51 shorter events, 1.2 us)
Async XLA Ops:
  6.5 31.7 %copy-start = (bf16[1024,1,512]{2,0,1:T(8,128)(2,1)S(1)}, bf16[1024,1,512]{2,0,1:T(8,128)(2,1)}, u32[]{:S(2)}) copy-start(bf16[1024,1,512]{2,0,1:T(8,128)(2,1)} %param.22) | copy-start | bytes 3145732
  6.5 31.3 %copy-start.3 = (bf16[512,1024]{1,0:T(8,128)(2,1)S(1)}, bf16[512,1024]{1,0:T(8,128)(2,1)}, u32[]{:S(2)}) copy-start(bf16[512,1024]{1,0:T(8,128)(2,1)} %param.21) | copy-start | bytes 3145732
  11.6 28.4 %copy-start.9 = (s32[64]{0:T(128)}, s32[64]{0:T(128)S(1)}, u32[]{:S(2)}) copy-start(s32[64]{0:T(128)S(1)} %multiply_add_fusion) | copy-start | bytes 772
  13.1 28.7 %all-to-all-start.2 = ((s32[64,1,2]{2,1,0:T(1,128)}), s32[64,1,2]{2,1,0:T(1,128)S(1)}, u32[]{:S(2)}, u32[]{:S(2)}) async-start(s32[64,1,2]{2,1,0:T(1,128)} %bitcast.136), calls=%async_computation.2 | async-start | bytes 65536 | tf_op jit(solution)/shard_map/all_to_all | solution.py:68
  38.3 2.0 copy-start.8
  38.3 2.1 copy-start.1
  38.3 14.0 %copy-start.2 = (s32[64]{0:T(128)S(1)}, s32[64]{0:T(128)}, u32[]{:S(2)}) copy-start(s32[64]{0:T(128)} %param.29) | copy-start | bytes 772
  41.8 11.2 %copy-start.6 = (s32[64,1,2]{2,1,0:T(1,128)}, s32[64,1,2]{2,1,0:T(1,128)S(1)}, u32[]{:S(2)}) copy-start(s32[64,1,2]{2,1,0:T(1,128)S(1)} %all-to-all-done.2) | copy-start | bytes 1540
  41.8 22.2 %all-to-all-start = ((s32[64,1,2]{2,1,0:T(1,128)}), s32[64,1,2]{2,1,0:T(1,128)}, u32[]{:S(2)}, u32[]{:S(2)}) async-start(s32[64,1,2]{2,1,0:T(1,128)} %bitcast.3), calls=%async_computation | async-start | bytes 65536 | tf_op jit(solution)/shard_map/all_to_all | solution.py:67
  64.0 99.6 %all-to-all-start.1 = ((bf16[64,2,8,128]{3,2,1,0:T(8,128)(2,1)}), bf16[64,2,8,128]{3,2,1,0:T(8,128)(2,1)}, u32[]{:S(2)}, u32[]{:S(2)}) async-start(bf16[64,2,8,128]{3,2,1,0:T(8,128)(2,1)} %bitcast.156), calls=%async_computation.1 | async-start | bytes 524288 | tf_op jit(solution)/shard_map/all_to_all | solution.py:66
  168.3 0.8 copy-start.4
  169.1 13.1 %copy-start.11 = (s32[64]{0:T(128)S(1)}, s32[64]{0:T(128)}, u32[]{:S(2)}) copy-start(s32[64]{0:T(128)} %param.28) | copy-start | bytes 772
  169.1 24.6 %copy-start.7 = (bf16[64,8,1,128]{3,1,0,2:T(8,128)(2,1)S(1)}, bf16[64,8,1,128]{3,1,0,2:T(8,128)(2,1)}, u32[]{:S(2)}) copy-start(bf16[64,8,1,128]{3,1,0,2:T(8,128)(2,1)} %get-tuple-element.260) | copy-start | bytes 393220
  169.1 24.6 %copy-start.10 = (s32[64]{0:T(128)S(1)}, s32[64]{0:T(128)}, u32[]{:S(2)}) copy-start(s32[64]{0:T(128)} %copy-done.9) | copy-start | bytes 772
  169.1 24.6 %copy-start.12 = (f32[64]{0:T(128)S(1)}, f32[64]{0:T(128)}, u32[]{:S(2)}) copy-start(f32[64]{0:T(128)} %get-tuple-element.262) | copy-start | bytes 772
  171.4 23.1 %copy-start.5 = (bf16[1,128,1024]{2,1,0:T(8,128)(2,1)S(1)}, bf16[1,128,1024]{2,1,0:T(8,128)(2,1)}, u32[]{:S(2)}) copy-start(bf16[1,128,1024]{2,1,0:T(8,128)(2,1)} %param.23) | copy-start | bytes 786436
  171.4 22.0 %all-to-all-start.3 = ((bf16[64,2,8,128]{3,2,1,0:T(8,128)(2,1)}), bf16[64,2,8,128]{3,2,1,0:T(8,128)(2,1)S(1)}, u32[]{:S(2)}, u32[]{:S(2)}) async-start(bf16[64,2,8,128]{3,2,1,0:T(8,128)(2,1)} %bitcast.137), calls=%async_computation.3 | async-start | bytes 524288 | tf_op jit(solution)/shard_map/all_to_all | solution.py:102
  181.9 56.6 %reduce-scatter.2.cloned.1.call-start = ((), (), s32[]{:S(2)}) async-start(), calls=%async_computation.5 | async-start | bytes 1179648 | tf_op jit(solution)/shard_map/reduce_scatter | solution.py:127
Sparse Core Ops, SparseCore 0:
  196.1 42.3 reduce-scatter.1
where the time goes:
time: 249 us; the launch traced here: 247 us
  other arithmetic  93.6 us (38%)
  waiting for transfers between devices  52.2 us (21%)
  starting transfers between devices  42.3 us (17%)
  local copies, waits for them, and re-layouts  37.5 us (15%)
  between operations  13.7 us (6%)
  matrix products  7.61 us (3%)
    convert_element_type x1, other arithmetic, on_device(): scaled = history_sum / (row_length + 1).astype(jnp.float32)[:, None, None]  40.9 us
    reduce_scatter x1, waiting for transfers between devices, on_device(): lax.psum_scatter(jnp.dot(gated, out_flat, preferred_element_type=jnp.floa...  40.9 us
    eq x1, other arithmetic, on_device(): row_match = row_local == 0  39.9 us
    all_to_all x1, waiting for transfers between devices, on_device(): lax.all_to_all(answers, 'replica', split_axis=0, concat_axis=0, tiled=True)  11.3 us
    all_to_all x1, starting transfers between devices, on_device(): lax.all_to_all(sent_count, 'replica', split_axis=0, concat_axis=0, tiled=...  10.8 us
    all_to_all x1, starting transfers between devices, on_device(): lax.all_to_all(sent_queries, 'replica', split_axis=0, concat_axis=0, tile...  10.5 us
    all_to_all x1, starting transfers between devices, on_device(): lax.all_to_all(sent_session, 'replica', split_axis=0, concat_axis=0, tile...  10.5 us
    all_to_all x1, starting transfers between devices, on_device(): lax.all_to_all(answers, 'replica', split_axis=0, concat_axis=0, tiled=True)  10.5 us
  transfers between devices with their start and end apart: 5, of which 2 were waited for; matrix products, arithmetic and copies ran while one was open for 48% of the time, Pallas kernels for 0%

commit v1 on v0

v1 whole, which is shorter than its diff:
```python
import functools

import jax
import jax.numpy as jnp
from jax import lax
from jax.experimental import pallas as pl
from jax.experimental.pallas import tpu as pltpu
from jax.sharding import PartitionSpec as P

epsilon = 1e-05
f32 = jnp.float32
bf16 = jnp.bfloat16


def layer_norm(values):
    average = jnp.mean(values, -1, keepdims=True)
    centred = values - average
    return centred * lax.rsqrt(jnp.mean(centred * centred, -1, keepdims=True) + epsilon)


def silu(values):
    half = values * 0.5
    return half + half * jnp.tanh(half)


def iota(shape, dimension):
    return lax.broadcasted_iota(jnp.int32, shape, dimension)


def to_column(row):
    n = row.shape[1]
    return jnp.sum(jnp.where(iota((n, n), 0) == iota((n, n), 1), row, 0.0), 1, keepdims=True)


def lookup(table_row, index_row):
    sessions, requests = table_row.shape[1], index_row.shape[1]
    named = iota((sessions, requests), 0) == index_row
    return jnp.sum(jnp.where(named, to_column(table_row.astype(f32)), 0.0), 0, keepdims=True)


def first_rows(slot_ref, session_ref, capacity, cands):
    owner = lookup(slot_ref[...], session_ref[...])
    requests = owner.shape[1]
    square = (requests, requests)
    earlier = (to_column(owner) == owner) & (iota(square, 0) < iota(square, 1))
    rank = jnp.sum(jnp.where(earlier, 1.0, 0.0), 0, keepdims=True)
    return (owner * capacity + rank) * cands


def send_kernel(capacity, cands, tokens_ref, w_ref, slot_ref, session_ref, sent_ref):
    rows = tokens_ref.shape[0]
    head_dim = w_ref.shape[1]
    slot_rows = sent_ref.shape[0]
    normed = layer_norm(tokens_ref[...].astype(f32)).astype(bf16)
    queries = silu(jnp.dot(normed, w_ref[...], preferred_element_type=f32)).astype(bf16)
    first = first_rows(slot_ref, session_ref, capacity, cands)
    requests = first.shape[1]
    spread = iota((requests, rows), 1) // cands == iota((requests, rows), 0)
    place = jnp.sum(jnp.where(spread, to_column(first), 0.0), 0, keepdims=True).astype(jnp.int32)
    place = place + iota((1, rows), 1) % cands
    chosen = jnp.where(iota((slot_rows, rows), 0) == place, 1.0, 0.0).astype(bf16)
    sent_ref[...] = jnp.dot(chosen, queries, preferred_element_type=f32).astype(bf16)


def local_kernel(
    capacity, cands, tokens_ref, w_ref, slot_ref, session_ref, count_ref, length_ref, own_ref, gate_ref, back_ref
):
    rows = tokens_ref.shape[0]
    head_dim = own_ref.shape[1]
    slot_rows = back_ref.shape[1]
    normed = layer_norm(tokens_ref[...].astype(f32)).astype(bf16)
    projected = silu(jnp.dot(normed, w_ref[...], preferred_element_type=f32)).astype(bf16).astype(f32)
    gate = projected[:, :head_dim]
    values = projected[:, head_dim : 2 * head_dim]
    queries = projected[:, 2 * head_dim : 3 * head_dim]
    keys = projected[:, 3 * head_dim :]
    first = first_rows(slot_ref, session_ref, capacity, cands)
    lengths = lookup(length_ref[...], session_ref[...])
    requests = first.shape[1]
    spread = iota((rows, requests), 0) // cands == iota((rows, requests), 1)

    def per_row(row):
        return jnp.sum(jnp.where(spread, row, 0.0), 1, keepdims=True)

    within = iota((rows, 1), 0) % cands
    place = per_row(first).astype(jnp.int32) + within
    back_ref[...] = jnp.where(iota((rows, slot_rows), 1) == place, 1.0, 0.0).astype(bf16)
    scores = jnp.sum(queries * keys, -1, keepdims=True) * head_dim ** (-0.5)
    own_ref[...] = silu(scores) * values / (per_row(lengths) + 1.0)
    alive = within.astype(f32) < per_row(count_ref[...].astype(f32))
    gate_ref[...] = jnp.where(alive, gate, 0.0).astype(bf16)


def history_kernel(block, me_ref, query_ref, keys_ref, values_ref, slot_ref, length_ref, out_ref):
    history, head_dim = keys_ref.shape
    mine = slot_ref[...] == me_ref[0]
    length = jnp.sum(jnp.where(mine, length_ref[...].astype(f32), 0.0), 1, keepdims=True)
    seen = iota((history, 1), 0).astype(f32) < length
    values = jnp.where(seen, values_ref[...], jnp.zeros((), bf16))
    keys = keys_ref[...]
    half_scale = 0.5 * head_dim ** (-0.5)
    for start in range(0, query_ref.shape[0], block):
        half = (
            lax.dot_general(
                query_ref[pl.ds(start, block), :], keys, (((1,), (1,)), ((), ())), preferred_element_type=f32
            )
            * half_scale
        )
        weights = (half + half * jnp.tanh(half)).astype(bf16)
        summed = jnp.dot(weights, values, preferred_element_type=f32)
        out_ref[pl.ds(start, block), :] = (summed / (length + 1.0)).astype(bf16)


def gate_kernel(returned_ref, back_ref, own_ref, gate_ref, out_ref):
    part = jnp.dot(back_ref[...], returned_ref[...], preferred_element_type=f32)
    out_ref[...] = (layer_norm(part + own_ref[...]) * gate_ref[...].astype(f32)).astype(bf16)


def output_kernel(group_ref, gated_ref, w_ref, tokens_ref, out_ref):
    total = tokens_ref[...].astype(f32)
    for head in range(gated_ref.shape[0]):
        total = total + jnp.dot(gated_ref[head], w_ref[head], preferred_element_type=f32)
    out_ref[...] = total.astype(bf16)


VMEM = pl.BlockSpec(memory_space=pltpu.VMEM)
SMEM = pl.BlockSpec(memory_space=pltpu.SMEM)
params = pltpu.CompilerParams(vmem_limit_bytes=40 * 1024 * 1024)


def on_device(
    tokens,
    w_in,
    w_out,
    cache_keys,
    cache_values,
    session_slot,
    request_session,
    cand_count,
    hist_len,
):
    replicas = lax.axis_size("replica")
    groups = lax.axis_size("tensor")
    my_index = lax.axis_index("replica").astype(jnp.int32).reshape(1)
    group_index = lax.axis_index("tensor").astype(jnp.int32).reshape(1)
    rows, model_width = tokens.shape
    head_dim = w_in.shape[2] // 4
    requests = request_session.shape[0]
    cands = rows // requests
    history = cache_keys.shape[1]
    capacity = max(2, (2 * requests + replicas - 1) // replicas)
    slot_rows = replicas * capacity * cands
    w_flat = w_in.reshape(model_width, 4 * head_dim)
    slots = session_slot.reshape(1, -1)
    lengths = hist_len.reshape(1, -1)
    named = request_session.reshape(1, -1)
    counts = cand_count.reshape(1, -1)
    w_whole = lax.all_gather(w_out, "tensor", axis=0, tiled=True)

    sent = pl.pallas_call(
        functools.partial(send_kernel, capacity, cands),
        grid=(1,),
        in_specs=[
            pl.BlockSpec((rows, model_width), lambda i: (0, 0)),
            pl.BlockSpec((model_width, head_dim), lambda i: (0, 2)),
            pl.BlockSpec((1, slots.shape[1]), lambda i: (0, 0)),
            pl.BlockSpec((1, requests), lambda i: (0, 0)),
        ],
        out_specs=pl.BlockSpec((slot_rows, head_dim), lambda i: (0, 0)),
        out_shape=jax.ShapeDtypeStruct((slot_rows, head_dim), bf16),
        compiler_params=params,
        name="send",
    )(tokens, w_flat, slots, named)
    got = lax.all_to_all(
        sent.reshape(replicas, capacity * cands, head_dim), "replica", split_axis=0, concat_axis=0, tiled=True
    )
    own, gate, back = pl.pallas_call(
        functools.partial(local_kernel, capacity, cands),
        in_specs=[VMEM] * 6,
        out_specs=[VMEM] * 3,
        out_shape=[
            jax.ShapeDtypeStruct((rows, head_dim), f32),
            jax.ShapeDtypeStruct((rows, head_dim), bf16),
            jax.ShapeDtypeStruct((rows, slot_rows), bf16),
        ],
        compiler_params=params,
        cost_estimate=pl.CostEstimate(
            flops=2 * rows * model_width * 4 * head_dim, bytes_accessed=4 << 20, transcendentals=rows * 4 * head_dim
        ),
        name="local",
    )(tokens, w_flat, slots, named, counts, lengths)
    answers = pl.pallas_call(
        functools.partial(history_kernel, min(256, slot_rows)),
        in_specs=[SMEM] + [VMEM] * 5,
        out_specs=VMEM,
        out_shape=jax.ShapeDtypeStruct((slot_rows, head_dim), bf16),
        compiler_params=params,
        name="history",
    )(
        my_index,
        got.reshape(slot_rows, head_dim),
        cache_keys.reshape(history, head_dim),
        cache_values.reshape(history, head_dim),
        slots,
        lengths,
    )
    returned = lax.all_to_all(
        answers.reshape(replicas, capacity * cands, head_dim), "replica", split_axis=0, concat_axis=0, tiled=True
    )
    gated = pl.pallas_call(
        gate_kernel,
        in_specs=[VMEM] * 4,
        out_specs=VMEM,
        out_shape=jax.ShapeDtypeStruct((rows, head_dim), bf16),
        compiler_params=params,
        name="gate",
    )(returned.reshape(slot_rows, head_dim), back, own, gate)
    share = rows // groups
    heads = lax.all_to_all(
        gated.reshape(groups, share, head_dim), "tensor", split_axis=0, concat_axis=0, tiled=True
    )
    return pl.pallas_call(
        output_kernel,
        grid_spec=pltpu.PrefetchScalarGridSpec(
            num_scalar_prefetch=1,
            grid=(1,),
            in_specs=[
                pl.BlockSpec((groups, share, head_dim), lambda i, g: (0, 0, 0)),
                pl.BlockSpec((groups, head_dim, model_width), lambda i, g: (0, 0, 0)),
                pl.BlockSpec((share, model_width), lambda i, g: (g[0], 0)),
            ],
            out_specs=pl.BlockSpec((share, model_width), lambda i, g: (0, 0)),
        ),
        out_shape=jax.ShapeDtypeStruct((share, model_width), bf16),
        compiler_params=params,
        name="output",
    )(group_index, heads, w_whole, tokens)


def solution(mesh):
    in_specs = (
        P("replica", None),
        P(None, "tensor", None),
        P("tensor", None, None),
        P("replica", None, "tensor", None),
        P("replica", None, "tensor", None),
        P(),
        P("replica"),
        P("replica"),
        P(),
    )
    out_specs = P(("replica", "tensor"), None)
    return jax.shard_map(
        on_device, mesh=mesh, in_specs=in_specs, out_specs=out_specs, check_vma=False
    )
```

time: 249 us -> 88.1 us (0.35)
  other arithmetic: 93.6 us -> 0 us
  local copies, waits for them, and re-layouts: 37.5 us -> 7.02 us
  waiting for transfers between devices: 52.2 us -> 30.9 us
  starting transfers between devices: 42.3 us -> 27.6 us
  Pallas kernels: 0 us -> 8.65 us
  matrix products: 7.61 us -> 0 us
    convert_element_type x8 -> x0, other arithmetic: 46.8 us -> none  [the longest x1 40.9 us: on_device(): scaled = history_sum / (row_length + 1).astype(jnp.float32)[:, None, None]]
    reduce_scatter x1 -> x0, waiting for transfers between devices: 40.9 us -> none  [on_device(): lax.psum_scatter(jnp.dot(gated, out_flat, preferred_element_type=jnp.floa...]
    eq x1 -> x0, other arithmetic: 39.9 us -> none  [on_device(): row_match = row_local == 0]
    gather x12 -> x0, local copies, waits for them, and re-layouts: 29.8 us -> none  [the longest x4 6.9 us: on_device(): row_local = jnp.take(session_slot, row_session) - my_index * sess_local]
    all_to_all x4 -> x3, waiting for transfers between devices: 11.3 us -> 30.2 us  [the longest x1 11.6 us: on_device(): lax.all_to_all(sent.reshape(replicas, capacity * cands, head_dim), 'repli...]
    all_to_all x4 -> x3, starting transfers between devices: 42.3 us -> 27.6 us  [the longest x1 10.8 us: on_device(): lax.all_to_all(sent.reshape(replicas, capacity * cands, head_dim), 'repli...]
    pallas_call x0 -> x5, Pallas kernels: none -> 8.65 us  [the longest x1 2.43 us: on_device(): pl.pallas_call(functools.partial(send_kernel, capacity, cands), grid=(1,)...]
    dot_general x6 -> x0, matrix products: 7.61 us -> none  [the longest x2 4.61 us: add_block(): jnp.einsum('hrj,jhd->rhd', weights, value_piece, preferred_element_type=j...]
  transfers between devices with their start and end apart: 5 -> 4, of which waited for: 2 -> 3; matrix products, arithmetic and copies ran while one was open for 48% -> 0% of each run, Pallas kernels for 0% -> 6%
where the time goes in v1:
time: 88.1 us; the launch traced here: 87.7 us
  waiting for transfers between devices  30.9 us (35%)
  starting transfers between devices  27.6 us (31%)
  between operations  13.5 us (15%)
  Pallas kernels  8.65 us (10%)
  local copies, waits for them, and re-layouts  7.02 us (8%)
    all_to_all x1, waiting for transfers between devices, on_device(): lax.all_to_all(sent.reshape(replicas, capacity * cands, head_dim), 'repli...  11.6 us
    all_to_all x1, starting transfers between devices, on_device(): lax.all_to_all(sent.reshape(replicas, capacity * cands, head_dim), 'repli...  10.8 us
    all_to_all x1, starting transfers between devices, on_device(): lax.all_to_all(gated.reshape(groups, share, head_dim), 'tensor', split_ax...  10.3 us
    all_to_all x1, waiting for transfers between devices, on_device(): lax.all_to_all(gated.reshape(groups, share, head_dim), 'tensor', split_ax...  9.37 us
    all_to_all x1, waiting for transfers between devices, on_device(): lax.all_to_all(answers.reshape(replicas, capacity * cands, head_dim), 're...  9.26 us
    unnamed x30, local copies, waits for them, and re-layouts  7.02 us
    all_to_all x1, starting transfers between devices, on_device(): lax.all_to_all(answers.reshape(replicas, capacity * cands, head_dim), 're...  6.47 us
    pallas_call x1, Pallas kernels, on_device(): pl.pallas_call(functools.partial(send_kernel, capacity, cands), grid=(1,)...  2.43 us
  transfers between devices with their start and end apart: 4, of which 3 were waited for; matrix products, arithmetic and copies ran while one was open for 0% of the time, Pallas kernels for 6%

profile of v1, /device:TPU:6, one launch (start us, length us, event | category | flops | bytes accessed | tf_op | source)
XLA Modules:
  0.0 87.7 jit_solution(12229742971572516298)
XLA Ops:
  6.5 0.0 copy-start.10
  6.5 0.0 copy-start.11
  6.5 0.0 copy-start.5
  6.5 0.0 all-gather.2.cloned.1.call-start
  6.5 0.7 all-gather.2.cloned.1.call-update
  7.3 0.0 copy-start
  7.3 1.2 %copy-done = bf16[512,1024]{1,0:T(8,128)(2,1)S(1)} copy-done((bf16[512,1024]{1,0:T(8,128)(2,1)S(1)}, bf16[512,1024]{1,0:T(8,128)(2,1)}, u32[]{:S(2)}) %copy-start) | copy-done | bytes 1048600
  8.5 0.0 copy-start.2
  8.5 1.2 %copy-done.2 = bf16[1024,1,512]{2,0,1:T(8,128)(2,1)S(1)} copy-done((bf16[1024,1,512]{2,0,1:T(8,128)(2,1)S(1)}, bf16[1024,1,512]{2,0,1:T(8,128)(2,1)}, u32[]{:S(2)}) %copy-start.2) | copy-done | bytes 1048600
  9.7 0.0 copy-start.9
  9.7 0.7 copy-done.9
  10.4 0.0 copy-start.12
  10.4 0.7 copy-done.12
  11.0 0.0 copy-start.6
  11.0 0.0 copy-start.1
  11.0 0.0 copy-start.3
  11.0 0.0 copy-start.13
  11.0 0.0 copy-start.14
  11.0 2.4 %send.1 = bf16[1024,128]{1,0:T(8,128)(2,1)} custom-call(bf16[512,1024]{1,0:T(8,128)(2,1)S(1)} %copy-done, bf16[1024,512]{1,0:T(8,128)(2,1)S(1)} %bitcast.14, s32[1,64]{1,0:T(1,128)S(1)} %bitcast.20, s32[1,64]{1,0:T(1,128)S(1)} %bitcast.25), custom_call_target="tpu_custom_call" | custom-call | tf_op jit(solution)/shard_map/send/pallas_call | solution.py:160
  13.5 10.8 %all-to-all-start = ((bf16[64,16,128]{2,1,0:T(8,128)(2,1)}), bf16[64,16,128]{2,1,0:T(8,128)(2,1)S(1)}, u32[]{:S(2)}, u32[]{:S(2)}) async-start(bf16[64,16,128]{2,1,0:T(8,128)(2,1)} %bitcast.5), calls=%async_computation | async-start | bytes 524288 | tf_op jit(solution)/shard_map/all_to_all | solution.py:174
  24.3 11.6 %all-to-all-done = bf16[64,16,128]{2,1,0:T(8,128)(2,1)S(1)} async-done(((bf16[64,16,128]{2,1,0:T(8,128)(2,1)}), bf16[64,16,128]{2,1,0:T(8,128)(2,1)S(1)}, u32[]{:S(2)}, u32[]{:S(2)}) %all-to-all-start) | async-done | bytes 262176 | tf_op jit(solution)/shard_map/all_to_all | solution.py:174
  35.8 0.0 copy-done.10
  35.9 0.0 copy-done.11
  35.9 0.0 copy-done.5
  35.9 0.0 copy-done.6
  35.9 2.3 %history.1 = bf16[1024,128]{1,0:T(8,128)(2,1)} custom-call(s32[1]{0:T(128)} %bitcast.1.me_ref, bf16[1024,128]{1,0:T(8,128)(2,1)S(1)} %bitcast.16, bf16[1024,128]{1,0:T(8,128)(2,1)S(1)} %bitcast.18, bf16[1024,128]{1,0:T(8,128)(2,1)S(1)} %bitcast.19, s32[1,64]{1,0:T(1,128)S(1)} %bitcast.21, s32[1,64]{1,0:T(1,128)S(1)} %bitcast.23), custom_call_target="tpu_custom_call" | custom-call | tf_op jit(solution)/shard_map/history/pallas_call | solution.py:192
  38.2 6.5 %all-to-all-start.1 = ((bf16[64,16,128]{2,1,0:T(8,128)(2,1)}), bf16[64,16,128]{2,1,0:T(8,128)(2,1)S(1)}, u32[]{:S(2)}, u32[]{:S(2)}) async-start(bf16[64,16,128]{2,1,0:T(8,128)(2,1)} %bitcast.10), calls=%async_computation.1 | async-start | bytes 524288 | tf_op jit(solution)/shard_map/all_to_all | solution.py:207
  44.7 0.0 copy-done.1
  44.7 0.0 copy-done.3
  44.7 0.0 copy-done.13
  44.7 0.0 copy-done.14
  44.7 1.5 %local.1 = (f32[512,128]{1,0:T(8,128)S(1)}, bf16[512,128]{1,0:T(8,128)(2,1)S(1)}, bf16[512,1024]{1,0:T(8,128)(2,1)S(1)}) custom-call(bf16[512,1024]{1,0:T(8,128)(2,1)S(1)} %copy-done.1, bf16[1024,512]{1,0:T(8,128)(2,1)S(1)} %bitcast.15, s32[1,64]{1,0:T(1,128)S(1)} %bitcast.22, s32[1,64]{1,0:T(1,128)S(1)} %bitcast.26, s32[1,64]{1,0:T(1,128)S(1)} %bitcast.27, ...), custom_call_target="tpu_custom_call" | custom-call | flops 536870912 | bytes 4194304 | tf_op jit(solution)/shard_map/local/pallas_call | solution.py:177
  46.3 0.0 copy-start.7
  46.3 0.7 copy-done.7
  47.0 9.3 %all-to-all-done.1 = bf16[64,16,128]{2,1,0:T(8,128)(2,1)S(1)} async-done(((bf16[64,16,128]{2,1,0:T(8,128)(2,1)}), bf16[64,16,128]{2,1,0:T(8,128)(2,1)S(1)}, u32[]{:S(2)}, u32[]{:S(2)}) %all-to-all-start.1) | async-done | bytes 262176 | tf_op jit(solution)/shard_map/all_to_all | solution.py:207
  56.2 0.0 copy-start.8
  56.2 0.9 %copy-done.8 = f32[512,128]{1,0:T(8,128)S(1)} copy-done((f32[512,128]{1,0:T(8,128)S(1)}, f32[512,128]{1,0:T(8,128)}, u32[]{:S(2)}) %copy-start.8) | copy-done | bytes 262168
  57.2 1.3 %gate.1 = bf16[512,128]{1,0:T(8,128)(2,1)} custom-call(bf16[1024,128]{1,0:T(8,128)(2,1)S(1)} %bitcast.17, bf16[512,1024]{1,0:T(8,128)(2,1)S(1)} %get-tuple-element.8.back_ref, f32[512,128]{1,0:T(8,128)S(1)} %copy-done.8, bf16[512,128]{1,0:T(8,128)(2,1)S(1)} %get-tuple-element.10.gate_ref), custom_call_target="tpu_custom_call" | custom-call | tf_op jit(solution)/shard_map/gate/pallas_call | solution.py:210
  58.4 10.3 %all-to-all-start.2 = ((bf16[8,64,128]{2,1,0:T(8,128)(2,1)}), bf16[8,64,128]{2,1,0:T(8,128)(2,1)S(1)}, u32[]{:S(2)}, u32[]{:S(2)}) async-start(bf16[8,64,128]{2,1,0:T(8,128)(2,1)} %bitcast.13), calls=%async_computation.2 | async-start | bytes 262144 | tf_op jit(solution)/shard_map/all_to_all | solution.py:219
  68.7 9.4 %all-to-all-done.2.gated_ref = bf16[8,64,128]{2,1,0:T(8,128)(2,1)S(1)} async-done(((bf16[8,64,128]{2,1,0:T(8,128)(2,1)}), bf16[8,64,128]{2,1,0:T(8,128)(2,1)S(1)}, u32[]{:S(2)}, u32[]{:S(2)}) %all-to-all-start.2) | async-done | bytes 131104 | tf_op jit(solution)/shard_map/all_to_all | solution.py:219
  78.1 0.0 all-gather.2.cloned.1.call-done.w_ref
  78.1 0.0 copy-start.4
  78.1 1.6 %copy-done.4 = bf16[8,128,1024]{2,1,0:T(8,128)(2,1)S(1)} copy-done((bf16[8,128,1024]{2,1,0:T(8,128)(2,1)S(1)}, bf16[8,128,1024]{2,1,0:T(8,128)(2,1)}, u32[]{:S(2)}) %copy-start.4) | copy-done | bytes 2097176
  79.7 1.1 %output.1 = bf16[64,1024]{1,0:T(8,128)(2,1)} custom-call(s32[1]{0:T(128)} %bitcast.group_ref, bf16[8,64,128]{2,1,0:T(8,128)(2,1)S(1)} %all-to-all-done.2.gated_ref, bf16[8,128,1024]{2,1,0:T(8,128)(2,1)S(1)} %copy-done.4, bf16[512,1024]{1,0:T(8,128)(2,1)S(1)} %copy-done.1), custom_call_target="tpu_custom_call" | custom-call | tf_op jit(solution)/shard_map/output/pallas_call | solution.py:222
Async XLA Ops:
  6.5 29.3 %copy-start.10 = (s32[64]{0:T(128)S(1)}, s32[64]{0:T(128)}, u32[]{:S(2)}) copy-start(s32[64]{0:T(128)} %param.14) | copy-start | bytes 772
  6.5 29.3 %copy-start.11 = (s32[64]{0:T(128)S(1)}, s32[64]{0:T(128)}, u32[]{:S(2)}) copy-start(s32[64]{0:T(128)} %param.17) | copy-start | bytes 772
  6.5 29.3 %copy-start.5 = (bf16[1,1024,1,128]{3,1,2,0:T(8,128)(2,1)S(1)}, bf16[1,1024,1,128]{3,1,2,0:T(8,128)(2,1)}, u32[]{:S(2)}) copy-start(bf16[1,1024,1,128]{3,1,2,0:T(8,128)(2,1)} %param.12) | copy-start | bytes 786436
  6.5 71.6 %all-gather.2.cloned.1.call-start = ((), (), s32[]{:S(2)}) async-start(), calls=%async_computation.3 | async-start | bytes 2359296 | tf_op jit(solution)/shard_map/all_gather | solution.py:158
  7.3 1.2 %copy-start = (bf16[512,1024]{1,0:T(8,128)(2,1)S(1)}, bf16[512,1024]{1,0:T(8,128)(2,1)}, u32[]{:S(2)}) copy-start(bf16[512,1024]{1,0:T(8,128)(2,1)} %tokens_ref.5) | copy-start | bytes 3145732
  8.5 1.2 %copy-start.2 = (bf16[1024,1,512]{2,0,1:T(8,128)(2,1)S(1)}, bf16[1024,1,512]{2,0,1:T(8,128)(2,1)}, u32[]{:S(2)}) copy-start(bf16[1024,1,512]{2,0,1:T(8,128)(2,1)} %param.10) | copy-start | bytes 3145732
  9.7 0.7 copy-start.9
  10.4 0.7 copy-start.12
  11.0 24.8 %copy-start.6 = (bf16[1,1024,1,128]{3,1,2,0:T(8,128)(2,1)S(1)}, bf16[1,1024,1,128]{3,1,2,0:T(8,128)(2,1)}, u32[]{:S(2)}) copy-start(bf16[1,1024,1,128]{3,1,2,0:T(8,128)(2,1)} %param.13) | copy-start | bytes 786436
  11.0 33.6 %copy-start.1 = (bf16[512,1024]{1,0:T(8,128)(2,1)S(1)}, bf16[512,1024]{1,0:T(8,128)(2,1)}, u32[]{:S(2)}) copy-start(bf16[512,1024]{1,0:T(8,128)(2,1)} %tokens_ref.5) | copy-start | bytes 3145732
  11.0 33.6 %copy-start.3 = (bf16[1024,1,512]{2,0,1:T(8,128)(2,1)S(1)}, bf16[1024,1,512]{2,0,1:T(8,128)(2,1)}, u32[]{:S(2)}) copy-start(bf16[1024,1,512]{2,0,1:T(8,128)(2,1)} %param.10) | copy-start | bytes 3145732
  11.0 33.6 %copy-start.13 = (s32[64]{0:T(128)S(1)}, s32[64]{0:T(128)}, u32[]{:S(2)}) copy-start(s32[64]{0:T(128)} %param.15) | copy-start | bytes 772
  11.0 33.7 %copy-start.14 = (s32[64]{0:T(128)S(1)}, s32[64]{0:T(128)}, u32[]{:S(2)}) copy-start(s32[64]{0:T(128)} %param.16) | copy-start | bytes 772
  13.5 22.4 %all-to-all-start = ((bf16[64,16,128]{2,1,0:T(8,128)(2,1)}), bf16[64,16,128]{2,1,0:T(8,128)(2,1)S(1)}, u32[]{:S(2)}, u32[]{:S(2)}) async-start(bf16[64,16,128]{2,1,0:T(8,128)(2,1)} %bitcast.5), calls=%async_computation | async-start | bytes 524288 | tf_op jit(solution)/shard_map/all_to_all | solution.py:174
  38.2 18.0 %all-to-all-start.1 = ((bf16[64,16,128]{2,1,0:T(8,128)(2,1)}), bf16[64,16,128]{2,1,0:T(8,128)(2,1)S(1)}, u32[]{:S(2)}, u32[]{:S(2)}) async-start(bf16[64,16,128]{2,1,0:T(8,128)(2,1)} %bitcast.10), calls=%async_computation.1 | async-start | bytes 524288 | tf_op jit(solution)/shard_map/all_to_all | solution.py:207
  46.3 0.7 copy-start.7
  56.2 1.0 %copy-start.8 = (f32[512,128]{1,0:T(8,128)S(1)}, f32[512,128]{1,0:T(8,128)}, u32[]{:S(2)}) copy-start(f32[512,128]{1,0:T(8,128)} %copy-done.7) | copy-start | bytes 786436
  58.4 19.7 %all-to-all-start.2 = ((bf16[8,64,128]{2,1,0:T(8,128)(2,1)}), bf16[8,64,128]{2,1,0:T(8,128)(2,1)S(1)}, u32[]{:S(2)}, u32[]{:S(2)}) async-start(bf16[8,64,128]{2,1,0:T(8,128)(2,1)} %bitcast.13), calls=%async_computation.2 | async-start | bytes 262144 | tf_op jit(solution)/shard_map/all_to_all | solution.py:219
  78.1 1.6 %copy-start.4 = (bf16[8,128,1024]{2,1,0:T(8,128)(2,1)S(1)}, bf16[8,128,1024]{2,1,0:T(8,128)(2,1)}, u32[]{:S(2)}) copy-start(bf16[8,128,1024]{2,1,0:T(8,128)(2,1)} %all-gather.2.cloned.1.call-done.w_ref) | copy-start | bytes 6291460
Sparse Core Ops, SparseCore 0:
  9.4 49.2 all-gather.1

commit v2 on v1

v2 whole, which is shorter than its diff:
```python
import functools

import jax
import jax.numpy as jnp
from jax import lax
from jax.experimental import pallas as pl
from jax.experimental.pallas import tpu as pltpu
from jax.sharding import PartitionSpec as P

epsilon = 1e-05
f32 = jnp.float32
bf16 = jnp.bfloat16


def layer_norm(values):
    average = jnp.mean(values, -1, keepdims=True)
    centred = values - average
    return centred * lax.rsqrt(jnp.mean(centred * centred, -1, keepdims=True) + epsilon)


def silu(values):
    half = values * 0.5
    return half + half * jnp.tanh(half)


def iota(shape, dimension):
    return lax.broadcasted_iota(jnp.int32, shape, dimension)


def to_column(row):
    n = row.shape[1]
    return jnp.sum(jnp.where(iota((n, n), 0) == iota((n, n), 1), row, 0.0), 1, keepdims=True)


def lookup(table_row, index_row):
    sessions, requests = table_row.shape[1], index_row.shape[1]
    named = iota((sessions, requests), 0) == index_row
    return jnp.sum(jnp.where(named, to_column(table_row.astype(f32)), 0.0), 0, keepdims=True)


def first_rows(slot_ref, session_ref, capacity, cands):
    owner = lookup(slot_ref[...], session_ref[...])
    requests = owner.shape[1]
    square = (requests, requests)
    earlier = (to_column(owner) == owner) & (iota(square, 0) < iota(square, 1))
    rank = jnp.sum(jnp.where(earlier, 1.0, 0.0), 0, keepdims=True)
    return (owner * capacity + rank) * cands


def send_kernel(
    capacity, cands, chunks, tokens_ref, w_ref, slot_ref, session_ref, sent_ref, held, weight, queries, placed, sems, w_sem, out_sems
):
    rows = tokens_ref.shape[0]
    head_dim = weight.shape[1]
    slot_rows = sent_ref.shape[0]
    chunk = rows // chunks
    fetch_w = pltpu.make_async_copy(w_ref.at[:, pl.ds(2 * head_dim, head_dim)], weight, w_sem)
    fetches = [
        pltpu.make_async_copy(
            tokens_ref.at[pl.ds(n * chunk, chunk), :], held.at[pl.ds(n * chunk, chunk), :], sems.at[n]
        )
        for n in range(chunks)
    ]
    fetches[0].start()
    fetch_w.start()
    for fetch in fetches[1:]:
        fetch.start()
    first = first_rows(slot_ref, session_ref, capacity, cands)
    requests = first.shape[1]
    spread = iota((requests, rows), 1) // cands == iota((requests, rows), 0)
    place = jnp.sum(jnp.where(spread, to_column(first), 0.0), 0, keepdims=True).astype(jnp.int32)
    place = place + iota((1, rows), 1) % cands
    for n, fetch in enumerate(fetches):
        part = pl.ds(n * chunk, chunk)
        fetch.wait()
        normed = layer_norm(held[part, :].astype(f32)).astype(bf16)
        if n == 0:
            fetch_w.wait()
        queries[part, :] = silu(jnp.dot(normed, weight[...], preferred_element_type=f32)).astype(bf16)
    block = slot_rows // chunks
    stores = []
    for n in range(chunks):
        part = pl.ds(n * block, block)
        chosen = jnp.where(iota((block, rows), 0) + n * block == place, 1.0, 0.0).astype(bf16)
        placed[part, :] = jnp.dot(chosen, queries[...], preferred_element_type=f32).astype(bf16)
        stores.append(pltpu.make_async_copy(placed.at[part, :], sent_ref.at[part, :], out_sems.at[n]))
        stores[-1].start()
    for store in stores:
        store.wait()


def local_kernel(
    capacity, cands, tokens_ref, w_ref, slot_ref, session_ref, count_ref, length_ref, out_ref, result, sem
):
    rows = tokens_ref.shape[0]
    head_dim = result.shape[1] // 3
    normed = layer_norm(tokens_ref[...].astype(f32)).astype(bf16)
    projected = silu(jnp.dot(normed, w_ref[...], preferred_element_type=f32)).astype(bf16).astype(f32)
    gate = projected[:, :head_dim]
    values = projected[:, head_dim : 2 * head_dim]
    queries = projected[:, 2 * head_dim : 3 * head_dim]
    keys = projected[:, 3 * head_dim :]
    lengths = lookup(length_ref[...], session_ref[...])
    requests = lengths.shape[1]
    spread = iota((rows, requests), 0) // cands == iota((rows, requests), 1)

    def per_row(row):
        return jnp.sum(jnp.where(spread, row, 0.0), 1, keepdims=True)

    within = (iota((rows, 1), 0) % cands).astype(f32)
    scores = jnp.sum(queries * keys, -1, keepdims=True) * head_dim ** (-0.5)
    result[:, :head_dim] = silu(scores) * values / (per_row(lengths) + 1.0)
    alive = within < per_row(count_ref[...].astype(f32))
    result[:, head_dim : 2 * head_dim] = jnp.where(alive, gate, 0.0)
    place = per_row(first_rows(slot_ref, session_ref, capacity, cands)) + within
    result[:, 2 * head_dim :] = jnp.broadcast_to(place, (rows, head_dim))
    store = pltpu.make_async_copy(result, out_ref, sem)
    store.start()
    store.wait()


def history_kernel(
    block, me_ref, slot_ref, length_ref, query_ref, keys_ref, values_ref, out_ref, query, keys, values, result, sems
):
    fetches = [
        pltpu.make_async_copy(source, target, sems.at[n])
        for n, (source, target) in enumerate(((keys_ref, keys), (query_ref, query), (values_ref, values)))
    ]
    for fetch in fetches:
        fetch.start()
    history, head_dim = keys_ref.shape
    length = jnp.zeros((), jnp.int32)
    for session in range(slot_ref.shape[0]):
        length = jnp.where(slot_ref[session] == me_ref[0], length_ref[session], length)
    seen = iota((history, 1), 0) < length
    divisor = (length + 1).astype(f32)
    half_scale = 0.5 * head_dim ** (-0.5)
    fetches[0].wait()
    fetches[1].wait()
    fetches[2].wait()
    seen_values = jnp.where(seen, values[...], jnp.zeros((), bf16))
    stores = []
    for n, start in enumerate(range(0, query_ref.shape[0], block)):
        part = pl.ds(start, block)
        half = (
            lax.dot_general(query[part, :], keys[...], (((1,), (1,)), ((), ())), preferred_element_type=f32)
            * half_scale
        )
        weights = (half + half * jnp.tanh(half)).astype(bf16)
        summed = jnp.dot(weights, seen_values, preferred_element_type=f32)
        result[part, :] = (summed / divisor).astype(bf16)
        stores.append(pltpu.make_async_copy(result.at[part, :], out_ref.at[part, :], sems.at[3 + n]))
        stores[-1].start()
    for store in stores:
        store.wait()


def gate_kernel(returned_ref, mine_ref, out_ref, returned, mine, result, sems):
    fetches = [
        pltpu.make_async_copy(mine_ref, mine, sems.at[0]),
        pltpu.make_async_copy(returned_ref, returned, sems.at[1]),
    ]
    for fetch in fetches:
        fetch.start()
    rows, head_dim = result.shape
    slot_rows = returned.shape[0]
    fetches[0].wait()
    place = mine[:, 2 * head_dim : 2 * head_dim + 1].astype(jnp.int32)
    back = jnp.where(iota((rows, slot_rows), 1) == place, 1.0, 0.0).astype(bf16)
    fetches[1].wait()
    part = jnp.dot(back, returned[...], preferred_element_type=f32)
    result[...] = (layer_norm(part + mine[:, :head_dim]) * mine[:, head_dim : 2 * head_dim]).astype(bf16)
    store = pltpu.make_async_copy(result, out_ref, sems.at[0])
    store.start()
    store.wait()


def output_kernel(group_ref, tokens_ref, gated_ref, *refs):
    groups = gated_ref.shape[0]
    pieces, (out_ref, gated, weight, tokens, result, sems) = refs[:groups], refs[groups:]
    head_dim = gated_ref.shape[2]
    share = out_ref.shape[0]
    me = group_ref[0]
    fetches = [pltpu.make_async_copy(gated_ref, gated, sems.at[groups])]
    for n, piece in enumerate(pieces):
        fetches.append(
            pltpu.make_async_copy(piece, weight.at[pl.ds(n * head_dim, head_dim), :], sems.at[n])
        )
    mine = pl.ds(pl.multiple_of(me * share, share), share)
    fetch_tokens = pltpu.make_async_copy(tokens_ref.at[mine, :], tokens, sems.at[groups + 1])
    for fetch in fetches:
        fetch.start()
    fetch_tokens.start()
    total = jnp.zeros(result.shape, f32)
    fetches[0].wait()
    for n in range(0, groups, 2):
        fetches[1 + n].wait()
        fetches[2 + n].wait()
        pair = jnp.concatenate(
            [gated[lax.rem(me + shift + groups, groups)] for shift in ring_order(groups)[n : n + 2]], axis=1
        )
        total = total + jnp.dot(
            pair, weight[pl.ds(n * head_dim, 2 * head_dim), :], preferred_element_type=f32
        )
    fetch_tokens.wait()
    result[...] = (tokens[...].astype(f32) + total).astype(bf16)
    store = pltpu.make_async_copy(result, out_ref, sems.at[groups])
    store.start()
    store.wait()


def ring_order(groups):
    order = [0]
    for step in range(1, groups // 2 + 1):
        order.append(-step)
        if 2 * step < groups:
            order.append(step)
    return order


ANY = pl.BlockSpec(memory_space=pl.ANY)
HBM = pl.BlockSpec(memory_space=pltpu.HBM)
VMEM = pl.BlockSpec(memory_space=pltpu.VMEM)
SMEM = pl.BlockSpec(memory_space=pltpu.SMEM)
params = pltpu.CompilerParams(vmem_limit_bytes=63 * 1024 * 1024)
tight = pltpu.CompilerParams(vmem_limit_bytes=54528 * 1024)
roomy = pltpu.CompilerParams(vmem_limit_bytes=24 * 1024 * 1024)


def on_device(
    tokens,
    w_in,
    w_out,
    cache_keys,
    cache_values,
    session_slot,
    request_session,
    cand_count,
    hist_len,
):
    replicas = lax.axis_size("replica")
    groups = lax.axis_size("tensor")
    my_index = lax.axis_index("replica").astype(jnp.int32).reshape(1)
    group_index = lax.axis_index("tensor").astype(jnp.int32).reshape(1)
    rows, model_width = tokens.shape
    head_dim = w_in.shape[2] // 4
    requests = request_session.shape[0]
    cands = rows // requests
    history = cache_keys.shape[1]
    capacity = max(2, (2 * requests + replicas - 1) // replicas)
    slot_rows = replicas * capacity * cands
    w_flat = w_in.reshape(model_width, 4 * head_dim)
    slots = session_slot.reshape(1, -1)
    lengths = hist_len.reshape(1, -1)
    named = request_session.reshape(1, -1)
    counts = cand_count.reshape(1, -1)
    chunks = 4

    sent = pl.pallas_call(
        functools.partial(send_kernel, capacity, cands, chunks),
        in_specs=[HBM, HBM, VMEM, VMEM],
        out_specs=HBM,
        out_shape=jax.ShapeDtypeStruct((slot_rows, head_dim), bf16),
        scratch_shapes=[
            pltpu.VMEM((rows, model_width), bf16),
            pltpu.VMEM((model_width, head_dim), bf16),
            pltpu.VMEM((rows, head_dim), bf16),
            pltpu.VMEM((slot_rows, head_dim), bf16),
            pltpu.SemaphoreType.DMA((chunks,)),
            pltpu.SemaphoreType.DMA,
            pltpu.SemaphoreType.DMA((chunks,)),
        ],
        compiler_params=params,
        name="send",
    )(tokens, w_flat, slots, named)
    got = lax.all_to_all(
        sent.reshape(replicas, capacity * cands, head_dim), "replica", split_axis=0, concat_axis=0, tiled=True
    )
    w_own, sent = lax.optimization_barrier((w_out.reshape(head_dim, model_width), sent))

    def shifted(piece, by):
        return lax.ppermute(piece, "tensor", [(z, (z + by) % groups) for z in range(groups)])

    pieces = {0: w_own}
    half = groups // 2
    near = (half + 1) // 2
    for step in range(1, near + 1):
        pieces[-step] = shifted(w_own, step)
        pieces[step] = shifted(w_own, -step)
    block = min(256, slot_rows)
    answers = pl.pallas_call(
        functools.partial(history_kernel, block),
        in_specs=[SMEM, SMEM, SMEM, ANY, HBM, HBM],
        out_specs=HBM,
        out_shape=jax.ShapeDtypeStruct((slot_rows, head_dim), bf16),
        scratch_shapes=[
            pltpu.VMEM((slot_rows, head_dim), bf16),
            pltpu.VMEM((history, head_dim), bf16),
            pltpu.VMEM((history, head_dim), bf16),
            pltpu.VMEM((slot_rows, head_dim), bf16),
            pltpu.SemaphoreType.DMA((3 + slot_rows // block,)),
        ],
        compiler_params=roomy,
        name="history",
    )(
        my_index,
        session_slot,
        hist_len,
        got.reshape(slot_rows, head_dim),
        cache_keys.reshape(history, head_dim),
        cache_values.reshape(history, head_dim),
    )
    pieces, named_later, answers = lax.optimization_barrier((pieces, named, answers))
    for step in range(near + 1, half + 1):
        pieces[-step] = shifted(pieces[-near], step - near)
        if 2 * step < groups:
            pieces[step] = shifted(pieces[near], near - step)
    mine = pl.pallas_call(
        functools.partial(local_kernel, capacity, cands),
        in_specs=[VMEM] * 6,
        out_specs=HBM,
        out_shape=jax.ShapeDtypeStruct((rows, 3 * head_dim), f32),
        scratch_shapes=[pltpu.VMEM((rows, 3 * head_dim), f32), pltpu.SemaphoreType.DMA],
        compiler_params=params,
        cost_estimate=pl.CostEstimate(
            flops=2 * rows * model_width * 4 * head_dim, bytes_accessed=4 << 20, transcendentals=rows * 4 * head_dim
        ),
        name="local",
    )(tokens, w_flat, slots, named_later, counts, lengths)
    returned = lax.all_to_all(
        answers.reshape(replicas, capacity * cands, head_dim), "replica", split_axis=0, concat_axis=0, tiled=True
    )
    gated = pl.pallas_call(
        gate_kernel,
        in_specs=[ANY, HBM],
        out_specs=HBM,
        out_shape=jax.ShapeDtypeStruct((rows, head_dim), bf16),
        scratch_shapes=[
            pltpu.VMEM((slot_rows, head_dim), bf16),
            pltpu.VMEM((rows, 3 * head_dim), f32),
            pltpu.VMEM((rows, head_dim), bf16),
            pltpu.SemaphoreType.DMA((2,)),
        ],
        compiler_params=tight,
        name="gate",
    )(returned.reshape(slot_rows, head_dim), mine)
    share = rows // groups
    heads = lax.all_to_all(
        gated.reshape(groups, share, head_dim), "tensor", split_axis=0, concat_axis=0, tiled=True
    )
    return pl.pallas_call(
        output_kernel,
        in_specs=[SMEM, HBM] + [ANY] * (1 + groups),
        out_specs=HBM,
        out_shape=jax.ShapeDtypeStruct((share, model_width), bf16),
        scratch_shapes=[
            pltpu.VMEM((groups, share, head_dim), bf16),
            pltpu.VMEM((groups * head_dim, model_width), bf16),
            pltpu.VMEM((share, model_width), bf16),
            pltpu.VMEM((share, model_width), bf16),
            pltpu.SemaphoreType.DMA((groups + 2,)),
        ],
        compiler_params=tight,
        name="output",
    )(group_index, tokens, heads, *[pieces[shift] for shift in ring_order(groups)])


def solution(mesh):
    in_specs = (
        P("replica", None),
        P(None, "tensor", None),
        P("tensor", None, None),
        P("replica", None, "tensor", None),
        P("replica", None, "tensor", None),
        P(),
        P("replica"),
        P("replica"),
        P(),
    )
    out_specs = P(("replica", "tensor"), None)
    return jax.shard_map(
        on_device, mesh=mesh, in_specs=in_specs, out_specs=out_specs, check_vma=False
    )
```

time: 88.1 us -> 95 us (1.078)
  starting transfers between devices: 27.6 us -> 56.8 us
  between operations: 13.5 us -> 0.22 us
  waiting for transfers between devices: 30.9 us -> 20.1 us
  Pallas kernels: 8.65 us -> 16.6 us
  local copies, waits for them, and re-layouts: 7.02 us -> 0.66 us
    ppermute x0 -> x7, starting transfers between devices: none -> 32.2 us  [shifted(): lax.ppermute(piece, 'tensor', [(z, (z + by) % groups) for z in range(grou...]
    all_to_all x1, waiting for transfers between devices: 11.6 us -> 0.01 us  [on_device(): lax.all_to_all(sent.reshape(replicas, capacity * cands, head_dim), 'repli...]
    ppermute x0 -> x7, waiting for transfers between devices: none -> 11.1 us  [shifted(): lax.ppermute(piece, 'tensor', [(z, (z + by) % groups) for z in range(grou...]
    all_to_all x1, waiting for transfers between devices: 9.26 us -> 0.01 us  [on_device(): lax.all_to_all(answers.reshape(replicas, capacity * cands, head_dim), 're...]
    all_to_all x1, starting transfers between devices: 10.3 us -> 3.38 us  [on_device(): lax.all_to_all(gated.reshape(groups, share, head_dim), 'tensor', split_ax...]
    unnamed x30 -> x12, local copies, waits for them, and re-layouts: 7.02 us -> 0.66 us
    pallas_call x4, Pallas kernels: 7.1 us -> 12.7 us  [the longest x1 4.49 us: on_device(): pl.pallas_call(functools.partial(send_kernel, capacity, cands, chunks), i...]
    all_to_all x1, starting transfers between devices: 6.47 us -> 10.3 us  [on_device(): lax.all_to_all(answers.reshape(replicas, capacity * cands, head_dim), 're...]
  transfers between devices with their start and end apart: 4 -> 10, of which waited for: 3 -> 4; matrix products, arithmetic and copies ran while one was open for 0% -> 0% of each run, Pallas kernels for 6% -> 10%
where the time goes in v2:
time: 95 us; the launch traced here: 94.3 us
  starting transfers between devices  56.8 us (60%)
  waiting for transfers between devices  20.1 us (21%)
  Pallas kernels  16.6 us (17%)
    ppermute x7, starting transfers between devices, shifted(): lax.ppermute(piece, 'tensor', [(z, (z + by) % groups) for z in range(grou...  32.2 us
    ppermute x7, waiting for transfers between devices, shifted(): lax.ppermute(piece, 'tensor', [(z, (z + by) % groups) for z in range(grou...  11.1 us
    all_to_all x1, starting transfers between devices, on_device(): lax.all_to_all(sent.reshape(replicas, capacity * cands, head_dim), 'repli...  10.9 us
    all_to_all x1, starting transfers between devices, on_device(): lax.all_to_all(answers.reshape(replicas, capacity * cands, head_dim), 're...  10.3 us
    all_to_all x1, waiting for transfers between devices, on_device(): lax.all_to_all(gated.reshape(groups, share, head_dim), 'tensor', split_ax...  8.96 us
    pallas_call x1, Pallas kernels, on_device(): pl.pallas_call(functools.partial(send_kernel, capacity, cands, chunks), i...  4.49 us
    pallas_call x1, Pallas kernels, on_device(): pl.pallas_call(functools.partial(local_kernel, capacity, cands), in_specs...  3.86 us
    all_to_all x1, starting transfers between devices, on_device(): lax.all_to_all(gated.reshape(groups, share, head_dim), 'tensor', split_ax...  3.38 us
  transfers between devices with their start and end apart: 10, of which 4 were waited for; matrix products, arithmetic and copies ran while one was open for 0% of the time, Pallas kernels for 10%

profile of v2, /device:TPU:6, one launch (start us, length us, event | category | flops | bytes accessed | tf_op | source)
XLA Modules:
  0.0 94.3 jit_solution(4213797548228363878)
XLA Ops:
  0.0 0.0 copy-start.2
  0.0 4.5 %send.1 = bf16[1024,128]{1,0:T(8,128)(2,1)} custom-call(bf16[512,1024]{1,0:T(8,128)(2,1)} %tokens_ref.5, bf16[1024,512]{1,0:T(8,128)(2,1)} %bitcast.27, s32[1,64]{1,0:T(1,128)} %bitcast.24, s32[1,64]{1,0:T(1,128)} %bitcast.30), custom_call_target="tpu_custom_call" | custom-call | tf_op jit(solution)/shard_map/send/pallas_call | solution.py:259
  4.5 0.0 copy-start
  4.5 0.0 copy-start.1
  4.5 10.9 %all-to-all-start = ((bf16[64,16,128]{2,1,0:T(8,128)(2,1)}), bf16[64,16,128]{2,1,0:T(8,128)(2,1)S(1)}, u32[]{:S(2)}, u32[]{:S(2)}) async-start(bf16[64,16,128]{2,1,0:T(8,128)(2,1)} %bitcast.29), calls=%async_computation | async-start | bytes 524288 | tf_op jit(solution)/shard_map/all_to_all | solution.py:276
  15.5 0.0 copy-done.2
  15.5 6.1 %collective-permute-start = (bf16[128,1024]{1,0:T(8,128)(2,1)S(1)}, bf16[128,1024]{1,0:T(8,128)(2,1)}, u32[]{:S(2)}, u32[]{:S(2)}) collective-permute-start(bf16[128,1024]{1,0:T(8,128)(2,1)S(1)} %bitcast.19), channel_id=1, source_target_pairs={{0,2},{1,3},{2,4},{3,5},{4,6},{5,7},{6,0},{7,1},{8,10},{9,11},{10,... | collective-permute-start | bytes 786440 | tf_op jit(solution)/shard_map/ppermute | solution.py:282
  21.6 4.3 %collective-permute-start.1 = (bf16[128,1024]{1,0:T(8,128)(2,1)S(1)}, bf16[128,1024]{1,0:T(8,128)(2,1)S(1)}, u32[]{:S(2)}, u32[]{:S(2)}) collective-permute-start(bf16[128,1024]{1,0:T(8,128)(2,1)S(1)} %bitcast.20), channel_id=1, source_target_pairs={{0,1},{1,2},{2,3},{3,4},{4,5},{5,6},{6,7},{7,0},{8,9},{9,10},{10,1... | collective-permute-start | bytes 786440 | tf_op jit(solution)/shard_map/ppermute | solution.py:282
  25.9 4.4 %collective-permute-start.2 = (bf16[128,1024]{1,0:T(8,128)(2,1)S(1)}, bf16[128,1024]{1,0:T(8,128)(2,1)S(1)}, u32[]{:S(2)}, u32[]{:S(2)}) collective-permute-start(bf16[128,1024]{1,0:T(8,128)(2,1)S(1)} %bitcast.21), channel_id=1, source_target_pairs={{0,7},{1,0},{2,1},{3,2},{4,3},{5,4},{6,5},{7,6},{8,15},{9,8},{10,9... | collective-permute-start | bytes 786440 | tf_op jit(solution)/shard_map/ppermute | solution.py:282
  30.3 4.8 %collective-permute-start.3 = (bf16[128,1024]{1,0:T(8,128)(2,1)S(1)}, bf16[128,1024]{1,0:T(8,128)(2,1)}, u32[]{:S(2)}, u32[]{:S(2)}) collective-permute-start(bf16[128,1024]{1,0:T(8,128)(2,1)S(1)} %bitcast.22), channel_id=1, source_target_pairs={{0,6},{1,7},{2,0},{3,1},{4,2},{5,3},{6,4},{7,5},{8,14},{9,15},{10,... | collective-permute-start | bytes 786440 | tf_op jit(solution)/shard_map/ppermute | solution.py:282
  35.1 0.0 all-to-all-done
  35.1 0.0 copy-start.3
  35.2 0.0 copy-start.4
  35.2 0.0 copy-done
  35.2 0.0 copy-done.1
  35.2 0.6 copy-done.3
  35.8 0.0 copy-done.4
  35.8 3.0 %history.1 = bf16[1024,128]{1,0:T(8,128)(2,1)} custom-call(s32[1]{0:T(128)} %bitcast.5.me_ref, s32[64]{0:T(128)S(1)} %copy-done.3, s32[64]{0:T(128)S(1)} %copy-done.4, bf16[1024,128]{1,0:T(8,128)(2,1)S(1)} %bitcast.15, bf16[1024,128]{1,0:T(8,128)(2,1)S(1)} %bitcast.17, bf16[1024,128]{1,0:T(8,128)(2,1)S(1)} %bitcast.18), custom_call_target="tpu_custom_call" | custom-call | tf_op jit(solution)/shard_map/history/pallas_call | solution.py:291
  38.8 0.4 collective-permute-done.refs_3_
  39.3 5.0 %collective-permute-done.1.refs_1_ = bf16[128,1024]{1,0:T(8,128)(2,1)S(1)} collective-permute-done((bf16[128,1024]{1,0:T(8,128)(2,1)S(1)}, bf16[128,1024]{1,0:T(8,128)(2,1)S(1)}, u32[]{:S(2)}, u32[]{:S(2)}) %collective-permute-start.1) | collective-permute-done | bytes 262176 | tf_op jit(solution)/shard_map/ppermute | solution.py:282
  44.3 0.0 collective-permute-done.2.refs_2_
  44.3 0.0 copy-start.5
  44.3 5.6 %collective-permute-done.3.refs_4_ = bf16[128,1024]{1,0:T(8,128)(2,1)} collective-permute-done((bf16[128,1024]{1,0:T(8,128)(2,1)S(1)}, bf16[128,1024]{1,0:T(8,128)(2,1)}, u32[]{:S(2)}, u32[]{:S(2)}) %collective-permute-start.3) | collective-permute-done | bytes 262176 | tf_op jit(solution)/shard_map/ppermute | solution.py:282
  49.9 0.0 copy-done.5
  49.9 10.3 %all-to-all-start.1 = ((bf16[64,16,128]{2,1,0:T(8,128)(2,1)}), bf16[64,16,128]{2,1,0:T(8,128)(2,1)S(1)}, u32[]{:S(2)}, u32[]{:S(2)}) async-start(bf16[64,16,128]{2,1,0:T(8,128)(2,1)} %bitcast.10), calls=%async_computation.1 | async-start | bytes 524288 | tf_op jit(solution)/shard_map/all_to_all | solution.py:330
  60.3 1.9 %collective-permute-start.4 = (bf16[128,1024]{1,0:T(8,128)(2,1)}, bf16[128,1024]{1,0:T(8,128)(2,1)}, u32[]{:S(2)}, u32[]{:S(2)}) collective-permute-start(bf16[128,1024]{1,0:T(8,128)(2,1)} %collective-permute-done.refs_3_), channel_id=1, source_target_pairs={{0,1},{1,2},{2,3},{3,4},{4,5},{5,6},{6,7},{7,0},{8,9},{9,10},{10,1... | collective-permute-start | bytes 786440 | tf_op jit(solution)/shard_map/ppermute | solution.py:282
  62.2 5.9 %collective-permute-start.6 = (bf16[128,1024]{1,0:T(8,128)(2,1)}, bf16[128,1024]{1,0:T(8,128)(2,1)}, u32[]{:S(2)}, u32[]{:S(2)}) collective-permute-start(bf16[128,1024]{1,0:T(8,128)(2,1)} %collective-permute-done.refs_3_), channel_id=1, source_target_pairs={{0,2},{1,3},{2,4},{3,5},{4,6},{5,7},{6,0},{7,1},{8,10},{9,11},{10,... | collective-permute-start | bytes 786440 | tf_op jit(solution)/shard_map/ppermute | solution.py:282
  68.1 4.8 %collective-permute-start.5 = (bf16[128,1024]{1,0:T(8,128)(2,1)}, bf16[128,1024]{1,0:T(8,128)(2,1)}, u32[]{:S(2)}, u32[]{:S(2)}) collective-permute-start(bf16[128,1024]{1,0:T(8,128)(2,1)} %collective-permute-done.3.refs_4_), channel_id=1, source_target_pairs={{0,7},{1,0},{2,1},{3,2},{4,3},{5,4},{6,5},{7,6},{8,15},{9,8},{10,9... | collective-permute-start | bytes 786440 | tf_op jit(solution)/shard_map/ppermute | solution.py:282
  72.8 3.9 %local.1.mine_ref = f32[512,384]{1,0:T(8,128)} custom-call(bf16[512,1024]{1,0:T(8,128)(2,1)} %tokens_ref.5, bf16[1024,512]{1,0:T(8,128)(2,1)} %bitcast.28, s32[1,64]{1,0:T(1,128)} %bitcast.25, s32[1,64]{1,0:T(1,128)} %bitcast.31, s32[1,64]{1,0:T(1,128)} %bitcast.32, s32[1,64]{1,0:T(1,128)} %bitcast.26), custom_call_target="tpu_custom_call" | custom-call | flops 536870912 | bytes 4194304 | tf_op jit(solution)/shard_map/local/pallas_call | solution.py:318
  76.7 0.0 all-to-all-done.1
  76.7 2.7 %gate.1 = bf16[512,128]{1,0:T(8,128)(2,1)} custom-call(bf16[1024,128]{1,0:T(8,128)(2,1)S(1)} %bitcast.16, f32[512,384]{1,0:T(8,128)} %local.1.mine_ref), custom_call_target="tpu_custom_call" | custom-call | tf_op jit(solution)/shard_map/gate/pallas_call | solution.py:333
  79.4 3.4 %all-to-all-start.2 = ((bf16[8,64,128]{2,1,0:T(8,128)(2,1)}), bf16[8,64,128]{2,1,0:T(8,128)(2,1)S(1)}, u32[]{:S(2)}, u32[]{:S(2)}) async-start(bf16[8,64,128]{2,1,0:T(8,128)(2,1)} %bitcast.14), calls=%async_computation.2 | async-start | bytes 262144 | tf_op jit(solution)/shard_map/all_to_all | solution.py:348
  82.8 0.0 collective-permute-done.4.refs_5_
  82.8 0.0 collective-permute-done.5.refs_6_
  82.9 0.0 collective-permute-done.6.refs_7_
  82.9 9.0 %all-to-all-done.2.gated_ref = bf16[8,64,128]{2,1,0:T(8,128)(2,1)S(1)} async-done(((bf16[8,64,128]{2,1,0:T(8,128)(2,1)}), bf16[8,64,128]{2,1,0:T(8,128)(2,1)S(1)}, u32[]{:S(2)}, u32[]{:S(2)}) %all-to-all-start.2) | async-done | bytes 131104 | tf_op jit(solution)/shard_map/all_to_all | solution.py:348
  91.8 2.5 %output.1 = bf16[64,1024]{1,0:T(8,128)(2,1)} custom-call(s32[1]{0:T(128)} %bitcast.group_ref, bf16[512,1024]{1,0:T(8,128)(2,1)} %tokens_ref.5, bf16[8,64,128]{2,1,0:T(8,128)(2,1)S(1)} %all-to-all-done.2.gated_ref, bf16[128,1024]{1,0:T(8,128)(2,1)S(1)} %bitcast.23, bf16[128,1024]{1,0:T(8,128)(2,1)S(1)} %collective-permute-done.1.refs_1_, ...), custom_call_target="tpu_custom_call" | custom-call | tf_op jit(solution)/shard_map/output/pallas_call | solution.py:351
Async XLA Ops:
  0.0 15.5 %copy-start.2 = (bf16[1,128,1024]{2,1,0:T(8,128)(2,1)S(1)}, bf16[1,128,1024]{2,1,0:T(8,128)(2,1)}, u32[]{:S(2)}) copy-start(bf16[1,128,1024]{2,1,0:T(8,128)(2,1)} %param.11) | copy-start | bytes 786436
  4.5 30.7 %copy-start = (bf16[1,1024,1,128]{3,1,2,0:T(8,128)(2,1)S(1)}, bf16[1,1024,1,128]{3,1,2,0:T(8,128)(2,1)}, u32[]{:S(2)}) copy-start(bf16[1,1024,1,128]{3,1,2,0:T(8,128)(2,1)} %param.12) | copy-start | bytes 786436
  4.5 30.7 %copy-start.1 = (bf16[1,1024,1,128]{3,1,2,0:T(8,128)(2,1)S(1)}, bf16[1,1024,1,128]{3,1,2,0:T(8,128)(2,1)}, u32[]{:S(2)}) copy-start(bf16[1,1024,1,128]{3,1,2,0:T(8,128)(2,1)} %param.13) | copy-start | bytes 786436
  4.5 30.6 %all-to-all-start = ((bf16[64,16,128]{2,1,0:T(8,128)(2,1)}), bf16[64,16,128]{2,1,0:T(8,128)(2,1)S(1)}, u32[]{:S(2)}, u32[]{:S(2)}) async-start(bf16[64,16,128]{2,1,0:T(8,128)(2,1)} %bitcast.29), calls=%async_computation | async-start | bytes 524288 | tf_op jit(solution)/shard_map/all_to_all | solution.py:276
  15.5 23.8 %collective-permute-start = (bf16[128,1024]{1,0:T(8,128)(2,1)S(1)}, bf16[128,1024]{1,0:T(8,128)(2,1)}, u32[]{:S(2)}, u32[]{:S(2)}) collective-permute-start(bf16[128,1024]{1,0:T(8,128)(2,1)S(1)} %bitcast.19), channel_id=1, source_target_pairs={{0,2},{1,3},{2,4},{3,5},{4,6},{5,7},{6,0},{7,1},{8,10},{9,11},{10,... | collective-permute-start | bytes 786440 | tf_op jit(solution)/shard_map/ppermute | solution.py:282
  21.6 22.7 %collective-permute-start.1 = (bf16[128,1024]{1,0:T(8,128)(2,1)S(1)}, bf16[128,1024]{1,0:T(8,128)(2,1)S(1)}, u32[]{:S(2)}, u32[]{:S(2)}) collective-permute-start(bf16[128,1024]{1,0:T(8,128)(2,1)S(1)} %bitcast.20), channel_id=1, source_target_pairs={{0,1},{1,2},{2,3},{3,4},{4,5},{5,6},{6,7},{7,0},{8,9},{9,10},{10,1... | collective-permute-start | bytes 786440 | tf_op jit(solution)/shard_map/ppermute | solution.py:282
  25.9 18.4 %collective-permute-start.2 = (bf16[128,1024]{1,0:T(8,128)(2,1)S(1)}, bf16[128,1024]{1,0:T(8,128)(2,1)S(1)}, u32[]{:S(2)}, u32[]{:S(2)}) collective-permute-start(bf16[128,1024]{1,0:T(8,128)(2,1)S(1)} %bitcast.21), channel_id=1, source_target_pairs={{0,7},{1,0},{2,1},{3,2},{4,3},{5,4},{6,5},{7,6},{8,15},{9,8},{10,9... | collective-permute-start | bytes 786440 | tf_op jit(solution)/shard_map/ppermute | solution.py:282
  30.3 19.6 %collective-permute-start.3 = (bf16[128,1024]{1,0:T(8,128)(2,1)S(1)}, bf16[128,1024]{1,0:T(8,128)(2,1)}, u32[]{:S(2)}, u32[]{:S(2)}) collective-permute-start(bf16[128,1024]{1,0:T(8,128)(2,1)S(1)} %bitcast.22), channel_id=1, source_target_pairs={{0,6},{1,7},{2,0},{3,1},{4,2},{5,3},{6,4},{7,5},{8,14},{9,15},{10,... | collective-permute-start | bytes 786440 | tf_op jit(solution)/shard_map/ppermute | solution.py:282
  35.1 0.7 copy-start.3
  35.2 0.7 copy-start.4
  44.3 5.7 %copy-start.5 = (bf16[128,1024]{1,0:T(8,128)(2,1)}, bf16[128,1024]{1,0:T(8,128)(2,1)S(1)}, u32[]{:S(2)}) copy-start(bf16[128,1024]{1,0:T(8,128)(2,1)S(1)} %collective-permute-done.2.refs_2_) | copy-start | bytes 786436
  49.9 26.8 %all-to-all-start.1 = ((bf16[64,16,128]{2,1,0:T(8,128)(2,1)}), bf16[64,16,128]{2,1,0:T(8,128)(2,1)S(1)}, u32[]{:S(2)}, u32[]{:S(2)}) async-start(bf16[64,16,128]{2,1,0:T(8,128)(2,1)} %bitcast.10), calls=%async_computation.1 | async-start | bytes 524288 | tf_op jit(solution)/shard_map/all_to_all | solution.py:330
  60.3 22.6 %collective-permute-start.4 = (bf16[128,1024]{1,0:T(8,128)(2,1)}, bf16[128,1024]{1,0:T(8,128)(2,1)}, u32[]{:S(2)}, u32[]{:S(2)}) collective-permute-start(bf16[128,1024]{1,0:T(8,128)(2,1)} %collective-permute-done.refs_3_), channel_id=1, source_target_pairs={{0,1},{1,2},{2,3},{3,4},{4,5},{5,6},{6,7},{7,0},{8,9},{9,10},{10,1... | collective-permute-start | bytes 786440 | tf_op jit(solution)/shard_map/ppermute | solution.py:282
  62.2 20.7 %collective-permute-start.6 = (bf16[128,1024]{1,0:T(8,128)(2,1)}, bf16[128,1024]{1,0:T(8,128)(2,1)}, u32[]{:S(2)}, u32[]{:S(2)}) collective-permute-start(bf16[128,1024]{1,0:T(8,128)(2,1)} %collective-permute-done.refs_3_), channel_id=1, source_target_pairs={{0,2},{1,3},{2,4},{3,5},{4,6},{5,7},{6,0},{7,1},{8,10},{9,11},{10,... | collective-permute-start | bytes 786440 | tf_op jit(solution)/shard_map/ppermute | solution.py:282
  68.1 14.8 %collective-permute-start.5 = (bf16[128,1024]{1,0:T(8,128)(2,1)}, bf16[128,1024]{1,0:T(8,128)(2,1)}, u32[]{:S(2)}, u32[]{:S(2)}) collective-permute-start(bf16[128,1024]{1,0:T(8,128)(2,1)} %collective-permute-done.3.refs_4_), channel_id=1, source_target_pairs={{0,7},{1,0},{2,1},{3,2},{4,3},{5,4},{6,5},{7,6},{8,15},{9,8},{10,9... | collective-permute-start | bytes 786440 | tf_op jit(solution)/shard_map/ppermute | solution.py:282
  79.4 12.4 %all-to-all-start.2 = ((bf16[8,64,128]{2,1,0:T(8,128)(2,1)}), bf16[8,64,128]{2,1,0:T(8,128)(2,1)S(1)}, u32[]{:S(2)}, u32[]{:S(2)}) async-start(bf16[8,64,128]{2,1,0:T(8,128)(2,1)} %bitcast.14), calls=%async_computation.2 | async-start | bytes 262144 | tf_op jit(solution)/shard_map/all_to_all | solution.py:348

commit v3 on v2

--- a/solution.py
+++ b/solution.py
@@ -175,47 +175,43 @@
     store.wait()
 
 
-def output_kernel(group_ref, tokens_ref, gated_ref, *refs):
-    groups = gated_ref.shape[0]
-    pieces, (out_ref, gated, weight, tokens, result, sems) = refs[:groups], refs[groups:]
-    head_dim = gated_ref.shape[2]
-    share = out_ref.shape[0]
-    me = group_ref[0]
-    fetches = [pltpu.make_async_copy(gated_ref, gated, sems.at[groups])]
-    for n, piece in enumerate(pieces):
-        fetches.append(
-            pltpu.make_async_copy(piece, weight.at[pl.ds(n * head_dim, head_dim), :], sems.at[n])
-        )
-    mine = pl.ds(pl.multiple_of(me * share, share), share)
-    fetch_tokens = pltpu.make_async_copy(tokens_ref.at[mine, :], tokens, sems.at[groups + 1])
+held_heads = ((0, 1), (2, 3), (4, -1), (-2, -3))
+
+
+def output_kernel(
+    group_ref, me_ref, tokens_ref, gated_ref, own_ref, one_ref, two_ref, last_ref, other_one_ref, other_two_ref,
+    out_ref, gated, weight, tokens, result, sems,
+):
+    groups, share, head_dim = gated_ref.shape
+    group = group_ref[0]
+    sign = jnp.where(me_ref[0] % 2 == 0, -1, 1)
+    fetches = [pltpu.make_async_copy(gated_ref, gated, sems.at[0])]
+    start = 0
+    for n, piece in enumerate((own_ref, one_ref, two_ref, last_ref, other_one_ref, other_two_ref)):
+        size = piece.shape[0]
+        fetches.append(pltpu.make_async_copy(piece, weight.at[pl.ds(start, size), :], sems.at[1 + n]))
+        start += size
+    mine = pl.ds(pl.multiple_of(group * share, share), share)
+    fetch_tokens = pltpu.make_async_copy(tokens_ref.at[mine, :], tokens, sems.at[7])
     for fetch in fetches:
         fetch.start()
     fetch_tokens.start()
     total = jnp.zeros(result.shape, f32)
     fetches[0].wait()
-    for n in range(0, groups, 2):
-        fetches[1 + n].wait()
-        fetches[2 + n].wait()
+    for n, heads in enumerate(held_heads):
+        for fetch in (fetches[1:3], fetches[3:4], fetches[4:6], fetches[6:7])[n]:
+            fetch.wait()
         pair = jnp.concatenate(
-            [gated[lax.rem(me + shift + groups, groups)] for shift in ring_order(groups)[n : n + 2]], axis=1
+            [gated[lax.rem(group + sign * head + groups, groups)] for head in heads], axis=1
         )
         total = total + jnp.dot(
-            pair, weight[pl.ds(n * head_dim, 2 * head_dim), :], preferred_element_type=f32
+            pair, weight[pl.ds(2 * n * head_dim, 2 * head_dim), :], preferred_element_type=f32
         )
     fetch_tokens.wait()
     result[...] = (tokens[...].astype(f32) + total).astype(bf16)
-    store = pltpu.make_async_copy(result, out_ref, sems.at[groups])
+    store = pltpu.make_async_copy(result, out_ref, sems.at[0])
     store.start()
     store.wait()
-
-
-def ring_order(groups):
-    order = [0]
-    for step in range(1, groups // 2 + 1):
-        order.append(-step)
-        if 2 * step < groups:
-            order.append(step)
-    return order
 
 
 ANY = pl.BlockSpec(memory_space=pl.ANY)
@@ -276,17 +272,21 @@
     got = lax.all_to_all(
         sent.reshape(replicas, capacity * cands, head_dim), "replica", split_axis=0, concat_axis=0, tiled=True
     )
-    w_own, sent = lax.optimization_barrier((w_out.reshape(head_dim, model_width), sent))
-
-    def shifted(piece, by):
-        return lax.ppermute(piece, "tensor", [(z, (z + by) % groups) for z in range(groups)])
-
-    pieces = {0: w_own}
-    half = groups // 2
-    near = (half + 1) // 2
-    for step in range(1, near + 1):
-        pieces[-step] = shifted(w_own, step)
-        pieces[step] = shifted(w_own, -step)
+    def passed(piece, by):
+        pairs = []
+        for r in range(replicas):
+            for z in range(groups):
+                pairs.append((r * groups + z, r * groups + (z + (by if r % 2 == 0 else -by)) % groups))
+        return lax.ppermute(piece, ("replica", "tensor"), pairs)
+
+    def swapped(piece):
+        return lax.ppermute(piece, "replica", [(r, r ^ 1) for r in range(replicas)])
+
+    w_own = w_out.reshape(head_dim, model_width)
+    next_one = passed(w_own, 1)
+    w_own, next_one, sent = lax.optimization_barrier((w_own, next_one, sent))
+    next_two = passed(jnp.concatenate([w_own, next_one], axis=0), 2)
+    other_one = swapped(next_one)
     block = min(256, slot_rows)
     answers = pl.pallas_call(
         functools.partial(history_kernel, block),
@@ -301,6 +301,7 @@
             pltpu.SemaphoreType.DMA((3 + slot_rows // block,)),
         ],
         compiler_params=roomy,
+        cost_estimate=pl.CostEstimate(flops=1 << 30, bytes_accessed=64 << 20, transcendentals=slot_rows * history),
         name="history",
     )(
         my_index,
@@ -310,11 +311,9 @@
         cache_keys.reshape(history, head_dim),
         cache_values.reshape(history, head_dim),
     )
-    pieces, named_later, answers = lax.optimization_barrier((pieces, named, answers))
-    for step in range(near + 1, half + 1):
-        pieces[-step] = shifted(pieces[-near], step - near)
-        if 2 * step < groups:
-            pieces[step] = shifted(pieces[near], near - step)
+    next_two, other_one, named_later, answers = lax.optimization_barrier((next_two, other_one, named, answers))
+    last = passed(next_two[head_dim:], 1)
+    other_two = swapped(next_two)
     mine = pl.pallas_call(
         functools.partial(local_kernel, capacity, cands),
         in_specs=[VMEM] * 6,
@@ -350,7 +349,7 @@
     )
     return pl.pallas_call(
         output_kernel,
-        in_specs=[SMEM, HBM] + [ANY] * (1 + groups),
+        in_specs=[SMEM, SMEM, HBM] + [ANY] * 7,
         out_specs=HBM,
         out_shape=jax.ShapeDtypeStruct((share, model_width), bf16),
         scratch_shapes=[
@@ -358,11 +357,11 @@
             pltpu.VMEM((groups * head_dim, model_width), bf16),
             pltpu.VMEM((share, model_width), bf16),
             pltpu.VMEM((share, model_width), bf16),
-            pltpu.SemaphoreType.DMA((groups + 2,)),
+            pltpu.SemaphoreType.DMA((8,)),
         ],
         compiler_params=tight,
         name="output",
-    )(group_index, tokens, heads, *[pieces[shift] for shift in ring_order(groups)])
+    )(group_index, my_index, tokens, heads, w_own, next_one, next_two, last, other_one, other_two)
 
 
 def solution(mesh):

time: 95 us -> 85.4 us (0.90)
  starting transfers between devices: 56.8 us -> 45.9 us
  local copies, waits for them, and re-layouts: 0.66 us -> 2.38 us
    ppermute x7 -> x5, starting transfers between devices: 32.2 us -> 14.4 us  [the longest x3 8.23 us: passed(): return lax.ppermute(piece, ('replica', 'tensor'), pairs)]
    ppermute x7 -> x5, waiting for transfers between devices: 11.1 us -> 2.99 us  [the longest x3 2.98 us: passed(): return lax.ppermute(piece, ('replica', 'tensor'), pairs)]
    all_to_all x1, starting transfers between devices: 10.9 us -> 16.8 us  [on_device(): lax.all_to_all(sent.reshape(replicas, capacity * cands, head_dim), 'repli...]
    all_to_all x1, waiting for transfers between devices: 0.01 us -> 5.33 us  [on_device(): lax.all_to_all(sent.reshape(replicas, capacity * cands, head_dim), 'repli...]
    all_to_all x1, waiting for transfers between devices: 0.01 us -> 2 us  [on_device(): lax.all_to_all(answers.reshape(replicas, capacity * cands, head_dim), 're...]
    slice x0 -> x1, local copies, waits for them, and re-layouts: none -> 1.7 us  [on_device(): last = passed(next_two[head_dim:], 1)]
    all_to_all x1, starting transfers between devices: 3.38 us -> 4.48 us  [on_device(): lax.all_to_all(gated.reshape(groups, share, head_dim), 'tensor', split_ax...]
  transfers between devices with their start and end apart: 10 -> 8, of which waited for: 4 -> 4; matrix products, arithmetic and copies ran while one was open for 0% -> 2% of each run, Pallas kernels for 10% -> 11%
where the time goes in v3:
time: 85.4 us; the launch traced here: 84.7 us
  starting transfers between devices  45.9 us (54%)
  waiting for transfers between devices  19.7 us (23%)
  Pallas kernels  16.5 us (19%)
  local copies, waits for them, and re-layouts  2.38 us (3%)
    all_to_all x1, starting transfers between devices, on_device(): lax.all_to_all(sent.reshape(replicas, capacity * cands, head_dim), 'repli...  16.8 us
    all_to_all x1, starting transfers between devices, on_device(): lax.all_to_all(answers.reshape(replicas, capacity * cands, head_dim), 're...  10.3 us
    all_to_all x1, waiting for transfers between devices, on_device(): lax.all_to_all(gated.reshape(groups, share, head_dim), 'tensor', split_ax...  9.35 us
    ppermute x3, starting transfers between devices, passed(): return lax.ppermute(piece, ('replica', 'tensor'), pairs)  8.23 us
    ppermute x2, starting transfers between devices, swapped(): return lax.ppermute(piece, 'replica', [(r, r ^ 1) for r in range(replicas)])  6.13 us
    all_to_all x1, waiting for transfers between devices, on_device(): lax.all_to_all(sent.reshape(replicas, capacity * cands, head_dim), 'repli...  5.33 us
    all_to_all x1, starting transfers between devices, on_device(): lax.all_to_all(gated.reshape(groups, share, head_dim), 'tensor', split_ax...  4.48 us
    pallas_call x1, Pallas kernels, on_device(): pl.pallas_call(functools.partial(send_kernel, capacity, cands, chunks), i...  4.45 us
  transfers between devices with their start and end apart: 8, of which 4 were waited for; matrix products, arithmetic and copies ran while one was open for 2% of the time, Pallas kernels for 11%

profile of v3, /device:TPU:6, one launch (start us, length us, event | category | flops | bytes accessed | tf_op | source)
XLA Modules:
  0.0 84.7 jit_solution(14119211001630178119)
XLA Ops:
  0.0 4.3 %collective-permute-start = (bf16[128,1024]{1,0:T(8,128)(2,1)}, bf16[128,1024]{1,0:T(8,128)(2,1)S(1)}, u32[]{:S(2)}, u32[]{:S(2)}) collective-permute-start(bf16[128,1024]{1,0:T(8,128)(2,1)} %bitcast.15), channel_id=1, source_target_pairs={{0,1},{1,2},{2,3},{3,4},{4,5},{5,6},{6,7},{7,0},{8,15},{9,8},{10,9... | collective-permute-start | bytes 786440 | tf_op jit(solution)/shard_map/ppermute | solution.py:280
  4.3 4.4 %send.1 = bf16[1024,128]{1,0:T(8,128)(2,1)} custom-call(bf16[512,1024]{1,0:T(8,128)(2,1)} %tokens_ref.5, bf16[1024,512]{1,0:T(8,128)(2,1)} %bitcast.25, s32[1,64]{1,0:T(1,128)} %bitcast.20, s32[1,64]{1,0:T(1,128)} %bitcast.28), custom_call_target="tpu_custom_call" | custom-call | tf_op jit(solution)/shard_map/send/pallas_call | solution.py:255
  8.7 0.0 copy-start
  8.7 16.8 %all-to-all-start = ((bf16[64,16,128]{2,1,0:T(8,128)(2,1)}), bf16[64,16,128]{2,1,0:T(8,128)(2,1)S(1)}, u32[]{:S(2)}, u32[]{:S(2)}) async-start(bf16[64,16,128]{2,1,0:T(8,128)(2,1)} %bitcast.27), calls=%async_computation | async-start | bytes 524288 | tf_op jit(solution)/shard_map/all_to_all | solution.py:272
  25.5 0.0 copy-start.3
  25.5 0.0 copy-start.4
  25.6 0.0 collective-permute-done.one_ref
  25.6 0.0 copy-done
  25.6 2.1 %collective-permute-start.1 = (bf16[256,1024]{1,0:T(8,128)(2,1)S(1)}, bf16[256,1024]{1,0:T(8,128)(2,1)}, u32[]{:S(2)}, u32[]{:S(2)}) collective-permute-start(bf16[256,1024]{1,0:T(8,128)(2,1)S(1)} %pad_maximum_fusion), channel_id=1, source_target_pairs={{0,2},{1,3},{2,4},{3,5},{4,6},{5,7},{6,0},{7,1},{8,14},{9,15},{10,... | collective-permute-start | bytes 1572872 | tf_op jit(solution)/shard_map/ppermute | solution.py:280
  27.7 4.1 %collective-permute-start.2 = (bf16[128,1024]{1,0:T(8,128)(2,1)S(1)}, bf16[128,1024]{1,0:T(8,128)(2,1)S(1)}, u32[]{:S(2)}, u32[]{:S(2)}) collective-permute-start(bf16[128,1024]{1,0:T(8,128)(2,1)S(1)} %collective-permute-done.one_ref), channel_id=1, source_target_pairs={{0,8},{8,0},{16,24},{24,16},{32,40},{40,32},{48,56},{56,48},{64,72... | collective-permute-start | bytes 786440 | tf_op jit(solution)/shard_map/ppermute | solution.py:283
  31.8 5.3 %all-to-all-done = bf16[64,16,128]{2,1,0:T(8,128)(2,1)S(1)} async-done(((bf16[64,16,128]{2,1,0:T(8,128)(2,1)}), bf16[64,16,128]{2,1,0:T(8,128)(2,1)S(1)}, u32[]{:S(2)}, u32[]{:S(2)}) %all-to-all-start) | async-done | bytes 262176 | tf_op jit(solution)/shard_map/all_to_all | solution.py:272
  37.1 0.0 copy-start.1
  37.1 0.0 copy-start.2
  37.1 0.0 copy-done.3
  37.1 0.0 copy-done.4
  37.1 0.6 copy-done.1
  37.7 0.0 copy-done.2
  37.8 3.0 %history.1 = bf16[1024,128]{1,0:T(8,128)(2,1)} custom-call(s32[1]{0:T(128)} %bitcast.1.me_ref, s32[64]{0:T(128)S(1)} %copy-done.1, s32[64]{0:T(128)S(1)} %copy-done.2, bf16[1024,128]{1,0:T(8,128)(2,1)S(1)} %bitcast.19, bf16[1024,128]{1,0:T(8,128)(2,1)S(1)} %bitcast.23, bf16[1024,128]{1,0:T(8,128)(2,1)S(1)} %bitcast.24), custom_call_target="tpu_custom_call" | custom-call | flops 1073741824 | bytes 67108864 | tf_op jit(solution)/shard_map/history/pallas_call | solution.py:291
  40.8 0.0 collective-permute-done.2.other_one_ref
  40.8 0.0 copy-start.5
  40.8 3.0 %collective-permute-done.1.two_ref = bf16[256,1024]{1,0:T(8,128)(2,1)} collective-permute-done((bf16[256,1024]{1,0:T(8,128)(2,1)S(1)}, bf16[256,1024]{1,0:T(8,128)(2,1)}, u32[]{:S(2)}, u32[]{:S(2)}) %collective-permute-start.1) | collective-permute-done | bytes 524320 | tf_op jit(solution)/shard_map/ppermute | solution.py:280
  43.8 0.0 copy-done.5
  43.8 10.3 %all-to-all-start.1 = ((bf16[64,16,128]{2,1,0:T(8,128)(2,1)}), bf16[64,16,128]{2,1,0:T(8,128)(2,1)S(1)}, u32[]{:S(2)}, u32[]{:S(2)}) async-start(bf16[64,16,128]{2,1,0:T(8,128)(2,1)} %bitcast.10), calls=%async_computation.1 | async-start | bytes 524288 | tf_op jit(solution)/shard_map/all_to_all | solution.py:329
  54.1 2.1 %collective-permute-start.4 = (bf16[256,1024]{1,0:T(8,128)(2,1)}, bf16[256,1024]{1,0:T(8,128)(2,1)}, u32[]{:S(2)}, u32[]{:S(2)}) collective-permute-start(bf16[256,1024]{1,0:T(8,128)(2,1)} %collective-permute-done.1.two_ref), channel_id=1, source_target_pairs={{0,8},{8,0},{16,24},{24,16},{32,40},{40,32},{48,56},{56,48},{64,72... | collective-permute-start | bytes 1572872 | tf_op jit(solution)/shard_map/ppermute | solution.py:283
  56.2 1.7 %slice.3 = bf16[128,1024]{1,0:T(8,128)(2,1)} slice(bf16[256,1024]{1,0:T(8,128)(2,1)} %collective-permute-done.1.two_ref), slice={[128:256], [0:1024]} | slice | bytes 524288 | tf_op jit(solution)/shard_map/slice | solution.py:315
  57.9 1.9 %collective-permute-start.3 = (bf16[128,1024]{1,0:T(8,128)(2,1)}, bf16[128,1024]{1,0:T(8,128)(2,1)}, u32[]{:S(2)}, u32[]{:S(2)}) collective-permute-start(bf16[128,1024]{1,0:T(8,128)(2,1)} %slice.3), channel_id=1, source_target_pairs={{0,1},{1,2},{2,3},{3,4},{4,5},{5,6},{6,7},{7,0},{8,15},{9,8},{10,9... | collective-permute-start | bytes 786440 | tf_op jit(solution)/shard_map/ppermute | solution.py:280
  59.8 3.9 %local.1.mine_ref = f32[512,384]{1,0:T(8,128)} custom-call(bf16[512,1024]{1,0:T(8,128)(2,1)} %tokens_ref.5, bf16[1024,512]{1,0:T(8,128)(2,1)} %bitcast.26, s32[1,64]{1,0:T(1,128)} %bitcast.21, s32[1,64]{1,0:T(1,128)} %bitcast.29, s32[1,64]{1,0:T(1,128)} %bitcast.30, s32[1,64]{1,0:T(1,128)} %bitcast.22), custom_call_target="tpu_custom_call" | custom-call | flops 536870912 | bytes 4194304 | tf_op jit(solution)/shard_map/local/pallas_call | solution.py:317
  63.7 2.0 %all-to-all-done.1 = bf16[64,16,128]{2,1,0:T(8,128)(2,1)S(1)} async-done(((bf16[64,16,128]{2,1,0:T(8,128)(2,1)}), bf16[64,16,128]{2,1,0:T(8,128)(2,1)S(1)}, u32[]{:S(2)}, u32[]{:S(2)}) %all-to-all-start.1) | async-done | bytes 262176 | tf_op jit(solution)/shard_map/all_to_all | solution.py:329
  65.7 2.7 %gate.1 = bf16[512,128]{1,0:T(8,128)(2,1)} custom-call(bf16[1024,128]{1,0:T(8,128)(2,1)S(1)} %bitcast.18, f32[512,384]{1,0:T(8,128)} %local.1.mine_ref), custom_call_target="tpu_custom_call" | custom-call | tf_op jit(solution)/shard_map/gate/pallas_call | solution.py:332
  68.4 4.5 %all-to-all-start.2 = ((bf16[8,64,128]{2,1,0:T(8,128)(2,1)}), bf16[8,64,128]{2,1,0:T(8,128)(2,1)S(1)}, u32[]{:S(2)}, u32[]{:S(2)}) async-start(bf16[8,64,128]{2,1,0:T(8,128)(2,1)} %bitcast.14), calls=%async_computation.2 | async-start | bytes 262144 | tf_op jit(solution)/shard_map/all_to_all | solution.py:347
  72.9 0.0 collective-permute-done.3.last_ref
  72.9 0.0 collective-permute-done.4.other_two_ref
  72.9 9.3 %all-to-all-done.2.gated_ref = bf16[8,64,128]{2,1,0:T(8,128)(2,1)S(1)} async-done(((bf16[8,64,128]{2,1,0:T(8,128)(2,1)}), bf16[8,64,128]{2,1,0:T(8,128)(2,1)S(1)}, u32[]{:S(2)}, u32[]{:S(2)}) %all-to-all-start.2) | async-done | bytes 131104 | tf_op jit(solution)/shard_map/all_to_all | solution.py:347
  82.2 2.5 %output.1 = bf16[64,1024]{1,0:T(8,128)(2,1)} custom-call(s32[1]{0:T(128)} %bitcast.group_ref, s32[1]{0:T(128)} %bitcast.1.me_ref, bf16[512,1024]{1,0:T(8,128)(2,1)} %tokens_ref.5, bf16[8,64,128]{2,1,0:T(8,128)(2,1)S(1)} %all-to-all-done.2.gated_ref, bf16[128,1024]{1,0:T(8,128)(2,1)S(1)} %bitcast.17, bf16[128,1024]{1,0:T(8,128)(2,1)S(1)} %collective-permute-done.one_ref, ...), custom_call_target="tpu_custom_call" | custom-call | tf_op jit(solution)/shard_map/output/pallas_call | solution.py:350
  (1 shorter events, 0.0 us)
Async XLA Ops:
  0.0 25.6 %collective-permute-start = (bf16[128,1024]{1,0:T(8,128)(2,1)}, bf16[128,1024]{1,0:T(8,128)(2,1)S(1)}, u32[]{:S(2)}, u32[]{:S(2)}) collective-permute-start(bf16[128,1024]{1,0:T(8,128)(2,1)} %bitcast.15), channel_id=1, source_target_pairs={{0,1},{1,2},{2,3},{3,4},{4,5},{5,6},{6,7},{7,0},{8,15},{9,8},{10,9... | collective-permute-start | bytes 786440 | tf_op jit(solution)/shard_map/ppermute | solution.py:280
  8.7 16.8 %copy-start = (bf16[1,128,1024]{2,1,0:T(8,128)(2,1)S(1)}, bf16[1,128,1024]{2,1,0:T(8,128)(2,1)}, u32[]{:S(2)}) copy-start(bf16[1,128,1024]{2,1,0:T(8,128)(2,1)} %param.11) | copy-start | bytes 786436
  8.7 28.3 %all-to-all-start = ((bf16[64,16,128]{2,1,0:T(8,128)(2,1)}), bf16[64,16,128]{2,1,0:T(8,128)(2,1)S(1)}, u32[]{:S(2)}, u32[]{:S(2)}) async-start(bf16[64,16,128]{2,1,0:T(8,128)(2,1)} %bitcast.27), calls=%async_computation | async-start | bytes 524288 | tf_op jit(solution)/shard_map/all_to_all | solution.py:272
  25.5 11.6 %copy-start.3 = (bf16[1,1024,1,128]{3,1,2,0:T(8,128)(2,1)S(1)}, bf16[1,1024,1,128]{3,1,2,0:T(8,128)(2,1)}, u32[]{:S(2)}) copy-start(bf16[1,1024,1,128]{3,1,2,0:T(8,128)(2,1)} %param.12) | copy-start | bytes 786436
  25.5 11.6 %copy-start.4 = (bf16[1,1024,1,128]{3,1,2,0:T(8,128)(2,1)S(1)}, bf16[1,1024,1,128]{3,1,2,0:T(8,128)(2,1)}, u32[]{:S(2)}) copy-start(bf16[1,1024,1,128]{3,1,2,0:T(8,128)(2,1)} %param.13) | copy-start | bytes 786436
  25.6 18.2 %collective-permute-start.1 = (bf16[256,1024]{1,0:T(8,128)(2,1)S(1)}, bf16[256,1024]{1,0:T(8,128)(2,1)}, u32[]{:S(2)}, u32[]{:S(2)}) collective-permute-start(bf16[256,1024]{1,0:T(8,128)(2,1)S(1)} %pad_maximum_fusion), channel_id=1, source_target_pairs={{0,2},{1,3},{2,4},{3,5},{4,6},{5,7},{6,0},{7,1},{8,14},{9,15},{10,... | collective-permute-start | bytes 1572872 | tf_op jit(solution)/shard_map/ppermute | solution.py:280
  27.7 13.1 %collective-permute-start.2 = (bf16[128,1024]{1,0:T(8,128)(2,1)S(1)}, bf16[128,1024]{1,0:T(8,128)(2,1)S(1)}, u32[]{:S(2)}, u32[]{:S(2)}) collective-permute-start(bf16[128,1024]{1,0:T(8,128)(2,1)S(1)} %collective-permute-done.one_ref), channel_id=1, source_target_pairs={{0,8},{8,0},{16,24},{24,16},{32,40},{40,32},{48,56},{56,48},{64,72... | collective-permute-start | bytes 786440 | tf_op jit(solution)/shard_map/ppermute | solution.py:283
  37.1 0.7 copy-start.1
  37.1 0.7 copy-start.2
  40.8 3.0 %copy-start.5 = (bf16[128,1024]{1,0:T(8,128)(2,1)}, bf16[128,1024]{1,0:T(8,128)(2,1)S(1)}, u32[]{:S(2)}) copy-start(bf16[128,1024]{1,0:T(8,128)(2,1)S(1)} %collective-permute-done.2.other_one_ref) | copy-start | bytes 786436
  43.8 21.9 %all-to-all-start.1 = ((bf16[64,16,128]{2,1,0:T(8,128)(2,1)}), bf16[64,16,128]{2,1,0:T(8,128)(2,1)S(1)}, u32[]{:S(2)}, u32[]{:S(2)}) async-start(bf16[64,16,128]{2,1,0:T(8,128)(2,1)} %bitcast.10), calls=%async_computation.1 | async-start | bytes 524288 | tf_op jit(solution)/shard_map/all_to_all | solution.py:329
  54.1 18.8 %collective-permute-start.4 = (bf16[256,1024]{1,0:T(8,128)(2,1)}, bf16[256,1024]{1,0:T(8,128)(2,1)}, u32[]{:S(2)}, u32[]{:S(2)}) collective-permute-start(bf16[256,1024]{1,0:T(8,128)(2,1)} %collective-permute-done.1.two_ref), channel_id=1, source_target_pairs={{0,8},{8,0},{16,24},{24,16},{32,40},{40,32},{48,56},{56,48},{64,72... | collective-permute-start | bytes 1572872 | tf_op jit(solution)/shard_map/ppermute | solution.py:283
  57.9 15.0 %collective-permute-start.3 = (bf16[128,1024]{1,0:T(8,128)(2,1)}, bf16[128,1024]{1,0:T(8,128)(2,1)}, u32[]{:S(2)}, u32[]{:S(2)}) collective-permute-start(bf16[128,1024]{1,0:T(8,128)(2,1)} %slice.3), channel_id=1, source_target_pairs={{0,1},{1,2},{2,3},{3,4},{4,5},{5,6},{6,7},{7,0},{8,15},{9,8},{10,9... | collective-permute-start | bytes 786440 | tf_op jit(solution)/shard_map/ppermute | solution.py:280
  68.4 13.8 %all-to-all-start.2 = ((bf16[8,64,128]{2,1,0:T(8,128)(2,1)}), bf16[8,64,128]{2,1,0:T(8,128)(2,1)S(1)}, u32[]{:S(2)}, u32[]{:S(2)}) async-start(bf16[8,64,128]{2,1,0:T(8,128)(2,1)} %bitcast.14), calls=%async_computation.2 | async-start | bytes 262144 | tf_op jit(solution)/shard_map/all_to_all | solution.py:347

commit v4 on v3

--- a/solution.py
+++ b/solution.py
@@ -48,7 +48,8 @@
 
 
 def send_kernel(
-    capacity, cands, chunks, tokens_ref, w_ref, slot_ref, session_ref, sent_ref, held, weight, queries, placed, sems, w_sem, out_sems
+    capacity, cands, chunks, tokens_ref, w_ref, slot_ref, session_ref, length_ref, me_ref, sent_ref, info_ref,
+    held, weight, queries, placed, info, sems, w_sem, out_sems,
 ):
     rows = tokens_ref.shape[0]
     head_dim = weight.shape[1]
@@ -65,6 +66,11 @@
     fetch_w.start()
     for fetch in fetches[1:]:
         fetch.start()
+    own = slot_ref[...] == me_ref[0]
+    length = jnp.sum(jnp.where(own, length_ref[...].astype(f32), 0.0), 1, keepdims=True)
+    info[...] = jnp.broadcast_to(length, info.shape)
+    stores = [pltpu.make_async_copy(info, info_ref, out_sems.at[chunks])]
+    stores[0].start()
     first = first_rows(slot_ref, session_ref, capacity, cands)
     requests = first.shape[1]
     spread = iota((requests, rows), 1) // cands == iota((requests, rows), 0)
@@ -78,7 +84,6 @@
             fetch_w.wait()
         queries[part, :] = silu(jnp.dot(normed, weight[...], preferred_element_type=f32)).astype(bf16)
     block = slot_rows // chunks
-    stores = []
     for n in range(chunks):
         part = pl.ds(n * block, block)
         chosen = jnp.where(iota((block, rows), 0) + n * block == place, 1.0, 0.0).astype(bf16)
@@ -120,24 +125,23 @@
 
 
 def history_kernel(
-    block, me_ref, slot_ref, length_ref, query_ref, keys_ref, values_ref, out_ref, query, keys, values, result, sems
+    block, info_ref, query_ref, keys_ref, values_ref, out_ref, info, query, keys, values, result, sems
 ):
     fetches = [
         pltpu.make_async_copy(source, target, sems.at[n])
-        for n, (source, target) in enumerate(((keys_ref, keys), (query_ref, query), (values_ref, values)))
+        for n, (source, target) in enumerate(
+            ((info_ref, info), (query_ref, query), (keys_ref, keys), (values_ref, values))
+        )
     ]
     for fetch in fetches:
         fetch.start()
     history, head_dim = keys_ref.shape
-    length = jnp.zeros((), jnp.int32)
-    for session in range(slot_ref.shape[0]):
-        length = jnp.where(slot_ref[session] == me_ref[0], length_ref[session], length)
-    seen = iota((history, 1), 0) < length
-    divisor = (length + 1).astype(f32)
     half_scale = 0.5 * head_dim ** (-0.5)
-    fetches[0].wait()
-    fetches[1].wait()
-    fetches[2].wait()
+    for fetch in fetches:
+        fetch.wait()
+    length = info[:1, :1]
+    divisor = length + 1.0
+    seen = iota((history, 1), 0).astype(f32) < length
     seen_values = jnp.where(seen, values[...], jnp.zeros((), bf16))
     stores = []
     for n, start in enumerate(range(0, query_ref.shape[0], block)):
@@ -149,7 +153,7 @@
         weights = (half + half * jnp.tanh(half)).astype(bf16)
         summed = jnp.dot(weights, seen_values, preferred_element_type=f32)
         result[part, :] = (summed / divisor).astype(bf16)
-        stores.append(pltpu.make_async_copy(result.at[part, :], out_ref.at[part, :], sems.at[3 + n]))
+        stores.append(pltpu.make_async_copy(result.at[part, :], out_ref.at[part, :], sems.at[4 + n]))
         stores[-1].start()
     for store in stores:
         store.wait()
@@ -179,34 +183,32 @@
 
 
 def output_kernel(
-    group_ref, me_ref, tokens_ref, gated_ref, own_ref, one_ref, two_ref, last_ref, other_one_ref, other_two_ref,
+    group_ref, me_ref, tokens_ref, gated_ref, own_ref, next_ref, last_ref, other_ref,
     out_ref, gated, weight, tokens, result, sems,
 ):
     groups, share, head_dim = gated_ref.shape
     group = group_ref[0]
     sign = jnp.where(me_ref[0] % 2 == 0, -1, 1)
+    double = 2 * head_dim
     fetches = [pltpu.make_async_copy(gated_ref, gated, sems.at[0])]
     start = 0
-    for n, piece in enumerate((own_ref, one_ref, two_ref, last_ref, other_one_ref, other_two_ref)):
-        size = piece.shape[0]
-        fetches.append(pltpu.make_async_copy(piece, weight.at[pl.ds(start, size), :], sems.at[1 + n]))
+    for n, source in enumerate((own_ref, next_ref, last_ref, other_ref)):
+        size = source.shape[0]
+        fetches.append(pltpu.make_async_copy(source, weight.at[pl.ds(start, size), :], sems.at[1 + n]))
         start += size
     mine = pl.ds(pl.multiple_of(group * share, share), share)
-    fetch_tokens = pltpu.make_async_copy(tokens_ref.at[mine, :], tokens, sems.at[7])
+    fetch_tokens = pltpu.make_async_copy(tokens_ref.at[mine, :], tokens, sems.at[5])
     for fetch in fetches:
         fetch.start()
     fetch_tokens.start()
     total = jnp.zeros(result.shape, f32)
-    fetches[0].wait()
-    for n, heads in enumerate(held_heads):
-        for fetch in (fetches[1:3], fetches[3:4], fetches[4:6], fetches[6:7])[n]:
+    for pair, waits in enumerate((fetches[:3], (), fetches[3:], ())):
+        for fetch in waits:
             fetch.wait()
-        pair = jnp.concatenate(
-            [gated[lax.rem(group + sign * head + groups, groups)] for head in heads], axis=1
+        rows = jnp.concatenate(
+            [gated[lax.rem(group + sign * head + groups, groups)] for head in held_heads[pair]], axis=1
         )
-        total = total + jnp.dot(
-            pair, weight[pl.ds(2 * n * head_dim, 2 * head_dim), :], preferred_element_type=f32
-        )
+        total = total + jnp.dot(rows, weight[pl.ds(pair * double, double), :], preferred_element_type=f32)
     fetch_tokens.wait()
     result[...] = (tokens[...].astype(f32) + total).astype(bf16)
     store = pltpu.make_async_copy(result, out_ref, sems.at[0])
@@ -221,6 +223,10 @@
 params = pltpu.CompilerParams(vmem_limit_bytes=63 * 1024 * 1024)
 tight = pltpu.CompilerParams(vmem_limit_bytes=54528 * 1024)
 roomy = pltpu.CompilerParams(vmem_limit_bytes=24 * 1024 * 1024)
+
+
+def after(value, other):
+    return lax.optimization_barrier((value, other))[0]
 
 
 def on_device(
@@ -252,23 +258,24 @@
     counts = cand_count.reshape(1, -1)
     chunks = 4
 
-    sent = pl.pallas_call(
+    sent, info = pl.pallas_call(
         functools.partial(send_kernel, capacity, cands, chunks),
-        in_specs=[HBM, HBM, VMEM, VMEM],
-        out_specs=HBM,
-        out_shape=jax.ShapeDtypeStruct((slot_rows, head_dim), bf16),
+        in_specs=[HBM, HBM, VMEM, VMEM, VMEM, SMEM],
+        out_specs=[HBM, HBM],
+        out_shape=[jax.ShapeDtypeStruct((slot_rows, head_dim), bf16), jax.ShapeDtypeStruct((8, 128), f32)],
         scratch_shapes=[
             pltpu.VMEM((rows, model_width), bf16),
             pltpu.VMEM((model_width, head_dim), bf16),
             pltpu.VMEM((rows, head_dim), bf16),
             pltpu.VMEM((slot_rows, head_dim), bf16),
+            pltpu.VMEM((8, 128), f32),
             pltpu.SemaphoreType.DMA((chunks,)),
             pltpu.SemaphoreType.DMA,
-            pltpu.SemaphoreType.DMA((chunks,)),
+            pltpu.SemaphoreType.DMA((chunks + 1,)),
         ],
         compiler_params=params,
         name="send",
-    )(tokens, w_flat, slots, named)
+    )(tokens, w_flat, slots, named, lengths, my_index)
     got = lax.all_to_all(
         sent.reshape(replicas, capacity * cands, head_dim), "replica", split_axis=0, concat_axis=0, tiled=True
     )
@@ -282,38 +289,34 @@
     def swapped(piece):
         return lax.ppermute(piece, "replica", [(r, r ^ 1) for r in range(replicas)])
 
-    w_own = w_out.reshape(head_dim, model_width)
-    next_one = passed(w_own, 1)
-    w_own, next_one, sent = lax.optimization_barrier((w_own, next_one, sent))
-    next_two = passed(jnp.concatenate([w_own, next_one], axis=0), 2)
-    other_one = swapped(next_one)
+    w_own = after(w_out.reshape(head_dim, model_width), sent)
+    nexts = [passed(w_own, by) for by in range(1, groups // 2)]
     block = min(256, slot_rows)
     answers = pl.pallas_call(
         functools.partial(history_kernel, block),
-        in_specs=[SMEM, SMEM, SMEM, ANY, HBM, HBM],
+        in_specs=[HBM, ANY, HBM, HBM],
         out_specs=HBM,
         out_shape=jax.ShapeDtypeStruct((slot_rows, head_dim), bf16),
         scratch_shapes=[
+            pltpu.VMEM((8, 128), f32),
             pltpu.VMEM((slot_rows, head_dim), bf16),
             pltpu.VMEM((history, head_dim), bf16),
             pltpu.VMEM((history, head_dim), bf16),
             pltpu.VMEM((slot_rows, head_dim), bf16),
-            pltpu.SemaphoreType.DMA((3 + slot_rows // block,)),
+            pltpu.SemaphoreType.DMA((4 + slot_rows // block,)),
         ],
-        compiler_params=roomy,
+        compiler_params=tight,
         cost_estimate=pl.CostEstimate(flops=1 << 30, bytes_accessed=64 << 20, transcendentals=slot_rows * history),
         name="history",
     )(
-        my_index,
-        session_slot,
-        hist_len,
+        info,
         got.reshape(slot_rows, head_dim),
         cache_keys.reshape(history, head_dim),
         cache_values.reshape(history, head_dim),
     )
-    next_two, other_one, named_later, answers = lax.optimization_barrier((next_two, other_one, named, answers))
-    last = passed(next_two[head_dim:], 1)
-    other_two = swapped(next_two)
+    nexts = jnp.concatenate([after(piece, answers) for piece in nexts], axis=0)
+    last = passed(nexts[-head_dim:], 1)
+    others = swapped(nexts)
     mine = pl.pallas_call(
         functools.partial(local_kernel, capacity, cands),
         in_specs=[VMEM] * 6,
@@ -321,11 +324,9 @@
         out_shape=jax.ShapeDtypeStruct((rows, 3 * head_dim), f32),
         scratch_shapes=[pltpu.VMEM((rows, 3 * head_dim), f32), pltpu.SemaphoreType.DMA],
         compiler_params=params,
-        cost_estimate=pl.CostEstimate(
-            flops=2 * rows * model_width * 4 * head_dim, bytes_accessed=4 << 20, transcendentals=rows * 4 * head_dim
-        ),
+        cost_estimate=pl.CostEstimate(flops=1 << 30, bytes_accessed=16 << 20, transcendentals=1 << 18),
         name="local",
-    )(tokens, w_flat, slots, named_later, counts, lengths)
+    )(tokens, w_flat, slots, after(named, answers), counts, lengths)
     returned = lax.all_to_all(
         answers.reshape(replicas, capacity * cands, head_dim), "replica", split_axis=0, concat_axis=0, tiled=True
     )
@@ -341,6 +342,7 @@
             pltpu.SemaphoreType.DMA((2,)),
         ],
         compiler_params=tight,
+        cost_estimate=pl.CostEstimate(flops=1 << 30, bytes_accessed=64 << 20, transcendentals=1 << 10),
         name="gate",
     )(returned.reshape(slot_rows, head_dim), mine)
     share = rows // groups
@@ -349,7 +351,7 @@
     )
     return pl.pallas_call(
         output_kernel,
-        in_specs=[SMEM, SMEM, HBM] + [ANY] * 7,
+        in_specs=[SMEM, SMEM, HBM] + [ANY] * 5,
         out_specs=HBM,
         out_shape=jax.ShapeDtypeStruct((share, model_width), bf16),
         scratch_shapes=[
@@ -357,11 +359,11 @@
             pltpu.VMEM((groups * head_dim, model_width), bf16),
             pltpu.VMEM((share, model_width), bf16),
             pltpu.VMEM((share, model_width), bf16),
-            pltpu.SemaphoreType.DMA((8,)),
+            pltpu.SemaphoreType.DMA((6,)),
         ],
         compiler_params=tight,
         name="output",
-    )(group_index, my_index, tokens, heads, w_own, next_one, next_two, last, other_one, other_two)
+    )(group_index, my_index, tokens, heads, w_own, nexts, last, others)
 
 
 def solution(mesh):

time: 85.4 us -> 78.6 us (0.920)
  waiting for transfers between devices: 19.7 us -> 9.42 us
  starting transfers between devices: 45.9 us -> 48.2 us
    ppermute x3 -> x4, starting transfers between devices: 8.23 us -> 21.1 us  [passed(): return lax.ppermute(piece, ('replica', 'tensor'), pairs)]
    all_to_all x1, starting transfers between devices: 16.8 us -> 10.9 us  [on_device(): lax.all_to_all(sent.reshape(replicas, capacity * cands, head_dim), 'repli...]
    all_to_all x1, waiting for transfers between devices: 5.33 us -> 0.01 us  [on_device(): lax.all_to_all(sent.reshape(replicas, capacity * cands, head_dim), 'repli...]
    ppermute x2 -> x1, starting transfers between devices: 6.13 us -> 2.05 us  [swapped(): return lax.ppermute(piece, 'replica', [(r, r ^ 1) for r in range(replicas)])]
    ppermute x3 -> x4, waiting for transfers between devices: 2.98 us -> 0.01 us  [passed(): return lax.ppermute(piece, ('replica', 'tensor'), pairs)]
    all_to_all x1, waiting for transfers between devices: 2 us -> 0.01 us  [on_device(): lax.all_to_all(answers.reshape(replicas, capacity * cands, head_dim), 're...]
    slice x1 -> x0, local copies, waits for them, and re-layouts: 1.7 us -> none  [on_device(): last = passed(next_two[head_dim:], 1)]
    concatenate x0 -> x1, local copies, waits for them, and re-layouts: none -> 1.66 us  [on_device(): nexts = jnp.concatenate([after(piece, answers) for piece in nexts], axis=0)]
  transfers between devices with their start and end apart: 8 -> 8, of which waited for: 4 -> 1; matrix products, arithmetic and copies ran while one was open for 2% -> 4% of each run, Pallas kernels for 11% -> 13%
where the time goes in v4:
time: 78.6 us; the launch traced here: 77.9 us
  starting transfers between devices  48.2 us (61%)
  Pallas kernels  17 us (22%)
  waiting for transfers between devices  9.42 us (12%)
  local copies, waits for them, and re-layouts  3.14 us (4%)
    ppermute x4, starting transfers between devices, passed(): return lax.ppermute(piece, ('replica', 'tensor'), pairs)  21.1 us
    all_to_all x1, starting transfers between devices, on_device(): lax.all_to_all(sent.reshape(replicas, capacity * cands, head_dim), 'repli...  10.9 us
    all_to_all x1, starting transfers between devices, on_device(): lax.all_to_all(answers.reshape(replicas, capacity * cands, head_dim), 're...  10.3 us
    all_to_all x1, waiting for transfers between devices, on_device(): lax.all_to_all(gated.reshape(groups, share, head_dim), 'tensor', split_ax...  9.4 us
    pallas_call x1, Pallas kernels, on_device(): pl.pallas_call(functools.partial(send_kernel, capacity, cands, chunks), i...  4.47 us
    pallas_call x1, Pallas kernels, on_device(): pl.pallas_call(functools.partial(local_kernel, capacity, cands), in_specs...  3.89 us
    all_to_all x1, starting transfers between devices, on_device(): lax.all_to_all(gated.reshape(groups, share, head_dim), 'tensor', split_ax...  3.77 us
    pallas_call x1, Pallas kernels, on_device(): pl.pallas_call(functools.partial(history_kernel, block), in_specs=[HBM, A...  3.38 us
  transfers between devices with their start and end apart: 8, of which 1 were waited for; matrix products, arithmetic and copies ran while one was open for 4% of the time, Pallas kernels for 13%

profile of v4, /device:TPU:6, one launch (start us, length us, event | category | flops | bytes accessed | tf_op | source)
XLA Modules:
  0.0 77.9 jit_solution(18254486258652089932)
XLA Ops:
  0.0 4.5 %send.1 = (bf16[1024,128]{1,0:T(8,128)(2,1)}, f32[8,128]{1,0:T(8,128)}) custom-call(bf16[512,1024]{1,0:T(8,128)(2,1)} %tokens_ref.5, bf16[1024,512]{1,0:T(8,128)(2,1)} %bitcast.21, s32[1,64]{1,0:T(1,128)} %bitcast.24, s32[1,64]{1,0:T(1,128)} %bitcast.26, s32[1,64]{1,0:T(1,128)} %bitcast.28, s32[1]{0:T(128)} %bitcast.1.me_ref), custom_call_target="tpu_custom_call" | custom-call | tf_op jit(solution)/shard_map/send/pallas_call | solution.py:261
  4.5 0.0 copy-start
  4.5 10.9 %all-to-all-start = ((bf16[64,16,128]{2,1,0:T(8,128)(2,1)}), bf16[64,16,128]{2,1,0:T(8,128)(2,1)S(1)}, u32[]{:S(2)}, u32[]{:S(2)}) async-start(bf16[64,16,128]{2,1,0:T(8,128)(2,1)} %bitcast.23), calls=%async_computation | async-start | bytes 524288 | tf_op jit(solution)/shard_map/all_to_all | solution.py:279
  15.4 0.0 copy-done
  15.5 0.0 copy-start.1
  15.5 4.3 %collective-permute-start = (bf16[128,1024]{1,0:T(8,128)(2,1)S(1)}, bf16[128,1024]{1,0:T(8,128)(2,1)S(1)}, u32[]{:S(2)}, u32[]{:S(2)}) collective-permute-start(bf16[128,1024]{1,0:T(8,128)(2,1)S(1)} %bitcast.15), channel_id=1, source_target_pairs={{0,1},{1,2},{2,3},{3,4},{4,5},{5,6},{6,7},{7,0},{8,15},{9,8},{10,9... | collective-permute-start | bytes 786440 | tf_op jit(solution)/shard_map/ppermute | solution.py:287
  19.7 6.1 %collective-permute-start.1 = (bf16[128,1024]{1,0:T(8,128)(2,1)S(1)}, bf16[128,1024]{1,0:T(8,128)(2,1)S(1)}, u32[]{:S(2)}, u32[]{:S(2)}) collective-permute-start(bf16[128,1024]{1,0:T(8,128)(2,1)S(1)} %bitcast.16), channel_id=1, source_target_pairs={{0,2},{1,3},{2,4},{3,5},{4,6},{5,7},{6,0},{7,1},{8,14},{9,15},{10,... | collective-permute-start | bytes 786440 | tf_op jit(solution)/shard_map/ppermute | solution.py:287
  25.9 7.3 %collective-permute-start.2 = (bf16[128,1024]{1,0:T(8,128)(2,1)S(1)}, bf16[128,1024]{1,0:T(8,128)(2,1)}, u32[]{:S(2)}, u32[]{:S(2)}) collective-permute-start(bf16[128,1024]{1,0:T(8,128)(2,1)S(1)} %bitcast.17), channel_id=1, source_target_pairs={{0,3},{1,4},{2,5},{3,6},{4,7},{5,0},{6,1},{7,2},{8,13},{9,14},{10,... | collective-permute-start | bytes 786440 | tf_op jit(solution)/shard_map/ppermute | solution.py:287
  33.2 0.0 all-to-all-done
  33.2 0.0 copy-done.1
  33.2 3.4 %history.1 = bf16[1024,128]{1,0:T(8,128)(2,1)} custom-call(f32[8,128]{1,0:T(8,128)S(1)} %copy-done.1, bf16[1024,128]{1,0:T(8,128)(2,1)S(1)} %bitcast.20, bf16[1024,128]{1,0:T(8,128)(2,1)} %bitcast.30, bf16[1024,128]{1,0:T(8,128)(2,1)} %bitcast.31), custom_call_target="tpu_custom_call" | custom-call | flops 1073741824 | bytes 67108864 | tf_op jit(solution)/shard_map/history/pallas_call | solution.py:295
  36.6 10.3 %all-to-all-start.1 = ((bf16[64,16,128]{2,1,0:T(8,128)(2,1)}), bf16[64,16,128]{2,1,0:T(8,128)(2,1)S(1)}, u32[]{:S(2)}, u32[]{:S(2)}) async-start(bf16[64,16,128]{2,1,0:T(8,128)(2,1)} %bitcast.10), calls=%async_computation.1 | async-start | bytes 524288 | tf_op jit(solution)/shard_map/all_to_all | solution.py:330
  46.9 0.0 collective-permute-done
  46.9 0.0 collective-permute-done.1
  46.9 0.7 constant_dynamic-update-slice_fusion.2
  47.7 0.0 collective-permute-done.2
  47.7 0.7 constant_dynamic-update-slice_fusion.1
  48.4 1.7 %constant_dynamic-update-slice_fusion.next_ref = bf16[384,1024]{1,0:T(8,128)(2,1)} fusion(bf16[384,1024]{1,0:T(8,128)(2,1)} %constant_dynamic-update-slice_fusion.1, bf16[128,1024]{1,0:T(8,128)(2,1)} %collective-permute-done.2), kind=kLoop, calls=%fused_computation | loop fusion | bytes 524288 | tf_op jit(solution)/shard_map/concatenate | solution.py:317
  50.1 2.0 %collective-permute-start.4 = (bf16[384,1024]{1,0:T(8,128)(2,1)}, bf16[384,1024]{1,0:T(8,128)(2,1)}, u32[]{:S(2)}, u32[]{:S(2)}) collective-permute-start(bf16[384,1024]{1,0:T(8,128)(2,1)} %constant_dynamic-update-slice_fusion.next_ref), channel_id=1, source_target_pairs={{0,8},{8,0},{16,24},{24,16},{32,40},{40,32},{48,56},{56,48},{64,72... | collective-permute-start | bytes 2359304 | tf_op jit(solution)/shard_map/ppermute | solution.py:290
  52.1 3.4 %collective-permute-start.3 = (bf16[128,1024]{1,0:T(8,128)(2,1)}, bf16[128,1024]{1,0:T(8,128)(2,1)S(1)}, u32[]{:S(2)}, u32[]{:S(2)}) collective-permute-start(bf16[128,1024]{1,0:T(8,128)(2,1)} %collective-permute-done.2), channel_id=1, source_target_pairs={{0,1},{1,2},{2,3},{3,4},{4,5},{5,6},{6,7},{7,0},{8,15},{9,8},{10,9... | collective-permute-start | bytes 786440 | tf_op jit(solution)/shard_map/ppermute | solution.py:287
  55.5 3.9 %local.1.mine_ref = f32[512,384]{1,0:T(8,128)} custom-call(bf16[512,1024]{1,0:T(8,128)(2,1)} %tokens_ref.5, bf16[1024,512]{1,0:T(8,128)(2,1)} %bitcast.22, s32[1,64]{1,0:T(1,128)} %bitcast.25, s32[1,64]{1,0:T(1,128)} %bitcast.27, s32[1,64]{1,0:T(1,128)} %bitcast.32, s32[1,64]{1,0:T(1,128)} %bitcast.29), custom_call_target="tpu_custom_call" | custom-call | flops 1073741824 | bytes 16777216 | tf_op jit(solution)/shard_map/local/pallas_call | solution.py:320
  59.4 0.0 all-to-all-done.1
  59.4 2.7 %gate.1 = bf16[512,128]{1,0:T(8,128)(2,1)} custom-call(bf16[1024,128]{1,0:T(8,128)(2,1)S(1)} %bitcast.19, f32[512,384]{1,0:T(8,128)} %local.1.mine_ref), custom_call_target="tpu_custom_call" | custom-call | flops 1073741824 | bytes 67108864 | tf_op jit(solution)/shard_map/gate/pallas_call | solution.py:333
  62.1 3.8 %all-to-all-start.2 = ((bf16[8,64,128]{2,1,0:T(8,128)(2,1)}), bf16[8,64,128]{2,1,0:T(8,128)(2,1)S(1)}, u32[]{:S(2)}, u32[]{:S(2)}) async-start(bf16[8,64,128]{2,1,0:T(8,128)(2,1)} %bitcast.13), calls=%async_computation.2 | async-start | bytes 262144 | tf_op jit(solution)/shard_map/all_to_all | solution.py:349
  65.9 0.0 collective-permute-done.3.last_ref
  65.9 9.4 %all-to-all-done.2.gated_ref = bf16[8,64,128]{2,1,0:T(8,128)(2,1)S(1)} async-done(((bf16[8,64,128]{2,1,0:T(8,128)(2,1)}), bf16[8,64,128]{2,1,0:T(8,128)(2,1)S(1)}, u32[]{:S(2)}, u32[]{:S(2)}) %all-to-all-start.2) | async-done | bytes 131104 | tf_op jit(solution)/shard_map/all_to_all | solution.py:349
  75.3 0.0 collective-permute-done.4.other_ref
  75.3 2.6 %output.1 = bf16[64,1024]{1,0:T(8,128)(2,1)} custom-call(s32[1]{0:T(128)} %bitcast.group_ref, s32[1]{0:T(128)} %bitcast.1.me_ref, bf16[512,1024]{1,0:T(8,128)(2,1)} %tokens_ref.5, bf16[8,64,128]{2,1,0:T(8,128)(2,1)S(1)} %all-to-all-done.2.gated_ref, bf16[128,1024]{1,0:T(8,128)(2,1)S(1)} %bitcast.18, ...), custom_call_target="tpu_custom_call" | custom-call | tf_op jit(solution)/shard_map/output/pallas_call | solution.py:352
Async XLA Ops:
  4.5 11.0 %copy-start = (bf16[1,128,1024]{2,1,0:T(8,128)(2,1)S(1)}, bf16[1,128,1024]{2,1,0:T(8,128)(2,1)}, u32[]{:S(2)}) copy-start(bf16[1,128,1024]{2,1,0:T(8,128)(2,1)} %param.11) | copy-start | bytes 786436
  4.5 28.7 %all-to-all-start = ((bf16[64,16,128]{2,1,0:T(8,128)(2,1)}), bf16[64,16,128]{2,1,0:T(8,128)(2,1)S(1)}, u32[]{:S(2)}, u32[]{:S(2)}) async-start(bf16[64,16,128]{2,1,0:T(8,128)(2,1)} %bitcast.23), calls=%async_computation | async-start | bytes 524288 | tf_op jit(solution)/shard_map/all_to_all | solution.py:279
  15.5 17.7 %copy-start.1 = (f32[8,128]{1,0:T(8,128)S(1)}, f32[8,128]{1,0:T(8,128)}, u32[]{:S(2)}) copy-start(f32[8,128]{1,0:T(8,128)} %get-tuple-element.12.info_ref) | copy-start | bytes 12292
  15.5 31.5 %collective-permute-start = (bf16[128,1024]{1,0:T(8,128)(2,1)S(1)}, bf16[128,1024]{1,0:T(8,128)(2,1)S(1)}, u32[]{:S(2)}, u32[]{:S(2)}) collective-permute-start(bf16[128,1024]{1,0:T(8,128)(2,1)S(1)} %bitcast.15), channel_id=1, source_target_pairs={{0,1},{1,2},{2,3},{3,4},{4,5},{5,6},{6,7},{7,0},{8,15},{9,8},{10,9... | collective-permute-start | bytes 786440 | tf_op jit(solution)/shard_map/ppermute | solution.py:287
  19.7 27.2 %collective-permute-start.1 = (bf16[128,1024]{1,0:T(8,128)(2,1)S(1)}, bf16[128,1024]{1,0:T(8,128)(2,1)S(1)}, u32[]{:S(2)}, u32[]{:S(2)}) collective-permute-start(bf16[128,1024]{1,0:T(8,128)(2,1)S(1)} %bitcast.16), channel_id=1, source_target_pairs={{0,2},{1,3},{2,4},{3,5},{4,6},{5,7},{6,0},{7,1},{8,14},{9,15},{10,... | collective-permute-start | bytes 786440 | tf_op jit(solution)/shard_map/ppermute | solution.py:287
  25.9 21.8 %collective-permute-start.2 = (bf16[128,1024]{1,0:T(8,128)(2,1)S(1)}, bf16[128,1024]{1,0:T(8,128)(2,1)}, u32[]{:S(2)}, u32[]{:S(2)}) collective-permute-start(bf16[128,1024]{1,0:T(8,128)(2,1)S(1)} %bitcast.17), channel_id=1, source_target_pairs={{0,3},{1,4},{2,5},{3,6},{4,7},{5,0},{6,1},{7,2},{8,13},{9,14},{10,... | collective-permute-start | bytes 786440 | tf_op jit(solution)/shard_map/ppermute | solution.py:287
  36.6 22.8 %all-to-all-start.1 = ((bf16[64,16,128]{2,1,0:T(8,128)(2,1)}), bf16[64,16,128]{2,1,0:T(8,128)(2,1)S(1)}, u32[]{:S(2)}, u32[]{:S(2)}) async-start(bf16[64,16,128]{2,1,0:T(8,128)(2,1)} %bitcast.10), calls=%async_computation.1 | async-start | bytes 524288 | tf_op jit(solution)/shard_map/all_to_all | solution.py:330
  50.1 25.2 %collective-permute-start.4 = (bf16[384,1024]{1,0:T(8,128)(2,1)}, bf16[384,1024]{1,0:T(8,128)(2,1)}, u32[]{:S(2)}, u32[]{:S(2)}) collective-permute-start(bf16[384,1024]{1,0:T(8,128)(2,1)} %constant_dynamic-update-slice_fusion.next_ref), channel_id=1, source_target_pairs={{0,8},{8,0},{16,24},{24,16},{32,40},{40,32},{48,56},{56,48},{64,72... | collective-permute-start | bytes 2359304 | tf_op jit(solution)/shard_map/ppermute | solution.py:290
  52.1 13.8 %collective-permute-start.3 = (bf16[128,1024]{1,0:T(8,128)(2,1)}, bf16[128,1024]{1,0:T(8,128)(2,1)S(1)}, u32[]{:S(2)}, u32[]{:S(2)}) collective-permute-start(bf16[128,1024]{1,0:T(8,128)(2,1)} %collective-permute-done.2), channel_id=1, source_target_pairs={{0,1},{1,2},{2,3},{3,4},{4,5},{5,6},{6,7},{7,0},{8,15},{9,8},{10,9... | collective-permute-start | bytes 786440 | tf_op jit(solution)/shard_map/ppermute | solution.py:287
  62.1 13.2 %all-to-all-start.2 = ((bf16[8,64,128]{2,1,0:T(8,128)(2,1)}), bf16[8,64,128]{2,1,0:T(8,128)(2,1)S(1)}, u32[]{:S(2)}, u32[]{:S(2)}) async-start(bf16[8,64,128]{2,1,0:T(8,128)(2,1)} %bitcast.13), calls=%async_computation.2 | async-start | bytes 262144 | tf_op jit(solution)/shard_map/all_to_all | solution.py:349

commit v5 on v4

--- a/solution.py
+++ b/solution.py
@@ -183,7 +183,7 @@
 
 
 def output_kernel(
-    group_ref, me_ref, tokens_ref, gated_ref, own_ref, next_ref, last_ref, other_ref,
+    group_ref, me_ref, tokens_ref, gated_ref, own_ref, next_ref, last_ref, other_ref, three_ref,
     out_ref, gated, weight, tokens, result, sems,
 ):
     groups, share, head_dim = gated_ref.shape
@@ -192,17 +192,17 @@
     double = 2 * head_dim
     fetches = [pltpu.make_async_copy(gated_ref, gated, sems.at[0])]
     start = 0
-    for n, source in enumerate((own_ref, next_ref, last_ref, other_ref)):
+    for n, source in enumerate((own_ref, next_ref, last_ref, other_ref, three_ref)):
         size = source.shape[0]
         fetches.append(pltpu.make_async_copy(source, weight.at[pl.ds(start, size), :], sems.at[1 + n]))
         start += size
     mine = pl.ds(pl.multiple_of(group * share, share), share)
-    fetch_tokens = pltpu.make_async_copy(tokens_ref.at[mine, :], tokens, sems.at[5])
+    fetch_tokens = pltpu.make_async_copy(tokens_ref.at[mine, :], tokens, sems.at[6])
     for fetch in fetches:
         fetch.start()
     fetch_tokens.start()
     total = jnp.zeros(result.shape, f32)
-    for pair, waits in enumerate((fetches[:3], (), fetches[3:], ())):
+    for pair, waits in enumerate((fetches[:3], fetches[3:4], fetches[4:5], fetches[5:])):
         for fetch in waits:
             fetch.wait()
         rows = jnp.concatenate(
@@ -279,18 +279,29 @@
     got = lax.all_to_all(
         sent.reshape(replicas, capacity * cands, head_dim), "replica", split_axis=0, concat_axis=0, tiled=True
     )
-    def passed(piece, by):
+    def passed(piece, by, flip=0):
         pairs = []
         for r in range(replicas):
             for z in range(groups):
-                pairs.append((r * groups + z, r * groups + (z + (by if r % 2 == 0 else -by)) % groups))
+                pairs.append((r * groups + z, (r ^ flip) * groups + (z + (by if r % 2 == 0 else -by)) % groups))
         return lax.ppermute(piece, ("replica", "tensor"), pairs)
 
     def swapped(piece):
         return lax.ppermute(piece, "replica", [(r, r ^ 1) for r in range(replicas)])
 
     w_own = after(w_out.reshape(head_dim, model_width), sent)
-    nexts = [passed(w_own, by) for by in range(1, groups // 2)]
+    next_one = passed(w_own, 1)
+    next_two = passed(w_own, 2)
+    mine = pl.pallas_call(
+        functools.partial(local_kernel, capacity, cands),
+        in_specs=[VMEM] * 6,
+        out_specs=HBM,
+        out_shape=jax.ShapeDtypeStruct((rows, 3 * head_dim), f32),
+        scratch_shapes=[pltpu.VMEM((rows, 3 * head_dim), f32), pltpu.SemaphoreType.DMA],
+        compiler_params=params,
+        cost_estimate=pl.CostEstimate(flops=1 << 30, bytes_accessed=16 << 20, transcendentals=1 << 18),
+        name="local",
+    )(tokens, w_flat, slots, after(named, sent), counts, lengths)
     block = min(256, slot_rows)
     answers = pl.pallas_call(
         functools.partial(history_kernel, block),
@@ -309,24 +320,16 @@
         cost_estimate=pl.CostEstimate(flops=1 << 30, bytes_accessed=64 << 20, transcendentals=slot_rows * history),
         name="history",
     )(
-        info,
+        after(info, mine),
         got.reshape(slot_rows, head_dim),
         cache_keys.reshape(history, head_dim),
         cache_values.reshape(history, head_dim),
     )
-    nexts = jnp.concatenate([after(piece, answers) for piece in nexts], axis=0)
-    last = passed(nexts[-head_dim:], 1)
+    next_one, next_two = after((next_one, next_two), answers)
+    nexts = jnp.concatenate([next_one, next_two], axis=0)
+    lasts = passed(nexts, 2)
     others = swapped(nexts)
-    mine = pl.pallas_call(
-        functools.partial(local_kernel, capacity, cands),
-        in_specs=[VMEM] * 6,
-        out_specs=HBM,
-        out_shape=jax.ShapeDtypeStruct((rows, 3 * head_dim), f32),
-        scratch_shapes=[pltpu.VMEM((rows, 3 * head_dim), f32), pltpu.SemaphoreType.DMA],
-        compiler_params=params,
-        cost_estimate=pl.CostEstimate(flops=1 << 30, bytes_accessed=16 << 20, transcendentals=1 << 18),
-        name="local",
-    )(tokens, w_flat, slots, after(named, answers), counts, lengths)
+    other_three = passed(next_two, 1, flip=1)
     returned = lax.all_to_all(
         answers.reshape(replicas, capacity * cands, head_dim), "replica", split_axis=0, concat_axis=0, tiled=True
     )
@@ -351,7 +354,7 @@
     )
     return pl.pallas_call(
         output_kernel,
-        in_specs=[SMEM, SMEM, HBM] + [ANY] * 5,
+        in_specs=[SMEM, SMEM, HBM] + [ANY] * 6,
         out_specs=HBM,
         out_shape=jax.ShapeDtypeStruct((share, model_width), bf16),
         scratch_shapes=[
@@ -359,11 +362,11 @@
             pltpu.VMEM((groups * head_dim, model_width), bf16),
             pltpu.VMEM((share, model_width), bf16),
             pltpu.VMEM((share, model_width), bf16),
-            pltpu.SemaphoreType.DMA((6,)),
+            pltpu.SemaphoreType.DMA((7,)),
         ],
         compiler_params=tight,
         name="output",
-    )(group_index, my_index, tokens, heads, w_own, nexts, last, others)
+    )(group_index, my_index, tokens, heads, w_own, nexts, lasts, others, other_three)
 
 
 def solution(mesh):

time: 78.6 us -> 78.4 us (level)
  waiting for transfers between devices: 9.42 us -> 11.3 us
  local copies, waits for them, and re-layouts: 3.14 us -> 1.68 us
    ppermute x4, starting transfers between devices: 21.1 us -> 16.6 us  [passed(): return lax.ppermute(piece, ('replica', 'tensor'), pairs)]
    all_to_all x1, waiting for transfers between devices: 9.4 us -> 4.98 us  [on_device(): lax.all_to_all(gated.reshape(groups, share, head_dim), 'tensor', split_ax...]
    ppermute x4, waiting for transfers between devices: 0.01 us -> 4.03 us  [passed(): return lax.ppermute(piece, ('replica', 'tensor'), pairs)]
    all_to_all x1, waiting for transfers between devices: 0.01 us -> 2.24 us  [on_device(): lax.all_to_all(answers.reshape(replicas, capacity * cands, head_dim), 're...]
    all_to_all x1, starting transfers between devices: 10.3 us -> 12.6 us  [on_device(): lax.all_to_all(answers.reshape(replicas, capacity * cands, head_dim), 're...]
    concatenate x1, local copies, waits for them, and re-layouts: 1.66 us -> 0.02 us  [on_device(): nexts = jnp.concatenate([next_one, next_two], axis=0)]
    all_to_all x1, starting transfers between devices: 3.77 us -> 5.38 us  [on_device(): lax.all_to_all(gated.reshape(groups, share, head_dim), 'tensor', split_ax...]
    unnamed x6 -> x11, local copies, waits for them, and re-layouts: 1.48 us -> 1.66 us
  transfers between devices with their start and end apart: 8 -> 8, of which waited for: 1 -> 3; matrix products, arithmetic and copies ran while one was open for 4% -> 1% of each run, Pallas kernels for 13% -> 13%
where the time goes in v5:
time: 78.4 us; the launch traced here: 77.7 us
  starting transfers between devices  47.5 us (61%)
  Pallas kernels  17 us (22%)
  waiting for transfers between devices  11.3 us (14%)
  local copies, waits for them, and re-layouts  1.68 us (2%)
    ppermute x4, starting transfers between devices, passed(): return lax.ppermute(piece, ('replica', 'tensor'), pairs)  16.6 us
    all_to_all x1, starting transfers between devices, on_device(): lax.all_to_all(answers.reshape(replicas, capacity * cands, head_dim), 're...  12.6 us
    all_to_all x1, starting transfers between devices, on_device(): lax.all_to_all(sent.reshape(replicas, capacity * cands, head_dim), 'repli...  10.9 us
    all_to_all x1, starting transfers between devices, on_device(): lax.all_to_all(gated.reshape(groups, share, head_dim), 'tensor', split_ax...  5.38 us
    all_to_all x1, waiting for transfers between devices, on_device(): lax.all_to_all(gated.reshape(groups, share, head_dim), 'tensor', split_ax...  4.98 us
    pallas_call x1, Pallas kernels, on_device(): pl.pallas_call(functools.partial(send_kernel, capacity, cands, chunks), i...  4.46 us
    ppermute x4, waiting for transfers between devices, passed(): return lax.ppermute(piece, ('replica', 'tensor'), pairs)  4.03 us
    pallas_call x1, Pallas kernels, on_device(): pl.pallas_call(functools.partial(local_kernel, capacity, cands), in_specs...  3.87 us
  transfers between devices with their start and end apart: 8, of which 3 were waited for; matrix products, arithmetic and copies ran while one was open for 1% of the time, Pallas kernels for 13%

profile of v5, /device:TPU:6, one launch (start us, length us, event | category | flops | bytes accessed | tf_op | source)
XLA Modules:
  0.0 77.7 jit_solution(8221337013017776329)
XLA Ops:
  0.0 4.5 %send.1 = (bf16[1024,128]{1,0:T(8,128)(2,1)}, f32[8,128]{1,0:T(8,128)}) custom-call(bf16[512,1024]{1,0:T(8,128)(2,1)} %tokens_ref.5, bf16[1024,512]{1,0:T(8,128)(2,1)} %bitcast.20, s32[1,64]{1,0:T(1,128)} %bitcast.23, s32[1,64]{1,0:T(1,128)} %bitcast.25, s32[1,64]{1,0:T(1,128)} %bitcast.27, s32[1]{0:T(128)} %bitcast.1.me_ref), custom_call_target="tpu_custom_call" | custom-call | tf_op jit(solution)/shard_map/send/pallas_call | solution.py:261
  4.5 0.0 copy-start
  4.5 10.9 %all-to-all-start = ((bf16[64,16,128]{2,1,0:T(8,128)(2,1)}), bf16[64,16,128]{2,1,0:T(8,128)(2,1)S(1)}, u32[]{:S(2)}, u32[]{:S(2)}) async-start(bf16[64,16,128]{2,1,0:T(8,128)(2,1)} %bitcast.22), calls=%async_computation | async-start | bytes 524288 | tf_op jit(solution)/shard_map/all_to_all | solution.py:279
  15.4 0.0 copy-done
  15.4 6.1 %collective-permute-start.1 = (bf16[128,1024]{1,0:T(8,128)(2,1)S(1)}, bf16[128,1024]{1,0:T(8,128)(2,1)S(1)}, u32[]{:S(2)}, u32[]{:S(2)}) collective-permute-start(bf16[128,1024]{1,0:T(8,128)(2,1)S(1)} %bitcast.15), channel_id=1, source_target_pairs={{0,2},{1,3},{2,4},{3,5},{4,6},{5,7},{6,0},{7,1},{8,14},{9,15},{10,... | collective-permute-start | bytes 786440 | tf_op jit(solution)/shard_map/ppermute | solution.py:287
  21.5 4.3 %collective-permute-start = (bf16[128,1024]{1,0:T(8,128)(2,1)S(1)}, bf16[128,1024]{1,0:T(8,128)(2,1)}, u32[]{:S(2)}, u32[]{:S(2)}) collective-permute-start(bf16[128,1024]{1,0:T(8,128)(2,1)S(1)} %bitcast.16), channel_id=1, source_target_pairs={{0,1},{1,2},{2,3},{3,4},{4,5},{5,6},{6,7},{7,0},{8,15},{9,8},{10,9... | collective-permute-start | bytes 786440 | tf_op jit(solution)/shard_map/ppermute | solution.py:287
  25.8 3.9 %local.1.mine_ref = f32[512,384]{1,0:T(8,128)} custom-call(bf16[512,1024]{1,0:T(8,128)(2,1)} %tokens_ref.5, bf16[1024,512]{1,0:T(8,128)(2,1)} %bitcast.21, s32[1,64]{1,0:T(1,128)} %bitcast.24, s32[1,64]{1,0:T(1,128)} %bitcast.26, s32[1,64]{1,0:T(1,128)} %bitcast.31, s32[1,64]{1,0:T(1,128)} %bitcast.28), custom_call_target="tpu_custom_call" | custom-call | flops 1073741824 | bytes 16777216 | tf_op jit(solution)/shard_map/local/pallas_call | solution.py:295
  29.7 0.0 copy-start.1
  29.7 0.0 all-to-all-done
  29.7 0.7 copy-done.1
  30.4 3.4 %history.1 = bf16[1024,128]{1,0:T(8,128)(2,1)} custom-call(f32[8,128]{1,0:T(8,128)S(1)} %copy-done.1, bf16[1024,128]{1,0:T(8,128)(2,1)S(1)} %bitcast.19, bf16[1024,128]{1,0:T(8,128)(2,1)} %bitcast.29, bf16[1024,128]{1,0:T(8,128)(2,1)} %bitcast.30), custom_call_target="tpu_custom_call" | custom-call | flops 1073741824 | bytes 67108864 | tf_op jit(solution)/shard_map/history/pallas_call | solution.py:306
  33.8 12.6 %all-to-all-start.1 = ((bf16[64,16,128]{2,1,0:T(8,128)(2,1)}), bf16[64,16,128]{2,1,0:T(8,128)(2,1)S(1)}, u32[]{:S(2)}, u32[]{:S(2)}) async-start(bf16[64,16,128]{2,1,0:T(8,128)(2,1)} %bitcast.11), calls=%async_computation.1 | async-start | bytes 524288 | tf_op jit(solution)/shard_map/all_to_all | solution.py:333
  46.4 0.0 collective-permute-done.1
  46.4 0.0 collective-permute-done
  46.4 1.0 %constant_dynamic-update-slice_fusion.1 = bf16[256,1024]{1,0:T(8,128)(2,1)S(1)} fusion(bf16[128,1024]{1,0:T(8,128)(2,1)} %collective-permute-done), kind=kLoop, calls=%fused_computation.1 | loop fusion | bytes 524288
  47.4 0.0 copy-start.2
  47.4 2.1 %collective-permute-start.3 = (bf16[256,1024]{1,0:T(8,128)(2,1)S(1)}, bf16[256,1024]{1,0:T(8,128)(2,1)S(1)}, u32[]{:S(2)}, u32[]{:S(2)}) collective-permute-start(bf16[256,1024]{1,0:T(8,128)(2,1)S(1)} %constant_dynamic-update-slice_fusion.next_ref), channel_id=1, source_target_pairs={{0,8},{8,0},{16,24},{24,16},{32,40},{40,32},{48,56},{56,48},{64,72... | collective-permute-start | bytes 1572872 | tf_op jit(solution)/shard_map/ppermute | solution.py:290
  49.4 4.3 %collective-permute-start.2 = (bf16[256,1024]{1,0:T(8,128)(2,1)S(1)}, bf16[256,1024]{1,0:T(8,128)(2,1)S(1)}, u32[]{:S(2)}, u32[]{:S(2)}) collective-permute-start(bf16[256,1024]{1,0:T(8,128)(2,1)S(1)} %constant_dynamic-update-slice_fusion.next_ref), channel_id=1, source_target_pairs={{0,2},{1,3},{2,4},{3,5},{4,6},{5,7},{6,0},{7,1},{8,14},{9,15},{10,... | collective-permute-start | bytes 1572872 | tf_op jit(solution)/shard_map/ppermute | solution.py:287
  53.7 1.9 %collective-permute-start.4 = (bf16[128,1024]{1,0:T(8,128)(2,1)S(1)}, bf16[128,1024]{1,0:T(8,128)(2,1)S(1)}, u32[]{:S(2)}, u32[]{:S(2)}) collective-permute-start(bf16[128,1024]{1,0:T(8,128)(2,1)S(1)} %collective-permute-done.1), channel_id=1, source_target_pairs={{0,9},{1,10},{2,11},{3,12},{4,13},{5,14},{6,15},{7,8},{8,7},{9,0},... | collective-permute-start | bytes 786440 | tf_op jit(solution)/shard_map/ppermute | solution.py:287
  55.7 2.2 %all-to-all-done.1 = bf16[64,16,128]{2,1,0:T(8,128)(2,1)S(1)} async-done(((bf16[64,16,128]{2,1,0:T(8,128)(2,1)}), bf16[64,16,128]{2,1,0:T(8,128)(2,1)S(1)}, u32[]{:S(2)}, u32[]{:S(2)}) %all-to-all-start.1) | async-done | bytes 262176 | tf_op jit(solution)/shard_map/all_to_all | solution.py:333
  57.9 2.7 %gate.1 = bf16[512,128]{1,0:T(8,128)(2,1)} custom-call(bf16[1024,128]{1,0:T(8,128)(2,1)S(1)} %bitcast.18, f32[512,384]{1,0:T(8,128)} %local.1.mine_ref), custom_call_target="tpu_custom_call" | custom-call | flops 1073741824 | bytes 67108864 | tf_op jit(solution)/shard_map/gate/pallas_call | solution.py:336
  60.6 0.0 copy-done.2
  60.6 5.4 %all-to-all-start.2 = ((bf16[8,64,128]{2,1,0:T(8,128)(2,1)}), bf16[8,64,128]{2,1,0:T(8,128)(2,1)S(1)}, u32[]{:S(2)}, u32[]{:S(2)}) async-start(bf16[8,64,128]{2,1,0:T(8,128)(2,1)} %bitcast.13), calls=%async_computation.2 | async-start | bytes 262144 | tf_op jit(solution)/shard_map/all_to_all | solution.py:352
  66.0 4.0 %collective-permute-done.4.three_ref = bf16[128,1024]{1,0:T(8,128)(2,1)S(1)} collective-permute-done((bf16[128,1024]{1,0:T(8,128)(2,1)S(1)}, bf16[128,1024]{1,0:T(8,128)(2,1)S(1)}, u32[]{:S(2)}, u32[]{:S(2)}) %collective-permute-start.4) | collective-permute-done | bytes 262176 | tf_op jit(solution)/shard_map/ppermute | solution.py:287
  70.0 0.0 collective-permute-done.3.other_ref
  70.0 0.0 copy-start.3
  70.0 0.0 collective-permute-done.2.last_ref
  70.0 0.0 copy-start.4
  70.0 5.0 %all-to-all-done.2.gated_ref = bf16[8,64,128]{2,1,0:T(8,128)(2,1)S(1)} async-done(((bf16[8,64,128]{2,1,0:T(8,128)(2,1)}), bf16[8,64,128]{2,1,0:T(8,128)(2,1)S(1)}, u32[]{:S(2)}, u32[]{:S(2)}) %all-to-all-start.2) | async-done | bytes 131104 | tf_op jit(solution)/shard_map/all_to_all | solution.py:352
  75.0 0.0 copy-done.3
  75.0 0.0 copy-done.4
  75.0 2.6 %output.1 = bf16[64,1024]{1,0:T(8,128)(2,1)} custom-call(s32[1]{0:T(128)} %bitcast.group_ref, s32[1]{0:T(128)} %bitcast.1.me_ref, bf16[512,1024]{1,0:T(8,128)(2,1)} %tokens_ref.5, bf16[8,64,128]{2,1,0:T(8,128)(2,1)S(1)} %all-to-all-done.2.gated_ref, bf16[128,1024]{1,0:T(8,128)(2,1)S(1)} %bitcast.17, bf16[256,1024]{1,0:T(8,128)(2,1)} %copy-done.2, ...), custom_call_target="tpu_custom_call" | custom-call | tf_op jit(solution)/shard_map/output/pallas_call | solution.py:355
  (1 shorter events, 0.0 us)
Async XLA Ops:
  4.5 11.0 %copy-start = (bf16[1,128,1024]{2,1,0:T(8,128)(2,1)S(1)}, bf16[1,128,1024]{2,1,0:T(8,128)(2,1)}, u32[]{:S(2)}) copy-start(bf16[1,128,1024]{2,1,0:T(8,128)(2,1)} %param.11) | copy-start | bytes 786436
  4.5 25.2 %all-to-all-start = ((bf16[64,16,128]{2,1,0:T(8,128)(2,1)}), bf16[64,16,128]{2,1,0:T(8,128)(2,1)S(1)}, u32[]{:S(2)}, u32[]{:S(2)}) async-start(bf16[64,16,128]{2,1,0:T(8,128)(2,1)} %bitcast.22), calls=%async_computation | async-start | bytes 524288 | tf_op jit(solution)/shard_map/all_to_all | solution.py:279
  15.4 30.9 %collective-permute-start.1 = (bf16[128,1024]{1,0:T(8,128)(2,1)S(1)}, bf16[128,1024]{1,0:T(8,128)(2,1)S(1)}, u32[]{:S(2)}, u32[]{:S(2)}) collective-permute-start(bf16[128,1024]{1,0:T(8,128)(2,1)S(1)} %bitcast.15), channel_id=1, source_target_pairs={{0,2},{1,3},{2,4},{3,5},{4,6},{5,7},{6,0},{7,1},{8,14},{9,15},{10,... | collective-permute-start | bytes 786440 | tf_op jit(solution)/shard_map/ppermute | solution.py:287
  21.5 24.8 %collective-permute-start = (bf16[128,1024]{1,0:T(8,128)(2,1)S(1)}, bf16[128,1024]{1,0:T(8,128)(2,1)}, u32[]{:S(2)}, u32[]{:S(2)}) collective-permute-start(bf16[128,1024]{1,0:T(8,128)(2,1)S(1)} %bitcast.16), channel_id=1, source_target_pairs={{0,1},{1,2},{2,3},{3,4},{4,5},{5,6},{6,7},{7,0},{8,15},{9,8},{10,9... | collective-permute-start | bytes 786440 | tf_op jit(solution)/shard_map/ppermute | solution.py:287
  29.7 0.7 copy-start.1
  33.8 24.1 %all-to-all-start.1 = ((bf16[64,16,128]{2,1,0:T(8,128)(2,1)}), bf16[64,16,128]{2,1,0:T(8,128)(2,1)S(1)}, u32[]{:S(2)}, u32[]{:S(2)}) async-start(bf16[64,16,128]{2,1,0:T(8,128)(2,1)} %bitcast.11), calls=%async_computation.1 | async-start | bytes 524288 | tf_op jit(solution)/shard_map/all_to_all | solution.py:333
  47.4 13.3 %copy-start.2 = (bf16[256,1024]{1,0:T(8,128)(2,1)}, bf16[256,1024]{1,0:T(8,128)(2,1)S(1)}, u32[]{:S(2)}) copy-start(bf16[256,1024]{1,0:T(8,128)(2,1)S(1)} %constant_dynamic-update-slice_fusion.next_ref) | copy-start | bytes 1572868
  47.4 22.7 %collective-permute-start.3 = (bf16[256,1024]{1,0:T(8,128)(2,1)S(1)}, bf16[256,1024]{1,0:T(8,128)(2,1)S(1)}, u32[]{:S(2)}, u32[]{:S(2)}) collective-permute-start(bf16[256,1024]{1,0:T(8,128)(2,1)S(1)} %constant_dynamic-update-slice_fusion.next_ref), channel_id=1, source_target_pairs={{0,8},{8,0},{16,24},{24,16},{32,40},{40,32},{48,56},{56,48},{64,72... | collective-permute-start | bytes 1572872 | tf_op jit(solution)/shard_map/ppermute | solution.py:290
  49.4 20.6 %collective-permute-start.2 = (bf16[256,1024]{1,0:T(8,128)(2,1)S(1)}, bf16[256,1024]{1,0:T(8,128)(2,1)S(1)}, u32[]{:S(2)}, u32[]{:S(2)}) collective-permute-start(bf16[256,1024]{1,0:T(8,128)(2,1)S(1)} %constant_dynamic-update-slice_fusion.next_ref), channel_id=1, source_target_pairs={{0,2},{1,3},{2,4},{3,5},{4,6},{5,7},{6,0},{7,1},{8,14},{9,15},{10,... | collective-permute-start | bytes 1572872 | tf_op jit(solution)/shard_map/ppermute | solution.py:287
  53.7 16.3 %collective-permute-start.4 = (bf16[128,1024]{1,0:T(8,128)(2,1)S(1)}, bf16[128,1024]{1,0:T(8,128)(2,1)S(1)}, u32[]{:S(2)}, u32[]{:S(2)}) collective-permute-start(bf16[128,1024]{1,0:T(8,128)(2,1)S(1)} %collective-permute-done.1), channel_id=1, source_target_pairs={{0,9},{1,10},{2,11},{3,12},{4,13},{5,14},{6,15},{7,8},{8,7},{9,0},... | collective-permute-start | bytes 786440 | tf_op jit(solution)/shard_map/ppermute | solution.py:287
  60.6 14.4 %all-to-all-start.2 = ((bf16[8,64,128]{2,1,0:T(8,128)(2,1)}), bf16[8,64,128]{2,1,0:T(8,128)(2,1)S(1)}, u32[]{:S(2)}, u32[]{:S(2)}) async-start(bf16[8,64,128]{2,1,0:T(8,128)(2,1)} %bitcast.13), calls=%async_computation.2 | async-start | bytes 262144 | tf_op jit(solution)/shard_map/all_to_all | solution.py:352
  70.0 5.0 %copy-start.3 = (bf16[256,1024]{1,0:T(8,128)(2,1)}, bf16[256,1024]{1,0:T(8,128)(2,1)S(1)}, u32[]{:S(2)}) copy-start(bf16[256,1024]{1,0:T(8,128)(2,1)S(1)} %collective-permute-done.3.other_ref) | copy-start | bytes 1572868
  70.0 5.0 %copy-start.4 = (bf16[256,1024]{1,0:T(8,128)(2,1)}, bf16[256,1024]{1,0:T(8,128)(2,1)S(1)}, u32[]{:S(2)}) copy-start(bf16[256,1024]{1,0:T(8,128)(2,1)S(1)} %collective-permute-done.2.last_ref) | copy-start | bytes 1572868

commit v6 on v5

--- a/solution.py
+++ b/solution.py
@@ -66,9 +66,12 @@
     fetch_w.start()
     for fetch in fetches[1:]:
         fetch.start()
-    own = slot_ref[...] == me_ref[0]
-    length = jnp.sum(jnp.where(own, length_ref[...].astype(f32), 0.0), 1, keepdims=True)
-    info[...] = jnp.broadcast_to(length, info.shape)
+    for row, who in enumerate((me_ref[0], me_ref[0] ^ 1)):
+        named = slot_ref[...] == who
+        length = jnp.sum(jnp.where(named, length_ref[...].astype(f32), 0.0), 1, keepdims=True)
+        info[row : row + 1, :] = jnp.broadcast_to(length, (1, info.shape[1]))
+    core = (me_ref[0] & 1).astype(f32)
+    info[2:, :] = jnp.broadcast_to(core, (info.shape[0] - 2, info.shape[1]))
     stores = [pltpu.make_async_copy(info, info_ref, out_sems.at[chunks])]
     stores[0].start()
     first = first_rows(slot_ref, session_ref, capacity, cands)
@@ -125,35 +128,37 @@
 
 
 def history_kernel(
-    block, info_ref, query_ref, keys_ref, values_ref, out_ref, info, query, keys, values, result, sems
+    blocks, info_ref, query_ref, keys_ref, values_ref, other_keys_ref, other_values_ref, out_ref, result, sems
 ):
-    fetches = [
-        pltpu.make_async_copy(source, target, sems.at[n])
-        for n, (source, target) in enumerate(
-            ((info_ref, info), (query_ref, query), (keys_ref, keys), (values_ref, values))
-        )
-    ]
-    for fetch in fetches:
-        fetch.start()
     history, head_dim = keys_ref.shape
+    chips, _, held, _ = query_ref.shape
+    share = chips // blocks
     half_scale = 0.5 * head_dim ** (-0.5)
-    for fetch in fetches:
-        fetch.wait()
-    length = info[:1, :1]
-    divisor = length + 1.0
-    seen = iota((history, 1), 0).astype(f32) < length
-    seen_values = jnp.where(seen, values[...], jnp.zeros((), bf16))
+    second = info_ref[2:3, :] > 0.5
+    sides = []
+    for row, keys, values in ((0, keys_ref, values_ref), (1, other_keys_ref, other_values_ref)):
+        length = info_ref[row : row + 1, :1]
+        seen = iota((history, 1), 0).astype(f32) < length
+        sides.append((keys[...], jnp.where(seen, values[...], jnp.zeros((), bf16)), length + 1.0))
     stores = []
-    for n, start in enumerate(range(0, query_ref.shape[0], block)):
-        part = pl.ds(start, block)
-        half = (
-            lax.dot_general(query[part, :], keys[...], (((1,), (1,)), ((), ())), preferred_element_type=f32)
-            * half_scale
-        )
-        weights = (half + half * jnp.tanh(half)).astype(bf16)
-        summed = jnp.dot(weights, seen_values, preferred_element_type=f32)
-        result[part, :] = (summed / divisor).astype(bf16)
-        stores.append(pltpu.make_async_copy(result.at[part, :], out_ref.at[part, :], sems.at[4 + n]))
+    for n in range(blocks):
+        part = pl.ds(n * share, share)
+        first_rows_of = query_ref[part, 0].reshape(share * held, head_dim)
+        second_rows_of = query_ref[part, 1].reshape(share * held, head_dim)
+        mine = jnp.where(second, second_rows_of, first_rows_of)
+        others = jnp.where(second, first_rows_of, second_rows_of)
+        answers = []
+        for query, (keys, values, divisor) in zip((mine, others), sides):
+            half = (
+                lax.dot_general(query, keys, (((1,), (1,)), ((), ())), preferred_element_type=f32) * half_scale
+            )
+            weights = (half + half * jnp.tanh(half)).astype(bf16)
+            summed = jnp.dot(weights, values, preferred_element_type=f32)
+            answers.append((summed / divisor).astype(bf16))
+        mine, others = answers
+        result[part, 0] = jnp.where(second, others, mine).reshape(share, held, head_dim)
+        result[part, 1] = jnp.where(second, mine, others).reshape(share, held, head_dim)
+        stores.append(pltpu.make_async_copy(result.at[part], out_ref.at[part], sems.at[n]))
         stores[-1].start()
     for store in stores:
         store.wait()
@@ -276,9 +281,22 @@
         compiler_params=params,
         name="send",
     )(tokens, w_flat, slots, named, lengths, my_index)
-    got = lax.all_to_all(
-        sent.reshape(replicas, capacity * cands, head_dim), "replica", split_axis=0, concat_axis=0, tiled=True
-    )
+    chips = replicas // 2
+    held = capacity * cands
+    same_core = [[2 * chip + core for chip in range(chips)] for core in range(2)]
+
+    def exchanged(rows_of):
+        return lax.all_to_all(
+            rows_of.reshape(chips, 2 * held, head_dim),
+            "replica",
+            split_axis=0,
+            concat_axis=0,
+            tiled=True,
+            axis_index_groups=same_core,
+        )
+
+    got = exchanged(sent)
+
     def passed(piece, by, flip=0):
         pairs = []
         for r in range(replicas):
@@ -298,41 +316,40 @@
         out_specs=HBM,
         out_shape=jax.ShapeDtypeStruct((rows, 3 * head_dim), f32),
         scratch_shapes=[pltpu.VMEM((rows, 3 * head_dim), f32), pltpu.SemaphoreType.DMA],
-        compiler_params=params,
+        compiler_params=roomy,
         cost_estimate=pl.CostEstimate(flops=1 << 30, bytes_accessed=16 << 20, transcendentals=1 << 18),
         name="local",
     )(tokens, w_flat, slots, after(named, sent), counts, lengths)
-    block = min(256, slot_rows)
+    keys = cache_keys.reshape(history, head_dim)
+    values = cache_values.reshape(history, head_dim)
+    other_keys, other_values = swapped(after(keys, sent)), swapped(after(values, sent))
+    blocks = 2
     answers = pl.pallas_call(
-        functools.partial(history_kernel, block),
-        in_specs=[HBM, ANY, HBM, HBM],
+        functools.partial(history_kernel, blocks),
+        in_specs=[VMEM] * 6,
         out_specs=HBM,
-        out_shape=jax.ShapeDtypeStruct((slot_rows, head_dim), bf16),
+        out_shape=jax.ShapeDtypeStruct((chips, 2, held, head_dim), bf16),
         scratch_shapes=[
-            pltpu.VMEM((8, 128), f32),
-            pltpu.VMEM((slot_rows, head_dim), bf16),
-            pltpu.VMEM((history, head_dim), bf16),
-            pltpu.VMEM((history, head_dim), bf16),
-            pltpu.VMEM((slot_rows, head_dim), bf16),
-            pltpu.SemaphoreType.DMA((4 + slot_rows // block,)),
+            pltpu.VMEM((chips, 2, held, head_dim), bf16),
+            pltpu.SemaphoreType.DMA((blocks,)),
         ],
-        compiler_params=tight,
+        compiler_params=roomy,
         cost_estimate=pl.CostEstimate(flops=1 << 30, bytes_accessed=64 << 20, transcendentals=slot_rows * history),
         name="history",
     )(
         after(info, mine),
-        got.reshape(slot_rows, head_dim),
-        cache_keys.reshape(history, head_dim),
-        cache_values.reshape(history, head_dim),
+        got.reshape(chips, 2, held, head_dim),
+        keys,
+        values,
+        other_keys,
+        other_values,
     )
     next_one, next_two = after((next_one, next_two), answers)
     nexts = jnp.concatenate([next_one, next_two], axis=0)
     lasts = passed(nexts, 2)
     others = swapped(nexts)
     other_three = passed(next_two, 1, flip=1)
-    returned = lax.all_to_all(
-        answers.reshape(replicas, capacity * cands, head_dim), "replica", split_axis=0, concat_axis=0, tiled=True
-    )
+    returned = exchanged(answers)
     gated = pl.pallas_call(
         gate_kernel,
         in_specs=[ANY, HBM],

time: 78.4 us -> 79.9 us (1.019)
  the two profiles are of different devices: /device:TPU:6 before, /device:TPU:8 now
where the time goes in v6:
time: 79.9 us; the launch traced here: 79.2 us
  starting transfers between devices  52.9 us (66%)
  Pallas kernels  13.8 us (17%)
  waiting for transfers between devices  9.65 us (12%)
  local copies, waits for them, and re-layouts  2.54 us (3%)
    ppermute x4, starting transfers between devices, passed(): return lax.ppermute(piece, ('replica', 'tensor'), pairs)  20.4 us
    all_to_all x2, starting transfers between devices, exchanged(): lax.all_to_all(rows_of.reshape(chips, 2 * held, head_dim), 'replica', spl...  20.1 us
    all_to_all x1, waiting for transfers between devices, on_device(): lax.all_to_all(gated.reshape(groups, share, head_dim), 'tensor', split_ax...  8.08 us
    ppermute x3, starting transfers between devices, swapped(): return lax.ppermute(piece, 'replica', [(r, r ^ 1) for r in range(replicas)])  6.25 us
    all_to_all x1, starting transfers between devices, on_device(): lax.all_to_all(gated.reshape(groups, share, head_dim), 'tensor', split_ax...  6.17 us
    pallas_call x1, Pallas kernels, on_device(): pl.pallas_call(functools.partial(send_kernel, capacity, cands, chunks), i...  4.63 us
    pallas_call x1, Pallas kernels, on_device(): pl.pallas_call(gate_kernel, in_specs=[ANY, HBM], out_specs=HBM, out_shape...  2.7 us
    pallas_call x1, Pallas kernels, on_device(): pl.pallas_call(output_kernel, in_specs=[SMEM, SMEM, HBM] + [ANY] * 6, out...  2.63 us
  transfers between devices with their start and end apart: 10, of which 3 were waited for; matrix products, arithmetic and copies ran while one was open for 0% of the time, Pallas kernels for 8%

profile of v6, /device:TPU:8, one launch (start us, length us, event | category | flops | bytes accessed | tf_op | source)
XLA Modules:
  0.0 79.2 jit_solution(9248135255762388519)
XLA Ops:
  0.0 4.6 %send.1 = (bf16[1024,128]{1,0:T(8,128)(2,1)}, f32[8,128]{1,0:T(8,128)}) custom-call(bf16[512,1024]{1,0:T(8,128)(2,1)} %tokens_ref.5, bf16[1024,512]{1,0:T(8,128)(2,1)} %bitcast.15, s32[1,64]{1,0:T(1,128)} %bitcast.22, s32[1,64]{1,0:T(1,128)} %bitcast.24, s32[1,64]{1,0:T(1,128)} %bitcast.26, s32[1]{0:T(128)} %bitcast.1.me_ref), custom_call_target="tpu_custom_call" | custom-call | tf_op jit(solution)/shard_map/send/pallas_call | solution.py:266
  4.6 0.0 copy-start.6
  4.6 0.0 copy-start.2
  4.7 10.3 %all-to-all-start = ((bf16[32,32,128]{2,1,0:T(8,128)(2,1)}), bf16[32,32,128]{2,1,0:T(8,128)(2,1)S(1)}, u32[]{:S(2)}, u32[]{:S(2)}) async-start(bf16[32,32,128]{2,1,0:T(8,128)(2,1)} %bitcast.33), calls=%async_computation | async-start | bytes 524288 | tf_op jit(solution)/shard_map/all_to_all | solution.py:289
  15.0 0.0 copy-done.6
  15.0 1.9 %collective-permute-start = (bf16[1024,128]{1,0:T(8,128)(2,1)S(1)}, bf16[1024,128]{1,0:T(8,128)(2,1)S(1)}, u32[]{:S(2)}, u32[]{:S(2)}) collective-permute-start(bf16[1024,128]{1,0:T(8,128)(2,1)S(1)} %bitcast.28), channel_id=1, source_target_pairs={{0,8},{8,0},{16,24},{24,16},{32,40},{40,32},{48,56},{56,48},{64,72... | collective-permute-start | bytes 786440 | tf_op jit(solution)/shard_map/ppermute | solution.py:308
  16.9 0.0 copy-done.7
  16.9 2.4 %collective-permute-start.1 = (bf16[1024,128]{1,0:T(8,128)(2,1)S(1)}, bf16[1024,128]{1,0:T(8,128)(2,1)S(1)}, u32[]{:S(2)}, u32[]{:S(2)}) collective-permute-start(bf16[1024,128]{1,0:T(8,128)(2,1)S(1)} %bitcast.30), channel_id=1, source_target_pairs={{0,8},{8,0},{16,24},{24,16},{32,40},{40,32},{48,56},{56,48},{64,72... | collective-permute-start | bytes 786440 | tf_op jit(solution)/shard_map/ppermute | solution.py:308
  19.3 0.0 copy-start.9
  19.4 0.0 copy-done.2
  19.4 0.0 copy-start.3
  19.4 0.0 copy-start.4
  19.4 0.0 copy-start.5
  19.4 4.4 %collective-permute-start.2 = (bf16[128,1024]{1,0:T(8,128)(2,1)S(1)}, bf16[128,1024]{1,0:T(8,128)(2,1)S(1)}, u32[]{:S(2)}, u32[]{:S(2)}) collective-permute-start(bf16[128,1024]{1,0:T(8,128)(2,1)S(1)} %bitcast.17), channel_id=1, source_target_pairs={{0,1},{1,2},{2,3},{3,4},{4,5},{5,6},{6,7},{7,0},{8,15},{9,8},{10,9... | collective-permute-start | bytes 786440 | tf_op jit(solution)/shard_map/ppermute | solution.py:305
  23.8 6.1 %collective-permute-start.3 = (bf16[128,1024]{1,0:T(8,128)(2,1)S(1)}, bf16[128,1024]{1,0:T(8,128)(2,1)S(1)}, u32[]{:S(2)}, u32[]{:S(2)}) collective-permute-start(bf16[128,1024]{1,0:T(8,128)(2,1)S(1)} %bitcast.18), channel_id=1, source_target_pairs={{0,2},{1,3},{2,4},{3,5},{4,6},{5,7},{6,0},{7,1},{8,14},{9,15},{10,... | collective-permute-start | bytes 786440 | tf_op jit(solution)/shard_map/ppermute | solution.py:305
  29.9 0.0 copy-done.9
  29.9 0.0 copy-done.3
  29.9 0.0 copy-done.4
  29.9 0.0 copy-done.5
  30.0 0.0 copy-start
  30.0 1.2 %copy-done = bf16[512,1024]{1,0:T(8,128)(2,1)S(1)} copy-done((bf16[512,1024]{1,0:T(8,128)(2,1)S(1)}, bf16[512,1024]{1,0:T(8,128)(2,1)}, u32[]{:S(2)}) %copy-start) | copy-done | bytes 1048600
  31.2 1.2 %copy-done.1 = bf16[1024,1,512]{2,0,1:T(8,128)(2,1)S(1)} copy-done((bf16[1024,1,512]{2,0,1:T(8,128)(2,1)S(1)}, bf16[1024,1,512]{2,0,1:T(8,128)(2,1)}, u32[]{:S(2)}) %copy-start.1) | copy-done | bytes 1048600
  32.4 1.5 %local.1.mine_ref = f32[512,384]{1,0:T(8,128)S(1)} custom-call(bf16[512,1024]{1,0:T(8,128)(2,1)S(1)} %copy-done, bf16[1024,512]{1,0:T(8,128)(2,1)S(1)} %bitcast.16, s32[1,64]{1,0:T(1,128)S(1)} %bitcast.23, s32[1,64]{1,0:T(1,128)S(1)} %bitcast.25, s32[1,64]{1,0:T(1,128)S(1)} %bitcast.32, s32[1,64]{1,0:T(1,128)S(1)} %bitcast.27), custom_call_target="tpu_custom_call" | custom-call | flops 1073741824 | bytes 16777216 | tf_op jit(solution)/shard_map/local/pallas_call | solution.py:313
  33.9 0.0 copy-start.10
  33.9 0.0 collective-permute-done.other_keys_ref
  33.9 0.0 collective-permute-done.1.other_values_ref
  33.9 0.0 all-to-all-done
  33.9 0.0 copy-done.8
  33.9 2.4 %history.1 = bf16[32,2,16,128]{3,2,1,0:T(8,128)(2,1)} custom-call(f32[8,128]{1,0:T(8,128)S(1)} %copy-done.8, bf16[32,2,16,128]{3,2,1,0:T(8,128)(2,1)S(1)} %bitcast.20, bf16[1024,128]{1,0:T(8,128)(2,1)S(1)} %bitcast.29, bf16[1024,128]{1,0:T(8,128)(2,1)S(1)} %bitcast.31, bf16[1024,128]{1,0:T(8,128)(2,1)S(1)} %collective-permute-done.other_keys_ref, ...), custom_call_target="tpu_custom_call" | custom-call | flops 1073741824 | bytes 67108864 | tf_op jit(solution)/shard_map/history/pallas_call | solution.py:327
  36.3 0.0 copy-done.10
  36.3 9.8 %all-to-all-start.1 = ((bf16[32,32,128]{2,1,0:T(8,128)(2,1)}), bf16[32,32,128]{2,1,0:T(8,128)(2,1)S(1)}, u32[]{:S(2)}, u32[]{:S(2)}) async-start(bf16[32,32,128]{2,1,0:T(8,128)(2,1)} %bitcast.11), calls=%async_computation.1 | async-start | bytes 524288 | tf_op jit(solution)/shard_map/all_to_all | solution.py:289
  46.1 0.0 collective-permute-done.2
  46.1 0.0 collective-permute-done.3
  46.2 0.0 copy-start.11
  46.2 6.4 %collective-permute-start.4 = (bf16[256,1024]{1,0:T(8,128)(2,1)S(1)}, bf16[256,1024]{1,0:T(8,128)(2,1)S(1)}, u32[]{:S(2)}, u32[]{:S(2)}) collective-permute-start(bf16[256,1024]{1,0:T(8,128)(2,1)S(1)} %constant_dynamic-update-slice_fusion.next_ref), channel_id=1, source_target_pairs={{0,2},{1,3},{2,4},{3,5},{4,6},{5,7},{6,0},{7,1},{8,14},{9,15},{10,... | collective-permute-start | bytes 1572872 | tf_op jit(solution)/shard_map/ppermute | solution.py:305
  52.6 1.9 %collective-permute-start.5 = (bf16[256,1024]{1,0:T(8,128)(2,1)S(1)}, bf16[256,1024]{1,0:T(8,128)(2,1)S(1)}, u32[]{:S(2)}, u32[]{:S(2)}) collective-permute-start(bf16[256,1024]{1,0:T(8,128)(2,1)S(1)} %constant_dynamic-update-slice_fusion.next_ref), channel_id=1, source_target_pairs={{0,8},{8,0},{16,24},{24,16},{32,40},{40,32},{48,56},{56,48},{64,72... | collective-permute-start | bytes 1572872 | tf_op jit(solution)/shard_map/ppermute | solution.py:308
  54.6 3.5 %collective-permute-start.6 = (bf16[128,1024]{1,0:T(8,128)(2,1)S(1)}, bf16[128,1024]{1,0:T(8,128)(2,1)S(1)}, u32[]{:S(2)}, u32[]{:S(2)}) collective-permute-start(bf16[128,1024]{1,0:T(8,128)(2,1)S(1)} %collective-permute-done.3), channel_id=1, source_target_pairs={{0,9},{1,10},{2,11},{3,12},{4,13},{5,14},{6,15},{7,8},{8,7},{9,0},... | collective-permute-start | bytes 786440 | tf_op jit(solution)/shard_map/ppermute | solution.py:305
  58.0 0.6 all-to-all-done.1
  58.6 2.7 %gate.1 = bf16[512,128]{1,0:T(8,128)(2,1)} custom-call(bf16[1024,128]{1,0:T(8,128)(2,1)S(1)} %bitcast.21, f32[512,384]{1,0:T(8,128)} %copy-done.10), custom_call_target="tpu_custom_call" | custom-call | flops 1073741824 | bytes 67108864 | tf_op jit(solution)/shard_map/gate/pallas_call | solution.py:353
  61.3 0.0 copy-done.11
  61.3 6.2 %all-to-all-start.2 = ((bf16[8,64,128]{2,1,0:T(8,128)(2,1)}), bf16[8,64,128]{2,1,0:T(8,128)(2,1)S(1)}, u32[]{:S(2)}, u32[]{:S(2)}) async-start(bf16[8,64,128]{2,1,0:T(8,128)(2,1)} %bitcast.13), calls=%async_computation.2 | async-start | bytes 262144 | tf_op jit(solution)/shard_map/all_to_all | solution.py:369
  67.5 1.0 %collective-permute-done.6.three_ref = bf16[128,1024]{1,0:T(8,128)(2,1)S(1)} collective-permute-done((bf16[128,1024]{1,0:T(8,128)(2,1)S(1)}, bf16[128,1024]{1,0:T(8,128)(2,1)S(1)}, u32[]{:S(2)}, u32[]{:S(2)}) %collective-permute-start.6) | collective-permute-done | bytes 262176 | tf_op jit(solution)/shard_map/ppermute | solution.py:305
  68.5 0.0 collective-permute-done.4.last_ref
  68.5 0.0 collective-permute-done.5.other_ref
  68.5 8.1 %all-to-all-done.2.gated_ref = bf16[8,64,128]{2,1,0:T(8,128)(2,1)S(1)} async-done(((bf16[8,64,128]{2,1,0:T(8,128)(2,1)}), bf16[8,64,128]{2,1,0:T(8,128)(2,1)S(1)}, u32[]{:S(2)}, u32[]{:S(2)}) %all-to-all-start.2) | async-done | bytes 131104 | tf_op jit(solution)/shard_map/all_to_all | solution.py:369
  76.6 0.0 copy-done.12
  76.6 0.0 copy-done.13
  76.6 2.6 %output.1 = bf16[64,1024]{1,0:T(8,128)(2,1)} custom-call(s32[1]{0:T(128)} %bitcast.group_ref, s32[1]{0:T(128)} %bitcast.1.me_ref, bf16[512,1024]{1,0:T(8,128)(2,1)} %tokens_ref.5, bf16[8,64,128]{2,1,0:T(8,128)(2,1)S(1)} %all-to-all-done.2.gated_ref, bf16[128,1024]{1,0:T(8,128)(2,1)S(1)} %bitcast.19, bf16[256,1024]{1,0:T(8,128)(2,1)} %copy-done.11, ...), custom_call_target="tpu_custom_call" | custom-call | tf_op jit(solution)/shard_map/output/pallas_call | solution.py:372
  (7 shorter events, 0.0 us)
Async XLA Ops:
  0.0 16.9 %copy-start.7 = (bf16[1,1024,1,128]{3,1,2,0:T(8,128)(2,1)S(1)}, bf16[1,1024,1,128]{3,1,2,0:T(8,128)(2,1)}, u32[]{:S(2)}) copy-start(bf16[1,1024,1,128]{3,1,2,0:T(8,128)(2,1)} %param.13) | copy-start | bytes 786436
  4.6 10.3 %copy-start.6 = (bf16[1,1024,1,128]{3,1,2,0:T(8,128)(2,1)S(1)}, bf16[1,1024,1,128]{3,1,2,0:T(8,128)(2,1)}, u32[]{:S(2)}) copy-start(bf16[1,1024,1,128]{3,1,2,0:T(8,128)(2,1)} %param.12) | copy-start | bytes 786436
  4.6 14.7 %copy-start.2 = (bf16[1,128,1024]{2,1,0:T(8,128)(2,1)S(1)}, bf16[1,128,1024]{2,1,0:T(8,128)(2,1)}, u32[]{:S(2)}) copy-start(bf16[1,128,1024]{2,1,0:T(8,128)(2,1)} %param.11) | copy-start | bytes 786436
  4.7 29.3 %all-to-all-start = ((bf16[32,32,128]{2,1,0:T(8,128)(2,1)}), bf16[32,32,128]{2,1,0:T(8,128)(2,1)S(1)}, u32[]{:S(2)}, u32[]{:S(2)}) async-start(bf16[32,32,128]{2,1,0:T(8,128)(2,1)} %bitcast.33), calls=%async_computation | async-start | bytes 524288 | tf_op jit(solution)/shard_map/all_to_all | solution.py:289
  15.0 18.9 %collective-permute-start = (bf16[1024,128]{1,0:T(8,128)(2,1)S(1)}, bf16[1024,128]{1,0:T(8,128)(2,1)S(1)}, u32[]{:S(2)}, u32[]{:S(2)}) collective-permute-start(bf16[1024,128]{1,0:T(8,128)(2,1)S(1)} %bitcast.28), channel_id=1, source_target_pairs={{0,8},{8,0},{16,24},{24,16},{32,40},{40,32},{48,56},{56,48},{64,72... | collective-permute-start | bytes 786440 | tf_op jit(solution)/shard_map/ppermute | solution.py:308
  16.9 17.0 %collective-permute-start.1 = (bf16[1024,128]{1,0:T(8,128)(2,1)S(1)}, bf16[1024,128]{1,0:T(8,128)(2,1)S(1)}, u32[]{:S(2)}, u32[]{:S(2)}) collective-permute-start(bf16[1024,128]{1,0:T(8,128)(2,1)S(1)} %bitcast.30), channel_id=1, source_target_pairs={{0,8},{8,0},{16,24},{24,16},{32,40},{40,32},{48,56},{56,48},{64,72... | collective-permute-start | bytes 786440 | tf_op jit(solution)/shard_map/ppermute | solution.py:308
  19.3 10.6 %copy-start.9 = (s32[64]{0:T(128)S(1)}, s32[64]{0:T(128)}, u32[]{:S(2)}) copy-start(s32[64]{0:T(128)} %param.16) | copy-start | bytes 772
  19.4 10.6 %copy-start.3 = (s32[64]{0:T(128)S(1)}, s32[64]{0:T(128)}, u32[]{:S(2)}) copy-start(s32[64]{0:T(128)} %param.14) | copy-start | bytes 772
  19.4 10.6 %copy-start.4 = (s32[64]{0:T(128)S(1)}, s32[64]{0:T(128)}, u32[]{:S(2)}) copy-start(s32[64]{0:T(128)} %param.15) | copy-start | bytes 772
  19.4 10.6 %copy-start.5 = (s32[64]{0:T(128)S(1)}, s32[64]{0:T(128)}, u32[]{:S(2)}) copy-start(s32[64]{0:T(128)} %param.17) | copy-start | bytes 772
  19.4 26.7 %collective-permute-start.2 = (bf16[128,1024]{1,0:T(8,128)(2,1)S(1)}, bf16[128,1024]{1,0:T(8,128)(2,1)S(1)}, u32[]{:S(2)}, u32[]{:S(2)}) collective-permute-start(bf16[128,1024]{1,0:T(8,128)(2,1)S(1)} %bitcast.17), channel_id=1, source_target_pairs={{0,1},{1,2},{2,3},{3,4},{4,5},{5,6},{6,7},{7,0},{8,15},{9,8},{10,9... | collective-permute-start | bytes 786440 | tf_op jit(solution)/shard_map/ppermute | solution.py:305
  23.8 22.3 %collective-permute-start.3 = (bf16[128,1024]{1,0:T(8,128)(2,1)S(1)}, bf16[128,1024]{1,0:T(8,128)(2,1)S(1)}, u32[]{:S(2)}, u32[]{:S(2)}) collective-permute-start(bf16[128,1024]{1,0:T(8,128)(2,1)S(1)} %bitcast.18), channel_id=1, source_target_pairs={{0,2},{1,3},{2,4},{3,5},{4,6},{5,7},{6,0},{7,1},{8,14},{9,15},{10,... | collective-permute-start | bytes 786440 | tf_op jit(solution)/shard_map/ppermute | solution.py:305
  30.0 1.2 %copy-start = (bf16[512,1024]{1,0:T(8,128)(2,1)S(1)}, bf16[512,1024]{1,0:T(8,128)(2,1)}, u32[]{:S(2)}) copy-start(bf16[512,1024]{1,0:T(8,128)(2,1)} %tokens_ref.5) | copy-start | bytes 3145732
  31.2 1.2 %copy-start.1 = (bf16[1024,1,512]{2,0,1:T(8,128)(2,1)S(1)}, bf16[1024,1,512]{2,0,1:T(8,128)(2,1)}, u32[]{:S(2)}) copy-start(bf16[1024,1,512]{2,0,1:T(8,128)(2,1)} %param.10) | copy-start | bytes 3145732
  32.4 1.5 %copy-start.8 = (f32[8,128]{1,0:T(8,128)S(1)}, f32[8,128]{1,0:T(8,128)}, u32[]{:S(2)}) copy-start(f32[8,128]{1,0:T(8,128)} %get-tuple-element.17.info_ref) | copy-start | bytes 12292
  33.9 2.4 %copy-start.10 = (f32[512,384]{1,0:T(8,128)}, f32[512,384]{1,0:T(8,128)S(1)}, u32[]{:S(2)}) copy-start(f32[512,384]{1,0:T(8,128)S(1)} %local.1.mine_ref) | copy-start | bytes 2359300
  36.3 22.3 %all-to-all-start.1 = ((bf16[32,32,128]{2,1,0:T(8,128)(2,1)}), bf16[32,32,128]{2,1,0:T(8,128)(2,1)S(1)}, u32[]{:S(2)}, u32[]{:S(2)}) async-start(bf16[32,32,128]{2,1,0:T(8,128)(2,1)} %bitcast.11), calls=%async_computation.1 | async-start | bytes 524288 | tf_op jit(solution)/shard_map/all_to_all | solution.py:289
  46.2 15.1 %copy-start.11 = (bf16[256,1024]{1,0:T(8,128)(2,1)}, bf16[256,1024]{1,0:T(8,128)(2,1)S(1)}, u32[]{:S(2)}) copy-start(bf16[256,1024]{1,0:T(8,128)(2,1)S(1)} %constant_dynamic-update-slice_fusion.next_ref) | copy-start | bytes 1572868
  46.2 22.3 %collective-permute-start.4 = (bf16[256,1024]{1,0:T(8,128)(2,1)S(1)}, bf16[256,1024]{1,0:T(8,128)(2,1)S(1)}, u32[]{:S(2)}, u32[]{:S(2)}) collective-permute-start(bf16[256,1024]{1,0:T(8,128)(2,1)S(1)} %constant_dynamic-update-slice_fusion.next_ref), channel_id=1, source_target_pairs={{0,2},{1,3},{2,4},{3,5},{4,6},{5,7},{6,0},{7,1},{8,14},{9,15},{10,... | collective-permute-start | bytes 1572872 | tf_op jit(solution)/shard_map/ppermute | solution.py:305
  52.6 15.9 %collective-permute-start.5 = (bf16[256,1024]{1,0:T(8,128)(2,1)S(1)}, bf16[256,1024]{1,0:T(8,128)(2,1)S(1)}, u32[]{:S(2)}, u32[]{:S(2)}) collective-permute-start(bf16[256,1024]{1,0:T(8,128)(2,1)S(1)} %constant_dynamic-update-slice_fusion.next_ref), channel_id=1, source_target_pairs={{0,8},{8,0},{16,24},{24,16},{32,40},{40,32},{48,56},{56,48},{64,72... | collective-permute-start | bytes 1572872 | tf_op jit(solution)/shard_map/ppermute | solution.py:308
  54.6 13.9 %collective-permute-start.6 = (bf16[128,1024]{1,0:T(8,128)(2,1)S(1)}, bf16[128,1024]{1,0:T(8,128)(2,1)S(1)}, u32[]{:S(2)}, u32[]{:S(2)}) collective-permute-start(bf16[128,1024]{1,0:T(8,128)(2,1)S(1)} %collective-permute-done.3), channel_id=1, source_target_pairs={{0,9},{1,10},{2,11},{3,12},{4,13},{5,14},{6,15},{7,8},{8,7},{9,0},... | collective-permute-start | bytes 786440 | tf_op jit(solution)/shard_map/ppermute | solution.py:305
  61.3 15.3 %all-to-all-start.2 = ((bf16[8,64,128]{2,1,0:T(8,128)(2,1)}), bf16[8,64,128]{2,1,0:T(8,128)(2,1)S(1)}, u32[]{:S(2)}, u32[]{:S(2)}) async-start(bf16[8,64,128]{2,1,0:T(8,128)(2,1)} %bitcast.13), calls=%async_computation.2 | async-start | bytes 262144 | tf_op jit(solution)/shard_map/all_to_all | solution.py:369
  68.5 8.1 %copy-start.12 = (bf16[256,1024]{1,0:T(8,128)(2,1)}, bf16[256,1024]{1,0:T(8,128)(2,1)S(1)}, u32[]{:S(2)}) copy-start(bf16[256,1024]{1,0:T(8,128)(2,1)S(1)} %collective-permute-done.4.last_ref) | copy-start | bytes 1572868
  68.5 8.1 %copy-start.13 = (bf16[256,1024]{1,0:T(8,128)(2,1)}, bf16[256,1024]{1,0:T(8,128)(2,1)S(1)}, u32[]{:S(2)}) copy-start(bf16[256,1024]{1,0:T(8,128)(2,1)S(1)} %collective-permute-done.5.other_ref) | copy-start | bytes 1572868

commit v7 on v5

--- a/solution.py
+++ b/solution.py
@@ -95,7 +95,7 @@
 
 
 def local_kernel(
-    capacity, cands, tokens_ref, w_ref, slot_ref, session_ref, count_ref, length_ref, out_ref, result, sem
+    capacity, cands, tokens_ref, w_ref, slot_ref, session_ref, count_ref, length_ref, result
 ):
     rows = tokens_ref.shape[0]
     head_dim = result.shape[1] // 3
@@ -119,41 +119,28 @@
     result[:, head_dim : 2 * head_dim] = jnp.where(alive, gate, 0.0)
     place = per_row(first_rows(slot_ref, session_ref, capacity, cands)) + within
     result[:, 2 * head_dim :] = jnp.broadcast_to(place, (rows, head_dim))
-    store = pltpu.make_async_copy(result, out_ref, sem)
-    store.start()
-    store.wait()
-
-
-def history_kernel(
-    block, info_ref, query_ref, keys_ref, values_ref, out_ref, info, query, keys, values, result, sems
-):
-    fetches = [
-        pltpu.make_async_copy(source, target, sems.at[n])
-        for n, (source, target) in enumerate(
-            ((info_ref, info), (query_ref, query), (keys_ref, keys), (values_ref, values))
-        )
-    ]
-    for fetch in fetches:
-        fetch.start()
+
+
+def history_kernel(block, info_ref, query_ref, keys_ref, values_ref, out_ref, result, sems):
     history, head_dim = keys_ref.shape
     half_scale = 0.5 * head_dim ** (-0.5)
-    for fetch in fetches:
-        fetch.wait()
-    length = info[:1, :1]
+    length = info_ref[:1, :1]
     divisor = length + 1.0
     seen = iota((history, 1), 0).astype(f32) < length
-    seen_values = jnp.where(seen, values[...], jnp.zeros((), bf16))
+    seen_values = jnp.where(seen, values_ref[...], jnp.zeros((), bf16))
     stores = []
     for n, start in enumerate(range(0, query_ref.shape[0], block)):
         part = pl.ds(start, block)
         half = (
-            lax.dot_general(query[part, :], keys[...], (((1,), (1,)), ((), ())), preferred_element_type=f32)
+            lax.dot_general(
+                query_ref[part, :], keys_ref[...], (((1,), (1,)), ((), ())), preferred_element_type=f32
+            )
             * half_scale
         )
         weights = (half + half * jnp.tanh(half)).astype(bf16)
         summed = jnp.dot(weights, seen_values, preferred_element_type=f32)
         result[part, :] = (summed / divisor).astype(bf16)
-        stores.append(pltpu.make_async_copy(result.at[part, :], out_ref.at[part, :], sems.at[4 + n]))
+        stores.append(pltpu.make_async_copy(result.at[part, :], out_ref.at[part, :], sems.at[n]))
         stores[-1].start()
     for store in stores:
         store.wait()
@@ -179,39 +166,28 @@
     store.wait()
 
 
-held_heads = ((0, 1), (2, 3), (4, -1), (-2, -3))
-
-
 def output_kernel(
     group_ref, me_ref, tokens_ref, gated_ref, own_ref, next_ref, last_ref, other_ref, three_ref,
-    out_ref, gated, weight, tokens, result, sems,
+    out_ref, tokens, result, sems,
 ):
     groups, share, head_dim = gated_ref.shape
     group = group_ref[0]
+    mine = pl.ds(pl.multiple_of(group * share, share), share)
+    fetch_tokens = pltpu.make_async_copy(tokens_ref.at[mine, :], tokens, sems.at[0])
+    fetch_tokens.start()
     sign = jnp.where(me_ref[0] % 2 == 0, -1, 1)
-    double = 2 * head_dim
-    fetches = [pltpu.make_async_copy(gated_ref, gated, sems.at[0])]
-    start = 0
-    for n, source in enumerate((own_ref, next_ref, last_ref, other_ref, three_ref)):
-        size = source.shape[0]
-        fetches.append(pltpu.make_async_copy(source, weight.at[pl.ds(start, size), :], sems.at[1 + n]))
-        start += size
-    mine = pl.ds(pl.multiple_of(group * share, share), share)
-    fetch_tokens = pltpu.make_async_copy(tokens_ref.at[mine, :], tokens, sems.at[6])
-    for fetch in fetches:
-        fetch.start()
-    fetch_tokens.start()
     total = jnp.zeros(result.shape, f32)
-    for pair, waits in enumerate((fetches[:3], fetches[3:4], fetches[4:5], fetches[5:])):
-        for fetch in waits:
-            fetch.wait()
-        rows = jnp.concatenate(
-            [gated[lax.rem(group + sign * head + groups, groups)] for head in held_heads[pair]], axis=1
-        )
-        total = total + jnp.dot(rows, weight[pl.ds(pair * double, double), :], preferred_element_type=f32)
+    for heads, weight in (
+        ((1, 2), next_ref[...]),
+        ((3, 4), last_ref[...]),
+        ((-1, -2), other_ref[...]),
+        ((0, -3), jnp.concatenate([own_ref[...], three_ref[...]], axis=0)),
+    ):
+        rows = jnp.concatenate([gated_ref[lax.rem(group + sign * head + groups, groups)] for head in heads], axis=1)
+        total = total + jnp.dot(rows, weight, preferred_element_type=f32)
     fetch_tokens.wait()
     result[...] = (tokens[...].astype(f32) + total).astype(bf16)
-    store = pltpu.make_async_copy(result, out_ref, sems.at[0])
+    store = pltpu.make_async_copy(result, out_ref, sems.at[1])
     store.start()
     store.wait()
 
@@ -295,28 +271,23 @@
     mine = pl.pallas_call(
         functools.partial(local_kernel, capacity, cands),
         in_specs=[VMEM] * 6,
-        out_specs=HBM,
+        out_specs=VMEM,
         out_shape=jax.ShapeDtypeStruct((rows, 3 * head_dim), f32),
-        scratch_shapes=[pltpu.VMEM((rows, 3 * head_dim), f32), pltpu.SemaphoreType.DMA],
-        compiler_params=params,
+        compiler_params=roomy,
         cost_estimate=pl.CostEstimate(flops=1 << 30, bytes_accessed=16 << 20, transcendentals=1 << 18),
         name="local",
     )(tokens, w_flat, slots, after(named, sent), counts, lengths)
     block = min(256, slot_rows)
     answers = pl.pallas_call(
         functools.partial(history_kernel, block),
-        in_specs=[HBM, ANY, HBM, HBM],
+        in_specs=[VMEM] * 4,
         out_specs=HBM,
         out_shape=jax.ShapeDtypeStruct((slot_rows, head_dim), bf16),
         scratch_shapes=[
-            pltpu.VMEM((8, 128), f32),
             pltpu.VMEM((slot_rows, head_dim), bf16),
-            pltpu.VMEM((history, head_dim), bf16),
-            pltpu.VMEM((history, head_dim), bf16),
-            pltpu.VMEM((slot_rows, head_dim), bf16),
-            pltpu.SemaphoreType.DMA((4 + slot_rows // block,)),
+            pltpu.SemaphoreType.DMA((slot_rows // block,)),
         ],
-        compiler_params=tight,
+        compiler_params=roomy,
         cost_estimate=pl.CostEstimate(flops=1 << 30, bytes_accessed=64 << 20, transcendentals=slot_rows * history),
         name="history",
     )(
@@ -354,17 +325,15 @@
     )
     return pl.pallas_call(
         output_kernel,
-        in_specs=[SMEM, SMEM, HBM] + [ANY] * 6,
+        in_specs=[SMEM, SMEM, HBM] + [VMEM] * 6,
         out_specs=HBM,
         out_shape=jax.ShapeDtypeStruct((share, model_width), bf16),
         scratch_shapes=[
-            pltpu.VMEM((groups, share, head_dim), bf16),
-            pltpu.VMEM((groups * head_dim, model_width), bf16),
             pltpu.VMEM((share, model_width), bf16),
             pltpu.VMEM((share, model_width), bf16),
-            pltpu.SemaphoreType.DMA((7,)),
+            pltpu.SemaphoreType.DMA((2,)),
         ],
-        compiler_params=tight,
+        compiler_params=roomy,
         name="output",
     )(group_index, my_index, tokens, heads, w_own, nexts, lasts, others, other_three)
 

time: 78.4 us -> 77.2 us (0.985)
  Pallas kernels: 17 us -> 11.8 us
  local copies, waits for them, and re-layouts: 1.68 us -> 4.72 us
  waiting for transfers between devices: 11.3 us -> 12.2 us
    unnamed x11 -> x29, local copies, waits for them, and re-layouts: 1.66 us -> 4.7 us
    pallas_call x1, Pallas kernels: 3.87 us -> 1.4 us  [on_device(): pl.pallas_call(functools.partial(local_kernel, capacity, cands), in_specs...]
    pallas_call x2, Pallas kernels: 6.01 us -> 3.62 us  [the longest x1 2.29 us: on_device(): pl.pallas_call(functools.partial(history_kernel, block), in_specs=[VMEM]...]
    all_to_all x1, waiting for transfers between devices: 4.98 us -> 6.44 us  [on_device(): lax.all_to_all(gated.reshape(groups, share, head_dim), 'tensor', split_ax...]
    ppermute x4, waiting for transfers between devices: 4.03 us -> 2.58 us  [passed(): return lax.ppermute(piece, ('replica', 'tensor'), pairs)]
    all_to_all x1, waiting for transfers between devices: 2.24 us -> 3.18 us  [on_device(): lax.all_to_all(answers.reshape(replicas, capacity * cands, head_dim), 're...]
  transfers between devices with their start and end apart: 8 -> 8, of which waited for: 3 -> 3; matrix products, arithmetic and copies ran while one was open for 1% -> 0% of each run, Pallas kernels for 13% -> 8%
where the time goes in v7:
time: 77.2 us; the launch traced here: 76.6 us
  starting transfers between devices  47.6 us (62%)
  waiting for transfers between devices  12.2 us (16%)
  Pallas kernels  11.8 us (15%)
  local copies, waits for them, and re-layouts  4.72 us (6%)
    ppermute x4, starting transfers between devices, passed(): return lax.ppermute(piece, ('replica', 'tensor'), pairs)  16.7 us
    all_to_all x1, starting transfers between devices, on_device(): lax.all_to_all(answers.reshape(replicas, capacity * cands, head_dim), 're...  12.6 us
    all_to_all x1, starting transfers between devices, on_device(): lax.all_to_all(sent.reshape(replicas, capacity * cands, head_dim), 'repli...  10.9 us
    all_to_all x1, waiting for transfers between devices, on_device(): lax.all_to_all(gated.reshape(groups, share, head_dim), 'tensor', split_ax...  6.44 us
    all_to_all x1, starting transfers between devices, on_device(): lax.all_to_all(gated.reshape(groups, share, head_dim), 'tensor', split_ax...  5.36 us
    unnamed x29, local copies, waits for them, and re-layouts  4.7 us
    pallas_call x1, Pallas kernels, on_device(): pl.pallas_call(functools.partial(send_kernel, capacity, cands, chunks), i...  4.47 us
    all_to_all x1, waiting for transfers between devices, on_device(): lax.all_to_all(answers.reshape(replicas, capacity * cands, head_dim), 're...  3.18 us
  transfers between devices with their start and end apart: 8, of which 3 were waited for; matrix products, arithmetic and copies ran while one was open for 0% of the time, Pallas kernels for 8%

profile of v7, /device:TPU:6, one launch (start us, length us, event | category | flops | bytes accessed | tf_op | source)
XLA Modules:
  0.0 76.6 jit_solution(17020343111964189857)
XLA Ops:
  0.0 4.5 %send.1 = (bf16[1024,128]{1,0:T(8,128)(2,1)}, f32[8,128]{1,0:T(8,128)}) custom-call(bf16[512,1024]{1,0:T(8,128)(2,1)} %tokens_ref.5, bf16[1024,512]{1,0:T(8,128)(2,1)} %bitcast.15, s32[1,64]{1,0:T(1,128)} %bitcast.23, s32[1,64]{1,0:T(1,128)} %bitcast.25, s32[1,64]{1,0:T(1,128)} %bitcast.27, s32[1]{0:T(128)} %bitcast.1.me_ref), custom_call_target="tpu_custom_call" | custom-call | tf_op jit(solution)/shard_map/send/pallas_call | solution.py:237
  4.5 0.0 copy-start.3
  4.5 10.9 %all-to-all-start = ((bf16[64,16,128]{2,1,0:T(8,128)(2,1)}), bf16[64,16,128]{2,1,0:T(8,128)(2,1)S(1)}, u32[]{:S(2)}, u32[]{:S(2)}) async-start(bf16[64,16,128]{2,1,0:T(8,128)(2,1)} %bitcast.32), calls=%async_computation | async-start | bytes 524288 | tf_op jit(solution)/shard_map/all_to_all | solution.py:255
  15.4 0.0 copy-start.11
  15.5 0.0 copy-done.3
  15.5 0.0 copy-start.5
  15.5 0.0 copy-start.6
  15.5 0.0 copy-start.7
  15.5 6.2 %collective-permute-start.1 = (bf16[128,1024]{1,0:T(8,128)(2,1)S(1)}, bf16[128,1024]{1,0:T(8,128)(2,1)S(1)}, u32[]{:S(2)}, u32[]{:S(2)}) collective-permute-start(bf16[128,1024]{1,0:T(8,128)(2,1)S(1)} %bitcast.17), channel_id=1, source_target_pairs={{0,2},{1,3},{2,4},{3,5},{4,6},{5,7},{6,0},{7,1},{8,14},{9,15},{10,... | collective-permute-start | bytes 786440 | tf_op jit(solution)/shard_map/ppermute | solution.py:263
  21.7 4.3 %collective-permute-start = (bf16[128,1024]{1,0:T(8,128)(2,1)S(1)}, bf16[128,1024]{1,0:T(8,128)(2,1)S(1)}, u32[]{:S(2)}, u32[]{:S(2)}) collective-permute-start(bf16[128,1024]{1,0:T(8,128)(2,1)S(1)} %bitcast.18), channel_id=1, source_target_pairs={{0,1},{1,2},{2,3},{3,4},{4,5},{5,6},{6,7},{7,0},{8,15},{9,8},{10,9... | collective-permute-start | bytes 786440 | tf_op jit(solution)/shard_map/ppermute | solution.py:263
  26.0 0.0 copy-done.11
  26.0 0.0 copy-done.5
  26.0 0.0 copy-done.6
  26.0 0.0 copy-done.7
  26.1 0.0 copy-start
  26.1 1.2 %copy-done = bf16[512,1024]{1,0:T(8,128)(2,1)S(1)} copy-done((bf16[512,1024]{1,0:T(8,128)(2,1)S(1)}, bf16[512,1024]{1,0:T(8,128)(2,1)}, u32[]{:S(2)}) %copy-start) | copy-done | bytes 1048600
  27.3 0.0 copy-start.2
  27.3 1.2 %copy-done.2 = bf16[1024,1,512]{2,0,1:T(8,128)(2,1)S(1)} copy-done((bf16[1024,1,512]{2,0,1:T(8,128)(2,1)S(1)}, bf16[1024,1,512]{2,0,1:T(8,128)(2,1)}, u32[]{:S(2)}) %copy-start.2) | copy-done | bytes 1048600
  28.5 0.0 copy-start.8
  28.5 0.0 copy-start.9
  28.5 1.4 %local.1.mine_ref = f32[512,384]{1,0:T(8,128)S(1)} custom-call(bf16[512,1024]{1,0:T(8,128)(2,1)S(1)} %copy-done, bf16[1024,512]{1,0:T(8,128)(2,1)S(1)} %bitcast.16, s32[1,64]{1,0:T(1,128)S(1)} %bitcast.24, s32[1,64]{1,0:T(1,128)S(1)} %bitcast.26, s32[1,64]{1,0:T(1,128)S(1)} %bitcast.31, s32[1,64]{1,0:T(1,128)S(1)} %bitcast.28), custom_call_target="tpu_custom_call" | custom-call | flops 1073741824 | bytes 16777216 | tf_op jit(solution)/shard_map/local/pallas_call | solution.py:271
  29.9 0.0 copy-start.12
  29.9 0.9 %copy-done.12 = f32[512,384]{1,0:T(8,128)} copy-done((f32[512,384]{1,0:T(8,128)}, f32[512,384]{1,0:T(8,128)S(1)}, u32[]{:S(2)}) %copy-start.12) | copy-done | bytes 786456
  30.8 0.0 copy-start.10
  30.8 0.0 all-to-all-done
  30.8 0.0 copy-done.8
  30.8 0.0 copy-done.9
  30.8 0.7 copy-done.10
  31.5 2.3 %history.1 = bf16[1024,128]{1,0:T(8,128)(2,1)} custom-call(f32[8,128]{1,0:T(8,128)S(1)} %copy-done.10, bf16[1024,128]{1,0:T(8,128)(2,1)S(1)} %bitcast.21, bf16[1024,128]{1,0:T(8,128)(2,1)S(1)} %bitcast.29, bf16[1024,128]{1,0:T(8,128)(2,1)S(1)} %bitcast.30), custom_call_target="tpu_custom_call" | custom-call | flops 1073741824 | bytes 67108864 | tf_op jit(solution)/shard_map/history/pallas_call | solution.py:281
  33.8 12.6 %all-to-all-start.1 = ((bf16[64,16,128]{2,1,0:T(8,128)(2,1)}), bf16[64,16,128]{2,1,0:T(8,128)(2,1)S(1)}, u32[]{:S(2)}, u32[]{:S(2)}) async-start(bf16[64,16,128]{2,1,0:T(8,128)(2,1)} %bitcast.11), calls=%async_computation.1 | async-start | bytes 524288 | tf_op jit(solution)/shard_map/all_to_all | solution.py:304
  46.4 0.0 collective-permute-done.1
  46.4 0.0 copy-start.13
  46.4 0.0 collective-permute-done
  46.4 2.1 %collective-permute-start.3 = (bf16[256,1024]{1,0:T(8,128)(2,1)S(1)}, bf16[256,1024]{1,0:T(8,128)(2,1)S(1)}, u32[]{:S(2)}, u32[]{:S(2)}) collective-permute-start(bf16[256,1024]{1,0:T(8,128)(2,1)S(1)} %constant_dynamic-update-slice_fusion.next_ref), channel_id=1, source_target_pairs={{0,8},{8,0},{16,24},{24,16},{32,40},{40,32},{48,56},{56,48},{64,72... | collective-permute-start | bytes 1572872 | tf_op jit(solution)/shard_map/ppermute | solution.py:266
  48.5 0.0 copy-done.13
  48.5 4.3 %collective-permute-start.2 = (bf16[256,1024]{1,0:T(8,128)(2,1)S(1)}, bf16[256,1024]{1,0:T(8,128)(2,1)S(1)}, u32[]{:S(2)}, u32[]{:S(2)}) collective-permute-start(bf16[256,1024]{1,0:T(8,128)(2,1)S(1)} %constant_dynamic-update-slice_fusion.next_ref), channel_id=1, source_target_pairs={{0,2},{1,3},{2,4},{3,5},{4,6},{5,7},{6,0},{7,1},{8,14},{9,15},{10,... | collective-permute-start | bytes 1572872 | tf_op jit(solution)/shard_map/ppermute | solution.py:263
  52.8 1.9 %collective-permute-start.4 = (bf16[128,1024]{1,0:T(8,128)(2,1)}, bf16[128,1024]{1,0:T(8,128)(2,1)S(1)}, u32[]{:S(2)}, u32[]{:S(2)}) collective-permute-start(bf16[128,1024]{1,0:T(8,128)(2,1)} %copy-done.13), channel_id=1, source_target_pairs={{0,9},{1,10},{2,11},{3,12},{4,13},{5,14},{6,15},{7,8},{8,7},{9,0},... | collective-permute-start | bytes 786440 | tf_op jit(solution)/shard_map/ppermute | solution.py:263
  54.7 3.2 %all-to-all-done.1 = bf16[64,16,128]{2,1,0:T(8,128)(2,1)S(1)} async-done(((bf16[64,16,128]{2,1,0:T(8,128)(2,1)}), bf16[64,16,128]{2,1,0:T(8,128)(2,1)S(1)}, u32[]{:S(2)}, u32[]{:S(2)}) %all-to-all-start.1) | async-done | bytes 262176 | tf_op jit(solution)/shard_map/all_to_all | solution.py:304
  57.9 2.3 %gate.1 = bf16[512,128]{1,0:T(8,128)(2,1)S(1)} custom-call(bf16[1024,128]{1,0:T(8,128)(2,1)S(1)} %bitcast.20, f32[512,384]{1,0:T(8,128)} %copy-done.12), custom_call_target="tpu_custom_call" | custom-call | flops 1073741824 | bytes 67108864 | tf_op jit(solution)/shard_map/gate/pallas_call | solution.py:307
  60.2 0.0 copy-start.4
  60.2 0.6 copy-done.4
  60.9 5.4 %all-to-all-start.2 = ((bf16[8,64,128]{2,1,0:T(8,128)(2,1)}), bf16[8,64,128]{2,1,0:T(8,128)(2,1)S(1)}, u32[]{:S(2)}, u32[]{:S(2)}) async-start(bf16[8,64,128]{2,1,0:T(8,128)(2,1)} %bitcast.22), calls=%async_computation.2 | async-start | bytes 262144 | tf_op jit(solution)/shard_map/all_to_all | solution.py:323
  66.2 2.6 %collective-permute-done.4.three_ref = bf16[128,1024]{1,0:T(8,128)(2,1)S(1)} collective-permute-done((bf16[128,1024]{1,0:T(8,128)(2,1)}, bf16[128,1024]{1,0:T(8,128)(2,1)S(1)}, u32[]{:S(2)}, u32[]{:S(2)}) %collective-permute-start.4) | collective-permute-done | bytes 262176 | tf_op jit(solution)/shard_map/ppermute | solution.py:263
  68.8 0.0 collective-permute-done.3.other_ref
  68.8 0.0 collective-permute-done.2.last_ref
  68.8 6.4 %all-to-all-done.2.gated_ref = bf16[8,64,128]{2,1,0:T(8,128)(2,1)S(1)} async-done(((bf16[8,64,128]{2,1,0:T(8,128)(2,1)}), bf16[8,64,128]{2,1,0:T(8,128)(2,1)S(1)}, u32[]{:S(2)}, u32[]{:S(2)}) %all-to-all-start.2) | async-done | bytes 131104 | tf_op jit(solution)/shard_map/all_to_all | solution.py:323
  75.3 0.0 copy-done.1
  75.3 1.3 %output.1 = bf16[64,1024]{1,0:T(8,128)(2,1)} custom-call(s32[1]{0:T(128)} %bitcast.group_ref, s32[1]{0:T(128)} %bitcast.1.me_ref, bf16[512,1024]{1,0:T(8,128)(2,1)S(1)} %copy-done.1, bf16[8,64,128]{2,1,0:T(8,128)(2,1)S(1)} %all-to-all-done.2.gated_ref, bf16[128,1024]{1,0:T(8,128)(2,1)S(1)} %bitcast.19, ...), custom_call_target="tpu_custom_call" | custom-call | tf_op jit(solution)/shard_map/output/pallas_call | solution.py:326
  (3 shorter events, 0.0 us)
Async XLA Ops:
  4.5 11.0 %copy-start.3 = (bf16[1,128,1024]{2,1,0:T(8,128)(2,1)S(1)}, bf16[1,128,1024]{2,1,0:T(8,128)(2,1)}, u32[]{:S(2)}) copy-start(bf16[1,128,1024]{2,1,0:T(8,128)(2,1)} %param.11) | copy-start | bytes 786436
  4.5 26.3 %all-to-all-start = ((bf16[64,16,128]{2,1,0:T(8,128)(2,1)}), bf16[64,16,128]{2,1,0:T(8,128)(2,1)S(1)}, u32[]{:S(2)}, u32[]{:S(2)}) async-start(bf16[64,16,128]{2,1,0:T(8,128)(2,1)} %bitcast.32), calls=%async_computation | async-start | bytes 524288 | tf_op jit(solution)/shard_map/all_to_all | solution.py:255
  15.4 10.6 %copy-start.11 = (s32[64]{0:T(128)S(1)}, s32[64]{0:T(128)}, u32[]{:S(2)}) copy-start(s32[64]{0:T(128)} %param.16) | copy-start | bytes 772
  15.5 10.6 %copy-start.5 = (s32[64]{0:T(128)S(1)}, s32[64]{0:T(128)}, u32[]{:S(2)}) copy-start(s32[64]{0:T(128)} %param.14) | copy-start | bytes 772
  15.5 10.6 %copy-start.6 = (s32[64]{0:T(128)S(1)}, s32[64]{0:T(128)}, u32[]{:S(2)}) copy-start(s32[64]{0:T(128)} %param.15) | copy-start | bytes 772
  15.5 10.6 %copy-start.7 = (s32[64]{0:T(128)S(1)}, s32[64]{0:T(128)}, u32[]{:S(2)}) copy-start(s32[64]{0:T(128)} %param.17) | copy-start | bytes 772
  15.5 30.9 %collective-permute-start.1 = (bf16[128,1024]{1,0:T(8,128)(2,1)S(1)}, bf16[128,1024]{1,0:T(8,128)(2,1)S(1)}, u32[]{:S(2)}, u32[]{:S(2)}) collective-permute-start(bf16[128,1024]{1,0:T(8,128)(2,1)S(1)} %bitcast.17), channel_id=1, source_target_pairs={{0,2},{1,3},{2,4},{3,5},{4,6},{5,7},{6,0},{7,1},{8,14},{9,15},{10,... | collective-permute-start | bytes 786440 | tf_op jit(solution)/shard_map/ppermute | solution.py:263
  21.7 24.6 %collective-permute-start = (bf16[128,1024]{1,0:T(8,128)(2,1)S(1)}, bf16[128,1024]{1,0:T(8,128)(2,1)S(1)}, u32[]{:S(2)}, u32[]{:S(2)}) collective-permute-start(bf16[128,1024]{1,0:T(8,128)(2,1)S(1)} %bitcast.18), channel_id=1, source_target_pairs={{0,1},{1,2},{2,3},{3,4},{4,5},{5,6},{6,7},{7,0},{8,15},{9,8},{10,9... | collective-permute-start | bytes 786440 | tf_op jit(solution)/shard_map/ppermute | solution.py:263
  26.1 1.2 %copy-start = (bf16[512,1024]{1,0:T(8,128)(2,1)S(1)}, bf16[512,1024]{1,0:T(8,128)(2,1)}, u32[]{:S(2)}) copy-start(bf16[512,1024]{1,0:T(8,128)(2,1)} %tokens_ref.5) | copy-start | bytes 3145732
  27.3 1.2 %copy-start.2 = (bf16[1024,1,512]{2,0,1:T(8,128)(2,1)S(1)}, bf16[1024,1,512]{2,0,1:T(8,128)(2,1)}, u32[]{:S(2)}) copy-start(bf16[1024,1,512]{2,0,1:T(8,128)(2,1)} %param.10) | copy-start | bytes 3145732
  28.5 2.3 %copy-start.8 = (bf16[1,1024,1,128]{3,1,2,0:T(8,128)(2,1)S(1)}, bf16[1,1024,1,128]{3,1,2,0:T(8,128)(2,1)}, u32[]{:S(2)}) copy-start(bf16[1,1024,1,128]{3,1,2,0:T(8,128)(2,1)} %param.12) | copy-start | bytes 786436
  28.5 2.3 %copy-start.9 = (bf16[1,1024,1,128]{3,1,2,0:T(8,128)(2,1)S(1)}, bf16[1,1024,1,128]{3,1,2,0:T(8,128)(2,1)}, u32[]{:S(2)}) copy-start(bf16[1,1024,1,128]{3,1,2,0:T(8,128)(2,1)} %param.13) | copy-start | bytes 786436
  29.9 0.9 %copy-start.12 = (f32[512,384]{1,0:T(8,128)}, f32[512,384]{1,0:T(8,128)S(1)}, u32[]{:S(2)}) copy-start(f32[512,384]{1,0:T(8,128)S(1)} %local.1.mine_ref) | copy-start | bytes 2359300
  30.8 0.7 copy-start.10
  33.8 24.1 %all-to-all-start.1 = ((bf16[64,16,128]{2,1,0:T(8,128)(2,1)}), bf16[64,16,128]{2,1,0:T(8,128)(2,1)S(1)}, u32[]{:S(2)}, u32[]{:S(2)}) async-start(bf16[64,16,128]{2,1,0:T(8,128)(2,1)} %bitcast.11), calls=%async_computation.1 | async-start | bytes 524288 | tf_op jit(solution)/shard_map/all_to_all | solution.py:304
  46.4 2.1 %copy-start.13 = (bf16[128,1024]{1,0:T(8,128)(2,1)}, bf16[128,1024]{1,0:T(8,128)(2,1)S(1)}, u32[]{:S(2)}) copy-start(bf16[128,1024]{1,0:T(8,128)(2,1)S(1)} %collective-permute-done.1) | copy-start | bytes 786436
  46.4 22.4 %collective-permute-start.3 = (bf16[256,1024]{1,0:T(8,128)(2,1)S(1)}, bf16[256,1024]{1,0:T(8,128)(2,1)S(1)}, u32[]{:S(2)}, u32[]{:S(2)}) collective-permute-start(bf16[256,1024]{1,0:T(8,128)(2,1)S(1)} %constant_dynamic-update-slice_fusion.next_ref), channel_id=1, source_target_pairs={{0,8},{8,0},{16,24},{24,16},{32,40},{40,32},{48,56},{56,48},{64,72... | collective-permute-start | bytes 1572872 | tf_op jit(solution)/shard_map/ppermute | solution.py:266
  48.5 20.3 %collective-permute-start.2 = (bf16[256,1024]{1,0:T(8,128)(2,1)S(1)}, bf16[256,1024]{1,0:T(8,128)(2,1)S(1)}, u32[]{:S(2)}, u32[]{:S(2)}) collective-permute-start(bf16[256,1024]{1,0:T(8,128)(2,1)S(1)} %constant_dynamic-update-slice_fusion.next_ref), channel_id=1, source_target_pairs={{0,2},{1,3},{2,4},{3,5},{4,6},{5,7},{6,0},{7,1},{8,14},{9,15},{10,... | collective-permute-start | bytes 1572872 | tf_op jit(solution)/shard_map/ppermute | solution.py:263
  52.8 16.0 %collective-permute-start.4 = (bf16[128,1024]{1,0:T(8,128)(2,1)}, bf16[128,1024]{1,0:T(8,128)(2,1)S(1)}, u32[]{:S(2)}, u32[]{:S(2)}) collective-permute-start(bf16[128,1024]{1,0:T(8,128)(2,1)} %copy-done.13), channel_id=1, source_target_pairs={{0,9},{1,10},{2,11},{3,12},{4,13},{5,14},{6,15},{7,8},{8,7},{9,0},... | collective-permute-start | bytes 786440 | tf_op jit(solution)/shard_map/ppermute | solution.py:263
  57.9 17.3 %copy-start.1 = (bf16[512,1024]{1,0:T(8,128)(2,1)S(1)}, bf16[512,1024]{1,0:T(8,128)(2,1)}, u32[]{:S(2)}) copy-start(bf16[512,1024]{1,0:T(8,128)(2,1)} %tokens_ref.5) | copy-start | bytes 3145732
  60.2 0.7 copy-start.4
  60.9 14.4 %all-to-all-start.2 = ((bf16[8,64,128]{2,1,0:T(8,128)(2,1)}), bf16[8,64,128]{2,1,0:T(8,128)(2,1)S(1)}, u32[]{:S(2)}, u32[]{:S(2)}) async-start(bf16[8,64,128]{2,1,0:T(8,128)(2,1)} %bitcast.22), calls=%async_computation.2 | async-start | bytes 262144 | tf_op jit(solution)/shard_map/all_to_all | solution.py:323

commit v8 on v7

--- a/solution.py
+++ b/solution.py
@@ -167,7 +167,7 @@
 
 
 def output_kernel(
-    group_ref, me_ref, tokens_ref, gated_ref, own_ref, next_ref, last_ref, other_ref, three_ref,
+    group_ref, me_ref, tokens_ref, gated_ref, own_ref, next_ref, last_ref, other_ref, two_ref,
     out_ref, tokens, result, sems,
 ):
     groups, share, head_dim = gated_ref.shape
@@ -178,10 +178,10 @@
     sign = jnp.where(me_ref[0] % 2 == 0, -1, 1)
     total = jnp.zeros(result.shape, f32)
     for heads, weight in (
-        ((1, 2), next_ref[...]),
-        ((3, 4), last_ref[...]),
-        ((-1, -2), other_ref[...]),
-        ((0, -3), jnp.concatenate([own_ref[...], three_ref[...]], axis=0)),
+        ((1, 3), next_ref[...]),
+        ((2, 4), last_ref[...]),
+        ((-1, -3), other_ref[...]),
+        ((0, -2), jnp.concatenate([own_ref[...], two_ref[...]], axis=0)),
     ):
         rows = jnp.concatenate([gated_ref[lax.rem(group + sign * head + groups, groups)] for head in heads], axis=1)
         total = total + jnp.dot(rows, weight, preferred_element_type=f32)
@@ -267,7 +267,7 @@
 
     w_own = after(w_out.reshape(head_dim, model_width), sent)
     next_one = passed(w_own, 1)
-    next_two = passed(w_own, 2)
+    next_three = passed(w_own, 3)
     mine = pl.pallas_call(
         functools.partial(local_kernel, capacity, cands),
         in_specs=[VMEM] * 6,
@@ -296,11 +296,11 @@
         cache_keys.reshape(history, head_dim),
         cache_values.reshape(history, head_dim),
     )
-    next_one, next_two = after((next_one, next_two), answers)
-    nexts = jnp.concatenate([next_one, next_two], axis=0)
-    lasts = passed(nexts, 2)
+    next_one, next_three = after((next_one, next_three), answers)
+    nexts = jnp.concatenate([next_one, next_three], axis=0)
+    lasts = passed(nexts, 1)
     others = swapped(nexts)
-    other_three = passed(next_two, 1, flip=1)
+    other_two = passed(next_one, 1, flip=1)
     returned = lax.all_to_all(
         answers.reshape(replicas, capacity * cands, head_dim), "replica", split_axis=0, concat_axis=0, tiled=True
     )
@@ -335,7 +335,7 @@
         ],
         compiler_params=roomy,
         name="output",
-    )(group_index, my_index, tokens, heads, w_own, nexts, lasts, others, other_three)
+    )(group_index, my_index, tokens, heads, w_own, nexts, lasts, others, other_two)
 
 
 def solution(mesh):

time: 77.2 us -> 77.6 us (level)
  waiting for transfers between devices: 12.2 us -> 13.2 us
    all_to_all x1, waiting for transfers between devices: 6.44 us -> 9.34 us  [on_device(): lax.all_to_all(gated.reshape(groups, share, head_dim), 'tensor', split_ax...]
    ppermute x4, waiting for transfers between devices: 2.58 us -> 0.01 us  [passed(): return lax.ppermute(piece, ('replica', 'tensor'), pairs)]
    ppermute x4, starting transfers between devices: 16.7 us -> 19 us  [passed(): return lax.ppermute(piece, ('replica', 'tensor'), pairs)]
    all_to_all x1, starting transfers between devices: 12.6 us -> 10.3 us  [on_device(): lax.all_to_all(answers.reshape(replicas, capacity * cands, head_dim), 're...]
    all_to_all x1, starting transfers between devices: 5.36 us -> 4.57 us  [on_device(): lax.all_to_all(gated.reshape(groups, share, head_dim), 'tensor', split_ax...]
  transfers between devices with their start and end apart: 8 -> 8, of which waited for: 3 -> 2; matrix products, arithmetic and copies ran while one was open for 0% -> 0% of each run, Pallas kernels for 8% -> 8%
where the time goes in v8:
time: 77.6 us; the launch traced here: 76.9 us
  starting transfers between devices  47 us (61%)
  waiting for transfers between devices  13.2 us (17%)
  Pallas kernels  11.8 us (15%)
  local copies, waits for them, and re-layouts  4.72 us (6%)
    ppermute x4, starting transfers between devices, passed(): return lax.ppermute(piece, ('replica', 'tensor'), pairs)  19 us
    all_to_all x1, starting transfers between devices, on_device(): lax.all_to_all(sent.reshape(replicas, capacity * cands, head_dim), 'repli...  10.9 us
    all_to_all x1, starting transfers between devices, on_device(): lax.all_to_all(answers.reshape(replicas, capacity * cands, head_dim), 're...  10.3 us
    all_to_all x1, waiting for transfers between devices, on_device(): lax.all_to_all(gated.reshape(groups, share, head_dim), 'tensor', split_ax...  9.34 us
    unnamed x29, local copies, waits for them, and re-layouts  4.7 us
    all_to_all x1, starting transfers between devices, on_device(): lax.all_to_all(gated.reshape(groups, share, head_dim), 'tensor', split_ax...  4.57 us
    pallas_call x1, Pallas kernels, on_device(): pl.pallas_call(functools.partial(send_kernel, capacity, cands, chunks), i...  4.47 us
    all_to_all x1, waiting for transfers between devices, on_device(): lax.all_to_all(answers.reshape(replicas, capacity * cands, head_dim), 're...  3.85 us
  transfers between devices with their start and end apart: 8, of which 2 were waited for; matrix products, arithmetic and copies ran while one was open for 0% of the time, Pallas kernels for 8%

profile of v8, /device:TPU:6, one launch (start us, length us, event | category | flops | bytes accessed | tf_op | source)
XLA Modules:
  0.0 76.9 jit_solution(9049003626762198997)
XLA Ops:
  0.0 4.5 %send.1 = (bf16[1024,128]{1,0:T(8,128)(2,1)}, f32[8,128]{1,0:T(8,128)}) custom-call(bf16[512,1024]{1,0:T(8,128)(2,1)} %tokens_ref.5, bf16[1024,512]{1,0:T(8,128)(2,1)} %bitcast.15, s32[1,64]{1,0:T(1,128)} %bitcast.23, s32[1,64]{1,0:T(1,128)} %bitcast.25, s32[1,64]{1,0:T(1,128)} %bitcast.27, s32[1]{0:T(128)} %bitcast.1.me_ref), custom_call_target="tpu_custom_call" | custom-call | tf_op jit(solution)/shard_map/send/pallas_call | solution.py:237
  4.5 0.0 copy-start.3
  4.5 10.9 %all-to-all-start = ((bf16[64,16,128]{2,1,0:T(8,128)(2,1)}), bf16[64,16,128]{2,1,0:T(8,128)(2,1)S(1)}, u32[]{:S(2)}, u32[]{:S(2)}) async-start(bf16[64,16,128]{2,1,0:T(8,128)(2,1)} %bitcast.32), calls=%async_computation | async-start | bytes 524288 | tf_op jit(solution)/shard_map/all_to_all | solution.py:255
  15.4 0.0 copy-start.11
  15.5 0.0 copy-done.3
  15.5 0.0 copy-start.5
  15.5 0.0 copy-start.6
  15.5 0.0 copy-start.7
  15.5 8.0 %collective-permute-start.1 = (bf16[128,1024]{1,0:T(8,128)(2,1)S(1)}, bf16[128,1024]{1,0:T(8,128)(2,1)S(1)}, u32[]{:S(2)}, u32[]{:S(2)}) collective-permute-start(bf16[128,1024]{1,0:T(8,128)(2,1)S(1)} %bitcast.17), channel_id=1, source_target_pairs={{0,3},{1,4},{2,5},{3,6},{4,7},{5,0},{6,1},{7,2},{8,13},{9,14},{10,... | collective-permute-start | bytes 786440 | tf_op jit(solution)/shard_map/ppermute | solution.py:263
  23.5 5.5 %collective-permute-start = (bf16[128,1024]{1,0:T(8,128)(2,1)S(1)}, bf16[128,1024]{1,0:T(8,128)(2,1)S(1)}, u32[]{:S(2)}, u32[]{:S(2)}) collective-permute-start(bf16[128,1024]{1,0:T(8,128)(2,1)S(1)} %bitcast.18), channel_id=1, source_target_pairs={{0,1},{1,2},{2,3},{3,4},{4,5},{5,6},{6,7},{7,0},{8,15},{9,8},{10,9... | collective-permute-start | bytes 786440 | tf_op jit(solution)/shard_map/ppermute | solution.py:263
  29.0 0.0 copy-done.11
  29.0 0.0 copy-done.5
  29.1 0.0 copy-done.6
  29.1 0.0 copy-done.7
  29.1 0.0 copy-start
  29.1 1.2 %copy-done = bf16[512,1024]{1,0:T(8,128)(2,1)S(1)} copy-done((bf16[512,1024]{1,0:T(8,128)(2,1)S(1)}, bf16[512,1024]{1,0:T(8,128)(2,1)}, u32[]{:S(2)}) %copy-start) | copy-done | bytes 1048600
  30.3 0.0 copy-start.2
  30.3 1.2 %copy-done.2 = bf16[1024,1,512]{2,0,1:T(8,128)(2,1)S(1)} copy-done((bf16[1024,1,512]{2,0,1:T(8,128)(2,1)S(1)}, bf16[1024,1,512]{2,0,1:T(8,128)(2,1)}, u32[]{:S(2)}) %copy-start.2) | copy-done | bytes 1048600
  31.5 0.0 copy-start.8
  31.5 0.0 copy-start.9
  31.5 1.4 %local.1.mine_ref = f32[512,384]{1,0:T(8,128)S(1)} custom-call(bf16[512,1024]{1,0:T(8,128)(2,1)S(1)} %copy-done, bf16[1024,512]{1,0:T(8,128)(2,1)S(1)} %bitcast.16, s32[1,64]{1,0:T(1,128)S(1)} %bitcast.24, s32[1,64]{1,0:T(1,128)S(1)} %bitcast.26, s32[1,64]{1,0:T(1,128)S(1)} %bitcast.31, s32[1,64]{1,0:T(1,128)S(1)} %bitcast.28), custom_call_target="tpu_custom_call" | custom-call | flops 1073741824 | bytes 16777216 | tf_op jit(solution)/shard_map/local/pallas_call | solution.py:271
  32.9 0.0 copy-start.12
  32.9 0.9 %copy-done.12 = f32[512,384]{1,0:T(8,128)} copy-done((f32[512,384]{1,0:T(8,128)}, f32[512,384]{1,0:T(8,128)S(1)}, u32[]{:S(2)}) %copy-start.12) | copy-done | bytes 786456
  33.8 0.0 copy-start.10
  33.8 0.0 all-to-all-done
  33.8 0.0 copy-done.8
  33.8 0.0 copy-done.9
  33.8 0.7 copy-done.10
  34.5 2.3 %history.1 = bf16[1024,128]{1,0:T(8,128)(2,1)} custom-call(f32[8,128]{1,0:T(8,128)S(1)} %copy-done.10, bf16[1024,128]{1,0:T(8,128)(2,1)S(1)} %bitcast.21, bf16[1024,128]{1,0:T(8,128)(2,1)S(1)} %bitcast.29, bf16[1024,128]{1,0:T(8,128)(2,1)S(1)} %bitcast.30), custom_call_target="tpu_custom_call" | custom-call | flops 1073741824 | bytes 67108864 | tf_op jit(solution)/shard_map/history/pallas_call | solution.py:281
  36.8 10.3 %all-to-all-start.1 = ((bf16[64,16,128]{2,1,0:T(8,128)(2,1)}), bf16[64,16,128]{2,1,0:T(8,128)(2,1)S(1)}, u32[]{:S(2)}, u32[]{:S(2)}) async-start(bf16[64,16,128]{2,1,0:T(8,128)(2,1)} %bitcast.11), calls=%async_computation.1 | async-start | bytes 524288 | tf_op jit(solution)/shard_map/all_to_all | solution.py:304
  47.1 0.0 collective-permute-done.1
  47.2 0.0 collective-permute-done
  47.2 0.0 copy-start.13
  47.2 2.1 %collective-permute-start.3 = (bf16[256,1024]{1,0:T(8,128)(2,1)S(1)}, bf16[256,1024]{1,0:T(8,128)(2,1)S(1)}, u32[]{:S(2)}, u32[]{:S(2)}) collective-permute-start(bf16[256,1024]{1,0:T(8,128)(2,1)S(1)} %constant_dynamic-update-slice_fusion.next_ref), channel_id=1, source_target_pairs={{0,8},{8,0},{16,24},{24,16},{32,40},{40,32},{48,56},{56,48},{64,72... | collective-permute-start | bytes 1572872 | tf_op jit(solution)/shard_map/ppermute | solution.py:266
  49.3 0.0 copy-done.13
  49.3 3.4 %collective-permute-start.2 = (bf16[256,1024]{1,0:T(8,128)(2,1)S(1)}, bf16[256,1024]{1,0:T(8,128)(2,1)S(1)}, u32[]{:S(2)}, u32[]{:S(2)}) collective-permute-start(bf16[256,1024]{1,0:T(8,128)(2,1)S(1)} %constant_dynamic-update-slice_fusion.next_ref), channel_id=1, source_target_pairs={{0,1},{1,2},{2,3},{3,4},{4,5},{5,6},{6,7},{7,0},{8,15},{9,8},{10,9... | collective-permute-start | bytes 1572872 | tf_op jit(solution)/shard_map/ppermute | solution.py:263
  52.7 2.1 %collective-permute-start.4 = (bf16[128,1024]{1,0:T(8,128)(2,1)}, bf16[128,1024]{1,0:T(8,128)(2,1)S(1)}, u32[]{:S(2)}, u32[]{:S(2)}) collective-permute-start(bf16[128,1024]{1,0:T(8,128)(2,1)} %copy-done.13), channel_id=1, source_target_pairs={{0,9},{1,10},{2,11},{3,12},{4,13},{5,14},{6,15},{7,8},{8,7},{9,0},... | collective-permute-start | bytes 786440 | tf_op jit(solution)/shard_map/ppermute | solution.py:263
  54.8 3.9 %all-to-all-done.1 = bf16[64,16,128]{2,1,0:T(8,128)(2,1)S(1)} async-done(((bf16[64,16,128]{2,1,0:T(8,128)(2,1)}), bf16[64,16,128]{2,1,0:T(8,128)(2,1)S(1)}, u32[]{:S(2)}, u32[]{:S(2)}) %all-to-all-start.1) | async-done | bytes 262176 | tf_op jit(solution)/shard_map/all_to_all | solution.py:304
  58.7 2.3 %gate.1 = bf16[512,128]{1,0:T(8,128)(2,1)S(1)} custom-call(bf16[1024,128]{1,0:T(8,128)(2,1)S(1)} %bitcast.20, f32[512,384]{1,0:T(8,128)} %copy-done.12), custom_call_target="tpu_custom_call" | custom-call | flops 1073741824 | bytes 67108864 | tf_op jit(solution)/shard_map/gate/pallas_call | solution.py:307
  61.0 0.0 copy-start.4
  61.0 0.6 copy-done.4
  61.7 4.6 %all-to-all-start.2 = ((bf16[8,64,128]{2,1,0:T(8,128)(2,1)}), bf16[8,64,128]{2,1,0:T(8,128)(2,1)S(1)}, u32[]{:S(2)}, u32[]{:S(2)}) async-start(bf16[8,64,128]{2,1,0:T(8,128)(2,1)} %bitcast.22), calls=%async_computation.2 | async-start | bytes 262144 | tf_op jit(solution)/shard_map/all_to_all | solution.py:323
  66.2 0.0 collective-permute-done.4.two_ref
  66.2 0.0 collective-permute-done.3.other_ref
  66.3 0.0 collective-permute-done.2.last_ref
  66.3 9.3 %all-to-all-done.2.gated_ref = bf16[8,64,128]{2,1,0:T(8,128)(2,1)S(1)} async-done(((bf16[8,64,128]{2,1,0:T(8,128)(2,1)}), bf16[8,64,128]{2,1,0:T(8,128)(2,1)S(1)}, u32[]{:S(2)}, u32[]{:S(2)}) %all-to-all-start.2) | async-done | bytes 131104 | tf_op jit(solution)/shard_map/all_to_all | solution.py:323
  75.6 0.0 copy-done.1
  75.6 1.3 %output.1 = bf16[64,1024]{1,0:T(8,128)(2,1)} custom-call(s32[1]{0:T(128)} %bitcast.group_ref, s32[1]{0:T(128)} %bitcast.1.me_ref, bf16[512,1024]{1,0:T(8,128)(2,1)S(1)} %copy-done.1, bf16[8,64,128]{2,1,0:T(8,128)(2,1)S(1)} %all-to-all-done.2.gated_ref, bf16[128,1024]{1,0:T(8,128)(2,1)S(1)} %bitcast.19, ...), custom_call_target="tpu_custom_call" | custom-call | tf_op jit(solution)/shard_map/output/pallas_call | solution.py:326
  (3 shorter events, 0.0 us)
Async XLA Ops:
  4.5 11.0 %copy-start.3 = (bf16[1,128,1024]{2,1,0:T(8,128)(2,1)S(1)}, bf16[1,128,1024]{2,1,0:T(8,128)(2,1)}, u32[]{:S(2)}) copy-start(bf16[1,128,1024]{2,1,0:T(8,128)(2,1)} %param.11) | copy-start | bytes 786436
  4.5 29.3 %all-to-all-start = ((bf16[64,16,128]{2,1,0:T(8,128)(2,1)}), bf16[64,16,128]{2,1,0:T(8,128)(2,1)S(1)}, u32[]{:S(2)}, u32[]{:S(2)}) async-start(bf16[64,16,128]{2,1,0:T(8,128)(2,1)} %bitcast.32), calls=%async_computation | async-start | bytes 524288 | tf_op jit(solution)/shard_map/all_to_all | solution.py:255
  15.4 13.6 %copy-start.11 = (s32[64]{0:T(128)S(1)}, s32[64]{0:T(128)}, u32[]{:S(2)}) copy-start(s32[64]{0:T(128)} %param.16) | copy-start | bytes 772
  15.5 13.6 %copy-start.5 = (s32[64]{0:T(128)S(1)}, s32[64]{0:T(128)}, u32[]{:S(2)}) copy-start(s32[64]{0:T(128)} %param.14) | copy-start | bytes 772
  15.5 13.6 %copy-start.6 = (s32[64]{0:T(128)S(1)}, s32[64]{0:T(128)}, u32[]{:S(2)}) copy-start(s32[64]{0:T(128)} %param.15) | copy-start | bytes 772
  15.5 13.6 %copy-start.7 = (s32[64]{0:T(128)S(1)}, s32[64]{0:T(128)}, u32[]{:S(2)}) copy-start(s32[64]{0:T(128)} %param.17) | copy-start | bytes 772
  15.5 31.6 %collective-permute-start.1 = (bf16[128,1024]{1,0:T(8,128)(2,1)S(1)}, bf16[128,1024]{1,0:T(8,128)(2,1)S(1)}, u32[]{:S(2)}, u32[]{:S(2)}) collective-permute-start(bf16[128,1024]{1,0:T(8,128)(2,1)S(1)} %bitcast.17), channel_id=1, source_target_pairs={{0,3},{1,4},{2,5},{3,6},{4,7},{5,0},{6,1},{7,2},{8,13},{9,14},{10,... | collective-permute-start | bytes 786440 | tf_op jit(solution)/shard_map/ppermute | solution.py:263
  23.5 23.6 %collective-permute-start = (bf16[128,1024]{1,0:T(8,128)(2,1)S(1)}, bf16[128,1024]{1,0:T(8,128)(2,1)S(1)}, u32[]{:S(2)}, u32[]{:S(2)}) collective-permute-start(bf16[128,1024]{1,0:T(8,128)(2,1)S(1)} %bitcast.18), channel_id=1, source_target_pairs={{0,1},{1,2},{2,3},{3,4},{4,5},{5,6},{6,7},{7,0},{8,15},{9,8},{10,9... | collective-permute-start | bytes 786440 | tf_op jit(solution)/shard_map/ppermute | solution.py:263
  29.1 1.2 %copy-start = (bf16[512,1024]{1,0:T(8,128)(2,1)S(1)}, bf16[512,1024]{1,0:T(8,128)(2,1)}, u32[]{:S(2)}) copy-start(bf16[512,1024]{1,0:T(8,128)(2,1)} %tokens_ref.5) | copy-start | bytes 3145732
  30.3 1.2 %copy-start.2 = (bf16[1024,1,512]{2,0,1:T(8,128)(2,1)S(1)}, bf16[1024,1,512]{2,0,1:T(8,128)(2,1)}, u32[]{:S(2)}) copy-start(bf16[1024,1,512]{2,0,1:T(8,128)(2,1)} %param.10) | copy-start | bytes 3145732
  31.5 2.3 %copy-start.8 = (bf16[1,1024,1,128]{3,1,2,0:T(8,128)(2,1)S(1)}, bf16[1,1024,1,128]{3,1,2,0:T(8,128)(2,1)}, u32[]{:S(2)}) copy-start(bf16[1,1024,1,128]{3,1,2,0:T(8,128)(2,1)} %param.12) | copy-start | bytes 786436
  31.5 2.3 %copy-start.9 = (bf16[1,1024,1,128]{3,1,2,0:T(8,128)(2,1)S(1)}, bf16[1,1024,1,128]{3,1,2,0:T(8,128)(2,1)}, u32[]{:S(2)}) copy-start(bf16[1,1024,1,128]{3,1,2,0:T(8,128)(2,1)} %param.13) | copy-start | bytes 786436
  32.9 0.9 %copy-start.12 = (f32[512,384]{1,0:T(8,128)}, f32[512,384]{1,0:T(8,128)S(1)}, u32[]{:S(2)}) copy-start(f32[512,384]{1,0:T(8,128)S(1)} %local.1.mine_ref) | copy-start | bytes 2359300
  33.8 0.7 copy-start.10
  36.8 21.9 %all-to-all-start.1 = ((bf16[64,16,128]{2,1,0:T(8,128)(2,1)}), bf16[64,16,128]{2,1,0:T(8,128)(2,1)S(1)}, u32[]{:S(2)}, u32[]{:S(2)}) async-start(bf16[64,16,128]{2,1,0:T(8,128)(2,1)} %bitcast.11), calls=%async_computation.1 | async-start | bytes 524288 | tf_op jit(solution)/shard_map/all_to_all | solution.py:304
  47.2 2.1 %copy-start.13 = (bf16[128,1024]{1,0:T(8,128)(2,1)}, bf16[128,1024]{1,0:T(8,128)(2,1)S(1)}, u32[]{:S(2)}) copy-start(bf16[128,1024]{1,0:T(8,128)(2,1)S(1)} %collective-permute-done) | copy-start | bytes 786436
  47.2 19.0 %collective-permute-start.3 = (bf16[256,1024]{1,0:T(8,128)(2,1)S(1)}, bf16[256,1024]{1,0:T(8,128)(2,1)S(1)}, u32[]{:S(2)}, u32[]{:S(2)}) collective-permute-start(bf16[256,1024]{1,0:T(8,128)(2,1)S(1)} %constant_dynamic-update-slice_fusion.next_ref), channel_id=1, source_target_pairs={{0,8},{8,0},{16,24},{24,16},{32,40},{40,32},{48,56},{56,48},{64,72... | collective-permute-start | bytes 1572872 | tf_op jit(solution)/shard_map/ppermute | solution.py:266
  49.3 17.0 %collective-permute-start.2 = (bf16[256,1024]{1,0:T(8,128)(2,1)S(1)}, bf16[256,1024]{1,0:T(8,128)(2,1)S(1)}, u32[]{:S(2)}, u32[]{:S(2)}) collective-permute-start(bf16[256,1024]{1,0:T(8,128)(2,1)S(1)} %constant_dynamic-update-slice_fusion.next_ref), channel_id=1, source_target_pairs={{0,1},{1,2},{2,3},{3,4},{4,5},{5,6},{6,7},{7,0},{8,15},{9,8},{10,9... | collective-permute-start | bytes 1572872 | tf_op jit(solution)/shard_map/ppermute | solution.py:263
  52.7 13.6 %collective-permute-start.4 = (bf16[128,1024]{1,0:T(8,128)(2,1)}, bf16[128,1024]{1,0:T(8,128)(2,1)S(1)}, u32[]{:S(2)}, u32[]{:S(2)}) collective-permute-start(bf16[128,1024]{1,0:T(8,128)(2,1)} %copy-done.13), channel_id=1, source_target_pairs={{0,9},{1,10},{2,11},{3,12},{4,13},{5,14},{6,15},{7,8},{8,7},{9,0},... | collective-permute-start | bytes 786440 | tf_op jit(solution)/shard_map/ppermute | solution.py:263
  58.7 16.9 %copy-start.1 = (bf16[512,1024]{1,0:T(8,128)(2,1)S(1)}, bf16[512,1024]{1,0:T(8,128)(2,1)}, u32[]{:S(2)}) copy-start(bf16[512,1024]{1,0:T(8,128)(2,1)} %tokens_ref.5) | copy-start | bytes 3145732
  61.0 0.7 copy-start.4
  61.7 13.9 %all-to-all-start.2 = ((bf16[8,64,128]{2,1,0:T(8,128)(2,1)}), bf16[8,64,128]{2,1,0:T(8,128)(2,1)S(1)}, u32[]{:S(2)}, u32[]{:S(2)}) async-start(bf16[8,64,128]{2,1,0:T(8,128)(2,1)} %bitcast.22), calls=%async_computation.2 | async-start | bytes 262144 | tf_op jit(solution)/shard_map/all_to_all | solution.py:323

commit v9 on v8

--- a/solution.py
+++ b/solution.py
@@ -48,8 +48,8 @@
 
 
 def send_kernel(
-    capacity, cands, chunks, tokens_ref, w_ref, slot_ref, session_ref, length_ref, me_ref, sent_ref, info_ref,
-    held, weight, queries, placed, info, sems, w_sem, out_sems,
+    capacity, cands, chunks, tokens_ref, w_ref, slot_ref, session_ref, sent_ref,
+    held, weight, queries, placed, sems, w_sem, out_sems,
 ):
     rows = tokens_ref.shape[0]
     head_dim = weight.shape[1]
@@ -66,11 +66,7 @@
     fetch_w.start()
     for fetch in fetches[1:]:
         fetch.start()
-    own = slot_ref[...] == me_ref[0]
-    length = jnp.sum(jnp.where(own, length_ref[...].astype(f32), 0.0), 1, keepdims=True)
-    info[...] = jnp.broadcast_to(length, info.shape)
-    stores = [pltpu.make_async_copy(info, info_ref, out_sems.at[chunks])]
-    stores[0].start()
+    stores = []
     first = first_rows(slot_ref, session_ref, capacity, cands)
     requests = first.shape[1]
     spread = iota((requests, rows), 1) // cands == iota((requests, rows), 0)
@@ -95,7 +91,7 @@
 
 
 def local_kernel(
-    capacity, cands, tokens_ref, w_ref, slot_ref, session_ref, count_ref, length_ref, result
+    capacity, cands, tokens_ref, w_ref, slot_ref, session_ref, count_ref, length_ref, me_ref, mine_ref, info_ref, result, sem
 ):
     rows = tokens_ref.shape[0]
     head_dim = result.shape[1] // 3
@@ -119,6 +115,12 @@
     result[:, head_dim : 2 * head_dim] = jnp.where(alive, gate, 0.0)
     place = per_row(first_rows(slot_ref, session_ref, capacity, cands)) + within
     result[:, 2 * head_dim :] = jnp.broadcast_to(place, (rows, head_dim))
+    store = pltpu.make_async_copy(result, mine_ref, sem)
+    store.start()
+    own = slot_ref[...] == me_ref[0]
+    held = jnp.sum(jnp.where(own, length_ref[...].astype(f32), 0.0), 1, keepdims=True)
+    info_ref[...] = jnp.broadcast_to(held, info_ref.shape)
+    store.wait()
 
 
 def history_kernel(block, info_ref, query_ref, keys_ref, values_ref, out_ref, result, sems):
@@ -234,24 +236,23 @@
     counts = cand_count.reshape(1, -1)
     chunks = 4
 
-    sent, info = pl.pallas_call(
+    sent = pl.pallas_call(
         functools.partial(send_kernel, capacity, cands, chunks),
-        in_specs=[HBM, HBM, VMEM, VMEM, VMEM, SMEM],
-        out_specs=[HBM, HBM],
-        out_shape=[jax.ShapeDtypeStruct((slot_rows, head_dim), bf16), jax.ShapeDtypeStruct((8, 128), f32)],
+        in_specs=[HBM, HBM, VMEM, VMEM],
+        out_specs=HBM,
+        out_shape=jax.ShapeDtypeStruct((slot_rows, head_dim), bf16),
         scratch_shapes=[
             pltpu.VMEM((rows, model_width), bf16),
             pltpu.VMEM((model_width, head_dim), bf16),
             pltpu.VMEM((rows, head_dim), bf16),
             pltpu.VMEM((slot_rows, head_dim), bf16),
-            pltpu.VMEM((8, 128), f32),
             pltpu.SemaphoreType.DMA((chunks,)),
             pltpu.SemaphoreType.DMA,
-            pltpu.SemaphoreType.DMA((chunks + 1,)),
+            pltpu.SemaphoreType.DMA((chunks,)),
         ],
         compiler_params=params,
         name="send",
-    )(tokens, w_flat, slots, named, lengths, my_index)
+    )(tokens, w_flat, slots, named)
     got = lax.all_to_all(
         sent.reshape(replicas, capacity * cands, head_dim), "replica", split_axis=0, concat_axis=0, tiled=True
     )
@@ -268,15 +269,16 @@
     w_own = after(w_out.reshape(head_dim, model_width), sent)
     next_one = passed(w_own, 1)
     next_three = passed(w_own, 3)
-    mine = pl.pallas_call(
+    mine, info = pl.pallas_call(
         functools.partial(local_kernel, capacity, cands),
-        in_specs=[VMEM] * 6,
-        out_specs=VMEM,
-        out_shape=jax.ShapeDtypeStruct((rows, 3 * head_dim), f32),
+        in_specs=[VMEM] * 6 + [SMEM],
+        out_specs=[HBM, VMEM],
+        out_shape=[jax.ShapeDtypeStruct((rows, 3 * head_dim), f32), jax.ShapeDtypeStruct((8, 128), f32)],
+        scratch_shapes=[pltpu.VMEM((rows, 3 * head_dim), f32), pltpu.SemaphoreType.DMA],
         compiler_params=roomy,
         cost_estimate=pl.CostEstimate(flops=1 << 30, bytes_accessed=16 << 20, transcendentals=1 << 18),
         name="local",
-    )(tokens, w_flat, slots, after(named, sent), counts, lengths)
+    )(tokens, w_flat, slots, after(named, sent), counts, lengths, my_index)
     block = min(256, slot_rows)
     answers = pl.pallas_call(
         functools.partial(history_kernel, block),
@@ -291,7 +293,7 @@
         cost_estimate=pl.CostEstimate(flops=1 << 30, bytes_accessed=64 << 20, transcendentals=slot_rows * history),
         name="history",
     )(
-        after(info, mine),
+        info,
         got.reshape(slot_rows, head_dim),
         cache_keys.reshape(history, head_dim),
         cache_values.reshape(history, head_dim),

time: 77.6 us -> 77.5 us (level)
    unnamed x29 -> x27, local copies, waits for them, and re-layouts: 4.7 us -> 4.67 us
where the time goes in v9:
time: 77.5 us; the launch traced here: 76.9 us
  starting transfers between devices  46.8 us (60%)
  waiting for transfers between devices  13.2 us (17%)
  Pallas kernels  11.9 us (15%)
  local copies, waits for them, and re-layouts  4.69 us (6%)
    ppermute x4, starting transfers between devices, passed(): return lax.ppermute(piece, ('replica', 'tensor'), pairs)  18.9 us
    all_to_all x1, starting transfers between devices, on_device(): lax.all_to_all(sent.reshape(replicas, capacity * cands, head_dim), 'repli...  10.9 us
    all_to_all x1, starting transfers between devices, on_device(): lax.all_to_all(answers.reshape(replicas, capacity * cands, head_dim), 're...  10.3 us
    all_to_all x1, waiting for transfers between devices, on_device(): lax.all_to_all(gated.reshape(groups, share, head_dim), 'tensor', split_ax...  9.34 us
    unnamed x27, local copies, waits for them, and re-layouts  4.67 us
    all_to_all x1, starting transfers between devices, on_device(): lax.all_to_all(gated.reshape(groups, share, head_dim), 'tensor', split_ax...  4.57 us
    pallas_call x1, Pallas kernels, on_device(): pl.pallas_call(functools.partial(send_kernel, capacity, cands, chunks), i...  4.45 us
    all_to_all x1, waiting for transfers between devices, on_device(): lax.all_to_all(answers.reshape(replicas, capacity * cands, head_dim), 're...  3.85 us
  transfers between devices with their start and end apart: 8, of which 2 were waited for; matrix products, arithmetic and copies ran while one was open for 0% of the time, Pallas kernels for 8%

profile of v9, /device:TPU:6, one launch (start us, length us, event | category | flops | bytes accessed | tf_op | source)
XLA Modules:
  0.0 76.9 jit_solution(4461059329691919062)
XLA Ops:
  0.0 4.4 %send.1 = bf16[1024,128]{1,0:T(8,128)(2,1)} custom-call(bf16[512,1024]{1,0:T(8,128)(2,1)} %tokens_ref.5, bf16[1024,512]{1,0:T(8,128)(2,1)} %bitcast.15, s32[1,64]{1,0:T(1,128)} %bitcast.23, s32[1,64]{1,0:T(1,128)} %bitcast.25), custom_call_target="tpu_custom_call" | custom-call | tf_op jit(solution)/shard_map/send/pallas_call | solution.py:239
  4.5 0.0 copy-start.3
  4.5 0.0 copy-start.10
  4.5 10.9 %all-to-all-start = ((bf16[64,16,128]{2,1,0:T(8,128)(2,1)}), bf16[64,16,128]{2,1,0:T(8,128)(2,1)S(1)}, u32[]{:S(2)}, u32[]{:S(2)}) async-start(bf16[64,16,128]{2,1,0:T(8,128)(2,1)} %bitcast.31), calls=%async_computation | async-start | bytes 524288 | tf_op jit(solution)/shard_map/all_to_all | solution.py:256
  15.4 0.0 copy-done.3
  15.4 7.9 %collective-permute-start.1 = (bf16[128,1024]{1,0:T(8,128)(2,1)S(1)}, bf16[128,1024]{1,0:T(8,128)(2,1)S(1)}, u32[]{:S(2)}, u32[]{:S(2)}) collective-permute-start(bf16[128,1024]{1,0:T(8,128)(2,1)S(1)} %bitcast.17), channel_id=1, source_target_pairs={{0,3},{1,4},{2,5},{3,6},{4,7},{5,0},{6,1},{7,2},{8,13},{9,14},{10,... | collective-permute-start | bytes 786440 | tf_op jit(solution)/shard_map/ppermute | solution.py:264
  23.3 5.5 %collective-permute-start = (bf16[128,1024]{1,0:T(8,128)(2,1)S(1)}, bf16[128,1024]{1,0:T(8,128)(2,1)S(1)}, u32[]{:S(2)}, u32[]{:S(2)}) collective-permute-start(bf16[128,1024]{1,0:T(8,128)(2,1)S(1)} %bitcast.18), channel_id=1, source_target_pairs={{0,1},{1,2},{2,3},{3,4},{4,5},{5,6},{6,7},{7,0},{8,15},{9,8},{10,9... | collective-permute-start | bytes 786440 | tf_op jit(solution)/shard_map/ppermute | solution.py:264
  28.9 0.0 copy-start.5
  28.9 0.0 copy-start.6
  28.9 0.0 copy-start.9
  28.9 0.0 copy-done.10
  28.9 0.6 copy-done.5
  29.5 0.0 copy-done.6
  29.5 0.0 copy-done.9
  29.5 0.0 copy-start
  29.5 1.2 %copy-done = bf16[512,1024]{1,0:T(8,128)(2,1)S(1)} copy-done((bf16[512,1024]{1,0:T(8,128)(2,1)S(1)}, bf16[512,1024]{1,0:T(8,128)(2,1)}, u32[]{:S(2)}) %copy-start) | copy-done | bytes 1048600
  30.8 0.0 copy-start.2
  30.8 1.2 %copy-done.2 = bf16[1024,1,512]{2,0,1:T(8,128)(2,1)S(1)} copy-done((bf16[1024,1,512]{2,0,1:T(8,128)(2,1)S(1)}, bf16[1024,1,512]{2,0,1:T(8,128)(2,1)}, u32[]{:S(2)}) %copy-start.2) | copy-done | bytes 1048600
  32.0 0.0 copy-start.7
  32.0 0.0 copy-start.8
  32.0 1.5 %local.1 = (f32[512,384]{1,0:T(8,128)S(1)}, f32[8,128]{1,0:T(8,128)S(1)}) custom-call(bf16[512,1024]{1,0:T(8,128)(2,1)S(1)} %copy-done, bf16[1024,512]{1,0:T(8,128)(2,1)S(1)} %bitcast.16, s32[1,64]{1,0:T(1,128)S(1)} %bitcast.24, s32[1,64]{1,0:T(1,128)S(1)} %bitcast.26, s32[1,64]{1,0:T(1,128)S(1)} %bitcast.29, s32[1,64]{1,0:T(1,128)S(1)} %bitcast.30, ...), custom_call_target="tpu_custom_call" | custom-call | flops 1073741824 | bytes 16777216 | tf_op jit(solution)/shard_map/local/pallas_call | solution.py:272
  33.5 0.0 copy-start.11
  33.6 0.9 %copy-done.11 = f32[512,384]{1,0:T(8,128)} copy-done((f32[512,384]{1,0:T(8,128)}, f32[512,384]{1,0:T(8,128)S(1)}, u32[]{:S(2)}) %copy-start.11) | copy-done | bytes 786456
  34.4 0.0 all-to-all-done
  34.4 0.0 copy-done.7
  34.4 0.0 copy-done.8
  34.4 2.3 %history.1 = bf16[1024,128]{1,0:T(8,128)(2,1)} custom-call(f32[8,128]{1,0:T(8,128)S(1)} %get-tuple-element.12.info_ref, bf16[1024,128]{1,0:T(8,128)(2,1)S(1)} %bitcast.21, bf16[1024,128]{1,0:T(8,128)(2,1)S(1)} %bitcast.27, bf16[1024,128]{1,0:T(8,128)(2,1)S(1)} %bitcast.28), custom_call_target="tpu_custom_call" | custom-call | flops 1073741824 | bytes 67108864 | tf_op jit(solution)/shard_map/history/pallas_call | solution.py:283
  36.7 10.3 %all-to-all-start.1 = ((bf16[64,16,128]{2,1,0:T(8,128)(2,1)}), bf16[64,16,128]{2,1,0:T(8,128)(2,1)S(1)}, u32[]{:S(2)}, u32[]{:S(2)}) async-start(bf16[64,16,128]{2,1,0:T(8,128)(2,1)} %bitcast.11), calls=%async_computation.1 | async-start | bytes 524288 | tf_op jit(solution)/shard_map/all_to_all | solution.py:306
  47.1 0.0 collective-permute-done.1
  47.1 0.0 collective-permute-done
  47.1 0.0 copy-start.12
  47.2 2.1 %collective-permute-start.3 = (bf16[256,1024]{1,0:T(8,128)(2,1)S(1)}, bf16[256,1024]{1,0:T(8,128)(2,1)S(1)}, u32[]{:S(2)}, u32[]{:S(2)}) collective-permute-start(bf16[256,1024]{1,0:T(8,128)(2,1)S(1)} %constant_dynamic-update-slice_fusion.next_ref), channel_id=1, source_target_pairs={{0,8},{8,0},{16,24},{24,16},{32,40},{40,32},{48,56},{56,48},{64,72... | collective-permute-start | bytes 1572872 | tf_op jit(solution)/shard_map/ppermute | solution.py:267
  49.2 0.0 copy-done.12
  49.2 3.4 %collective-permute-start.2 = (bf16[256,1024]{1,0:T(8,128)(2,1)S(1)}, bf16[256,1024]{1,0:T(8,128)(2,1)S(1)}, u32[]{:S(2)}, u32[]{:S(2)}) collective-permute-start(bf16[256,1024]{1,0:T(8,128)(2,1)S(1)} %constant_dynamic-update-slice_fusion.next_ref), channel_id=1, source_target_pairs={{0,1},{1,2},{2,3},{3,4},{4,5},{5,6},{6,7},{7,0},{8,15},{9,8},{10,9... | collective-permute-start | bytes 1572872 | tf_op jit(solution)/shard_map/ppermute | solution.py:264
  52.6 2.1 %collective-permute-start.4 = (bf16[128,1024]{1,0:T(8,128)(2,1)}, bf16[128,1024]{1,0:T(8,128)(2,1)S(1)}, u32[]{:S(2)}, u32[]{:S(2)}) collective-permute-start(bf16[128,1024]{1,0:T(8,128)(2,1)} %copy-done.12), channel_id=1, source_target_pairs={{0,9},{1,10},{2,11},{3,12},{4,13},{5,14},{6,15},{7,8},{8,7},{9,0},... | collective-permute-start | bytes 786440 | tf_op jit(solution)/shard_map/ppermute | solution.py:264
  54.8 3.9 %all-to-all-done.1 = bf16[64,16,128]{2,1,0:T(8,128)(2,1)S(1)} async-done(((bf16[64,16,128]{2,1,0:T(8,128)(2,1)}), bf16[64,16,128]{2,1,0:T(8,128)(2,1)S(1)}, u32[]{:S(2)}, u32[]{:S(2)}) %all-to-all-start.1) | async-done | bytes 262176 | tf_op jit(solution)/shard_map/all_to_all | solution.py:306
  58.6 0.0 copy-start.1
  58.6 2.3 %gate.1 = bf16[512,128]{1,0:T(8,128)(2,1)S(1)} custom-call(bf16[1024,128]{1,0:T(8,128)(2,1)S(1)} %bitcast.20, f32[512,384]{1,0:T(8,128)} %copy-done.11), custom_call_target="tpu_custom_call" | custom-call | flops 1073741824 | bytes 67108864 | tf_op jit(solution)/shard_map/gate/pallas_call | solution.py:309
  61.0 0.0 copy-start.4
  61.0 0.6 copy-done.4
  61.6 4.6 %all-to-all-start.2 = ((bf16[8,64,128]{2,1,0:T(8,128)(2,1)}), bf16[8,64,128]{2,1,0:T(8,128)(2,1)S(1)}, u32[]{:S(2)}, u32[]{:S(2)}) async-start(bf16[8,64,128]{2,1,0:T(8,128)(2,1)} %bitcast.22), calls=%async_computation.2 | async-start | bytes 262144 | tf_op jit(solution)/shard_map/all_to_all | solution.py:325
  66.2 0.0 collective-permute-done.4.two_ref
  66.2 0.0 collective-permute-done.3.other_ref
  66.2 0.0 collective-permute-done.2.last_ref
  66.2 9.3 %all-to-all-done.2.gated_ref = bf16[8,64,128]{2,1,0:T(8,128)(2,1)S(1)} async-done(((bf16[8,64,128]{2,1,0:T(8,128)(2,1)}), bf16[8,64,128]{2,1,0:T(8,128)(2,1)S(1)}, u32[]{:S(2)}, u32[]{:S(2)}) %all-to-all-start.2) | async-done | bytes 131104 | tf_op jit(solution)/shard_map/all_to_all | solution.py:325
  75.5 0.0 copy-done.1
  75.6 1.3 %output.1 = bf16[64,1024]{1,0:T(8,128)(2,1)} custom-call(s32[1]{0:T(128)} %bitcast.group_ref, s32[1]{0:T(128)} %bitcast.1.me_ref, bf16[512,1024]{1,0:T(8,128)(2,1)S(1)} %copy-done.1, bf16[8,64,128]{2,1,0:T(8,128)(2,1)S(1)} %all-to-all-done.2.gated_ref, bf16[128,1024]{1,0:T(8,128)(2,1)S(1)} %bitcast.19, ...), custom_call_target="tpu_custom_call" | custom-call | tf_op jit(solution)/shard_map/output/pallas_call | solution.py:328
  (2 shorter events, 0.0 us)
Async XLA Ops:
  4.5 11.0 %copy-start.3 = (bf16[1,128,1024]{2,1,0:T(8,128)(2,1)S(1)}, bf16[1,128,1024]{2,1,0:T(8,128)(2,1)}, u32[]{:S(2)}) copy-start(bf16[1,128,1024]{2,1,0:T(8,128)(2,1)} %param.11) | copy-start | bytes 786436
  4.5 24.4 %copy-start.10 = (s32[64]{0:T(128)S(1)}, s32[64]{0:T(128)}, u32[]{:S(2)}) copy-start(s32[64]{0:T(128)} %param.17) | copy-start | bytes 772
  4.5 30.0 %all-to-all-start = ((bf16[64,16,128]{2,1,0:T(8,128)(2,1)}), bf16[64,16,128]{2,1,0:T(8,128)(2,1)S(1)}, u32[]{:S(2)}, u32[]{:S(2)}) async-start(bf16[64,16,128]{2,1,0:T(8,128)(2,1)} %bitcast.31), calls=%async_computation | async-start | bytes 524288 | tf_op jit(solution)/shard_map/all_to_all | solution.py:256
  15.4 31.6 %collective-permute-start.1 = (bf16[128,1024]{1,0:T(8,128)(2,1)S(1)}, bf16[128,1024]{1,0:T(8,128)(2,1)S(1)}, u32[]{:S(2)}, u32[]{:S(2)}) collective-permute-start(bf16[128,1024]{1,0:T(8,128)(2,1)S(1)} %bitcast.17), channel_id=1, source_target_pairs={{0,3},{1,4},{2,5},{3,6},{4,7},{5,0},{6,1},{7,2},{8,13},{9,14},{10,... | collective-permute-start | bytes 786440 | tf_op jit(solution)/shard_map/ppermute | solution.py:264
  23.3 23.7 %collective-permute-start = (bf16[128,1024]{1,0:T(8,128)(2,1)S(1)}, bf16[128,1024]{1,0:T(8,128)(2,1)S(1)}, u32[]{:S(2)}, u32[]{:S(2)}) collective-permute-start(bf16[128,1024]{1,0:T(8,128)(2,1)S(1)} %bitcast.18), channel_id=1, source_target_pairs={{0,1},{1,2},{2,3},{3,4},{4,5},{5,6},{6,7},{7,0},{8,15},{9,8},{10,9... | collective-permute-start | bytes 786440 | tf_op jit(solution)/shard_map/ppermute | solution.py:264
  28.9 0.7 copy-start.5
  28.9 0.7 copy-start.6
  28.9 0.7 copy-start.9
  29.5 1.2 %copy-start = (bf16[512,1024]{1,0:T(8,128)(2,1)S(1)}, bf16[512,1024]{1,0:T(8,128)(2,1)}, u32[]{:S(2)}) copy-start(bf16[512,1024]{1,0:T(8,128)(2,1)} %tokens_ref.5) | copy-start | bytes 3145732
  30.8 1.2 %copy-start.2 = (bf16[1024,1,512]{2,0,1:T(8,128)(2,1)S(1)}, bf16[1024,1,512]{2,0,1:T(8,128)(2,1)}, u32[]{:S(2)}) copy-start(bf16[1024,1,512]{2,0,1:T(8,128)(2,1)} %param.10) | copy-start | bytes 3145732
  32.0 2.4 %copy-start.7 = (bf16[1,1024,1,128]{3,1,2,0:T(8,128)(2,1)S(1)}, bf16[1,1024,1,128]{3,1,2,0:T(8,128)(2,1)}, u32[]{:S(2)}) copy-start(bf16[1,1024,1,128]{3,1,2,0:T(8,128)(2,1)} %param.12) | copy-start | bytes 786436
  32.0 2.4 %copy-start.8 = (bf16[1,1024,1,128]{3,1,2,0:T(8,128)(2,1)S(1)}, bf16[1,1024,1,128]{3,1,2,0:T(8,128)(2,1)}, u32[]{:S(2)}) copy-start(bf16[1,1024,1,128]{3,1,2,0:T(8,128)(2,1)} %param.13) | copy-start | bytes 786436
  33.5 0.9 %copy-start.11 = (f32[512,384]{1,0:T(8,128)}, f32[512,384]{1,0:T(8,128)S(1)}, u32[]{:S(2)}) copy-start(f32[512,384]{1,0:T(8,128)S(1)} %get-tuple-element.13.mine_ref) | copy-start | bytes 2359300
  36.7 21.9 %all-to-all-start.1 = ((bf16[64,16,128]{2,1,0:T(8,128)(2,1)}), bf16[64,16,128]{2,1,0:T(8,128)(2,1)S(1)}, u32[]{:S(2)}, u32[]{:S(2)}) async-start(bf16[64,16,128]{2,1,0:T(8,128)(2,1)} %bitcast.11), calls=%async_computation.1 | async-start | bytes 524288 | tf_op jit(solution)/shard_map/all_to_all | solution.py:306
  47.1 2.1 %copy-start.12 = (bf16[128,1024]{1,0:T(8,128)(2,1)}, bf16[128,1024]{1,0:T(8,128)(2,1)S(1)}, u32[]{:S(2)}) copy-start(bf16[128,1024]{1,0:T(8,128)(2,1)S(1)} %collective-permute-done) | copy-start | bytes 786436
  47.2 19.0 %collective-permute-start.3 = (bf16[256,1024]{1,0:T(8,128)(2,1)S(1)}, bf16[256,1024]{1,0:T(8,128)(2,1)S(1)}, u32[]{:S(2)}, u32[]{:S(2)}) collective-permute-start(bf16[256,1024]{1,0:T(8,128)(2,1)S(1)} %constant_dynamic-update-slice_fusion.next_ref), channel_id=1, source_target_pairs={{0,8},{8,0},{16,24},{24,16},{32,40},{40,32},{48,56},{56,48},{64,72... | collective-permute-start | bytes 1572872 | tf_op jit(solution)/shard_map/ppermute | solution.py:267
  49.2 17.0 %collective-permute-start.2 = (bf16[256,1024]{1,0:T(8,128)(2,1)S(1)}, bf16[256,1024]{1,0:T(8,128)(2,1)S(1)}, u32[]{:S(2)}, u32[]{:S(2)}) collective-permute-start(bf16[256,1024]{1,0:T(8,128)(2,1)S(1)} %constant_dynamic-update-slice_fusion.next_ref), channel_id=1, source_target_pairs={{0,1},{1,2},{2,3},{3,4},{4,5},{5,6},{6,7},{7,0},{8,15},{9,8},{10,9... | collective-permute-start | bytes 1572872 | tf_op jit(solution)/shard_map/ppermute | solution.py:264
  52.6 13.5 %collective-permute-start.4 = (bf16[128,1024]{1,0:T(8,128)(2,1)}, bf16[128,1024]{1,0:T(8,128)(2,1)S(1)}, u32[]{:S(2)}, u32[]{:S(2)}) collective-permute-start(bf16[128,1024]{1,0:T(8,128)(2,1)} %copy-done.12), channel_id=1, source_target_pairs={{0,9},{1,10},{2,11},{3,12},{4,13},{5,14},{6,15},{7,8},{8,7},{9,0},... | collective-permute-start | bytes 786440 | tf_op jit(solution)/shard_map/ppermute | solution.py:264
  58.6 16.9 %copy-start.1 = (bf16[512,1024]{1,0:T(8,128)(2,1)S(1)}, bf16[512,1024]{1,0:T(8,128)(2,1)}, u32[]{:S(2)}) copy-start(bf16[512,1024]{1,0:T(8,128)(2,1)} %tokens_ref.5) | copy-start | bytes 3145732
  61.0 0.7 copy-start.4
  61.6 13.9 %all-to-all-start.2 = ((bf16[8,64,128]{2,1,0:T(8,128)(2,1)}), bf16[8,64,128]{2,1,0:T(8,128)(2,1)S(1)}, u32[]{:S(2)}, u32[]{:S(2)}) async-start(bf16[8,64,128]{2,1,0:T(8,128)(2,1)} %bitcast.22), calls=%async_computation.2 | async-start | bytes 262144 | tf_op jit(solution)/shard_map/all_to_all | solution.py:325

commit v10 on v9

--- a/solution.py
+++ b/solution.py
@@ -49,7 +49,7 @@
 
 def send_kernel(
     capacity, cands, chunks, tokens_ref, w_ref, slot_ref, session_ref, sent_ref,
-    held, weight, queries, placed, sems, w_sem, out_sems,
+    held, weight, queries, placed, chosen, sems, w_sem, out_sems,
 ):
     rows = tokens_ref.shape[0]
     head_dim = weight.shape[1]
@@ -72,6 +72,7 @@
     spread = iota((requests, rows), 1) // cands == iota((requests, rows), 0)
     place = jnp.sum(jnp.where(spread, to_column(first), 0.0), 0, keepdims=True).astype(jnp.int32)
     place = place + iota((1, rows), 1) % cands
+    chosen[...] = jnp.where(iota((slot_rows, rows), 0) == place, 1.0, 0.0).astype(bf16)
     for n, fetch in enumerate(fetches):
         part = pl.ds(n * chunk, chunk)
         fetch.wait()
@@ -82,8 +83,7 @@
     block = slot_rows // chunks
     for n in range(chunks):
         part = pl.ds(n * block, block)
-        chosen = jnp.where(iota((block, rows), 0) + n * block == place, 1.0, 0.0).astype(bf16)
-        placed[part, :] = jnp.dot(chosen, queries[...], preferred_element_type=f32).astype(bf16)
+        placed[part, :] = jnp.dot(chosen[part, :], queries[...], preferred_element_type=f32).astype(bf16)
         stores.append(pltpu.make_async_copy(placed.at[part, :], sent_ref.at[part, :], out_sems.at[n]))
         stores[-1].start()
     for store in stores:
@@ -91,36 +91,55 @@
 
 
 def local_kernel(
-    capacity, cands, tokens_ref, w_ref, slot_ref, session_ref, count_ref, length_ref, me_ref, mine_ref, info_ref, result, sem
+    capacity, cands, chunks, tokens_ref, w_ref, slot_ref, session_ref, count_ref, length_ref, me_ref,
+    mine_ref, info_ref, held, weight, result, sems, w_sem, out_sems,
 ):
     rows = tokens_ref.shape[0]
     head_dim = result.shape[1] // 3
-    normed = layer_norm(tokens_ref[...].astype(f32)).astype(bf16)
-    projected = silu(jnp.dot(normed, w_ref[...], preferred_element_type=f32)).astype(bf16).astype(f32)
-    gate = projected[:, :head_dim]
-    values = projected[:, head_dim : 2 * head_dim]
-    queries = projected[:, 2 * head_dim : 3 * head_dim]
-    keys = projected[:, 3 * head_dim :]
+    chunk = rows // chunks
+    fetch_w = pltpu.make_async_copy(w_ref, weight, w_sem)
+    fetches = []
+    for n in range(chunks):
+        part = pl.ds(n * chunk, chunk)
+        fetches.append(pltpu.make_async_copy(tokens_ref.at[part, :], held.at[part, :], sems.at[n]))
+    fetches[0].start()
+    fetch_w.start()
+    for fetch in fetches[1:]:
+        fetch.start()
+    own = slot_ref[...] == me_ref[0]
+    length = jnp.sum(jnp.where(own, length_ref[...].astype(f32), 0.0), 1, keepdims=True)
+    info_ref[...] = jnp.broadcast_to(length, info_ref.shape)
     lengths = lookup(length_ref[...], session_ref[...])
+    counts = count_ref[...].astype(f32)
+    first = first_rows(slot_ref, session_ref, capacity, cands)
     requests = lengths.shape[1]
-    spread = iota((rows, requests), 0) // cands == iota((rows, requests), 1)
-
-    def per_row(row):
-        return jnp.sum(jnp.where(spread, row, 0.0), 1, keepdims=True)
-
-    within = (iota((rows, 1), 0) % cands).astype(f32)
-    scores = jnp.sum(queries * keys, -1, keepdims=True) * head_dim ** (-0.5)
-    result[:, :head_dim] = silu(scores) * values / (per_row(lengths) + 1.0)
-    alive = within < per_row(count_ref[...].astype(f32))
-    result[:, head_dim : 2 * head_dim] = jnp.where(alive, gate, 0.0)
-    place = per_row(first_rows(slot_ref, session_ref, capacity, cands)) + within
-    result[:, 2 * head_dim :] = jnp.broadcast_to(place, (rows, head_dim))
-    store = pltpu.make_async_copy(result, mine_ref, sem)
-    store.start()
-    own = slot_ref[...] == me_ref[0]
-    held = jnp.sum(jnp.where(own, length_ref[...].astype(f32), 0.0), 1, keepdims=True)
-    info_ref[...] = jnp.broadcast_to(held, info_ref.shape)
-    store.wait()
+    stores = []
+    for n, fetch in enumerate(fetches):
+        part = pl.ds(n * chunk, chunk)
+        spread = (iota((chunk, requests), 0) + n * chunk) // cands == iota((chunk, requests), 1)
+
+        def per_row(row):
+            return jnp.sum(jnp.where(spread, row, 0.0), 1, keepdims=True)
+
+        fetch.wait()
+        normed = layer_norm(held[part, :].astype(f32)).astype(bf16)
+        if n == 0:
+            fetch_w.wait()
+        projected = silu(jnp.dot(normed, weight[...], preferred_element_type=f32)).astype(bf16).astype(f32)
+        gate = projected[:, :head_dim]
+        values = projected[:, head_dim : 2 * head_dim]
+        queries = projected[:, 2 * head_dim : 3 * head_dim]
+        keys = projected[:, 3 * head_dim :]
+        within = (iota((chunk, 1), 0) % cands).astype(f32)
+        scores = jnp.sum(queries * keys, -1, keepdims=True) * head_dim ** (-0.5)
+        result[part, :head_dim] = silu(scores) * values / (per_row(lengths) + 1.0)
+        result[part, head_dim : 2 * head_dim] = jnp.where(within < per_row(counts), gate, 0.0)
+        place = per_row(first) + within
+        result[part, 2 * head_dim :] = jnp.broadcast_to(place, (chunk, head_dim))
+        stores.append(pltpu.make_async_copy(result.at[part, :], mine_ref.at[part, :], out_sems.at[n]))
+        stores[-1].start()
+    for store in stores:
+        store.wait()
 
 
 def history_kernel(block, info_ref, query_ref, keys_ref, values_ref, out_ref, result, sems):
@@ -200,6 +219,7 @@
 SMEM = pl.BlockSpec(memory_space=pltpu.SMEM)
 params = pltpu.CompilerParams(vmem_limit_bytes=63 * 1024 * 1024)
 tight = pltpu.CompilerParams(vmem_limit_bytes=54528 * 1024)
+middle = pltpu.CompilerParams(vmem_limit_bytes=53760 * 1024)
 roomy = pltpu.CompilerParams(vmem_limit_bytes=24 * 1024 * 1024)
 
 
@@ -246,6 +266,7 @@
             pltpu.VMEM((model_width, head_dim), bf16),
             pltpu.VMEM((rows, head_dim), bf16),
             pltpu.VMEM((slot_rows, head_dim), bf16),
+            pltpu.VMEM((slot_rows, rows), bf16),
             pltpu.SemaphoreType.DMA((chunks,)),
             pltpu.SemaphoreType.DMA,
             pltpu.SemaphoreType.DMA((chunks,)),
@@ -270,12 +291,19 @@
     next_one = passed(w_own, 1)
     next_three = passed(w_own, 3)
     mine, info = pl.pallas_call(
-        functools.partial(local_kernel, capacity, cands),
-        in_specs=[VMEM] * 6 + [SMEM],
+        functools.partial(local_kernel, capacity, cands, chunks),
+        in_specs=[HBM] * 2 + [VMEM] * 4 + [SMEM],
         out_specs=[HBM, VMEM],
         out_shape=[jax.ShapeDtypeStruct((rows, 3 * head_dim), f32), jax.ShapeDtypeStruct((8, 128), f32)],
-        scratch_shapes=[pltpu.VMEM((rows, 3 * head_dim), f32), pltpu.SemaphoreType.DMA],
-        compiler_params=roomy,
+        scratch_shapes=[
+            pltpu.VMEM((rows, model_width), bf16),
+            pltpu.VMEM((model_width, 4 * head_dim), bf16),
+            pltpu.VMEM((rows, 3 * head_dim), f32),
+            pltpu.SemaphoreType.DMA((chunks,)),
+            pltpu.SemaphoreType.DMA,
+            pltpu.SemaphoreType.DMA((chunks,)),
+        ],
+        compiler_params=middle,
         cost_estimate=pl.CostEstimate(flops=1 << 30, bytes_accessed=16 << 20, transcendentals=1 << 18),
         name="local",
     )(tokens, w_flat, slots, after(named, sent), counts, lengths, my_index)

time: 77.5 us -> 78.4 us (1.012)
  Pallas kernels: 11.9 us -> 15.3 us
  local copies, waits for them, and re-layouts: 4.69 us -> 2.26 us
    pallas_call x1, Pallas kernels: 1.54 us -> 4.93 us  [on_device(): pl.pallas_call(functools.partial(local_kernel, capacity, cands, chunks),...]
    unnamed x27 -> x23, local copies, waits for them, and re-layouts: 4.67 us -> 2.24 us
  transfers between devices with their start and end apart: 8 -> 8, of which waited for: 2 -> 2; matrix products, arithmetic and copies ran while one was open for 0% -> 0% of each run, Pallas kernels for 8% -> 12%
where the time goes in v10:
time: 78.4 us; the launch traced here: 77.8 us
  starting transfers between devices  46.8 us (60%)
  Pallas kernels  15.3 us (20%)
  waiting for transfers between devices  13.2 us (17%)
  local copies, waits for them, and re-layouts  2.26 us (3%)
    ppermute x4, starting transfers between devices, passed(): return lax.ppermute(piece, ('replica', 'tensor'), pairs)  18.9 us
    all_to_all x1, starting transfers between devices, on_device(): lax.all_to_all(sent.reshape(replicas, capacity * cands, head_dim), 'repli...  10.9 us
    all_to_all x1, starting transfers between devices, on_device(): lax.all_to_all(answers.reshape(replicas, capacity * cands, head_dim), 're...  10.3 us
    all_to_all x1, waiting for transfers between devices, on_device(): lax.all_to_all(gated.reshape(groups, share, head_dim), 'tensor', split_ax...  9.34 us
    pallas_call x1, Pallas kernels, on_device(): pl.pallas_call(functools.partial(local_kernel, capacity, cands, chunks),...  4.93 us
    all_to_all x1, starting transfers between devices, on_device(): lax.all_to_all(gated.reshape(groups, share, head_dim), 'tensor', split_ax...  4.57 us
    pallas_call x1, Pallas kernels, on_device(): pl.pallas_call(functools.partial(send_kernel, capacity, cands, chunks), i...  4.46 us
    all_to_all x1, waiting for transfers between devices, on_device(): lax.all_to_all(answers.reshape(replicas, capacity * cands, head_dim), 're...  3.85 us
  transfers between devices with their start and end apart: 8, of which 2 were waited for; matrix products, arithmetic and copies ran while one was open for 0% of the time, Pallas kernels for 12%

profile of v10, /device:TPU:6, one launch (start us, length us, event | category | flops | bytes accessed | tf_op | source)
XLA Modules:
  0.0 77.8 jit_solution(8682282933593336187)
XLA Ops:
  0.0 4.5 %send.1 = bf16[1024,128]{1,0:T(8,128)(2,1)} custom-call(bf16[512,1024]{1,0:T(8,128)(2,1)} %tokens_ref.5, bf16[1024,512]{1,0:T(8,128)(2,1)} %bitcast.30, s32[1,64]{1,0:T(1,128)} %bitcast.21, s32[1,64]{1,0:T(1,128)} %bitcast.23), custom_call_target="tpu_custom_call" | custom-call | tf_op jit(solution)/shard_map/send/pallas_call | solution.py:259
  4.5 0.0 copy-start.1
  4.5 0.0 copy-start.8
  4.5 10.9 %all-to-all-start = ((bf16[64,16,128]{2,1,0:T(8,128)(2,1)}), bf16[64,16,128]{2,1,0:T(8,128)(2,1)S(1)}, u32[]{:S(2)}, u32[]{:S(2)}) async-start(bf16[64,16,128]{2,1,0:T(8,128)(2,1)} %bitcast.29), calls=%async_computation | async-start | bytes 524288 | tf_op jit(solution)/shard_map/all_to_all | solution.py:277
  15.4 0.0 copy-done.1
  15.5 7.9 %collective-permute-start.1 = (bf16[128,1024]{1,0:T(8,128)(2,1)S(1)}, bf16[128,1024]{1,0:T(8,128)(2,1)S(1)}, u32[]{:S(2)}, u32[]{:S(2)}) collective-permute-start(bf16[128,1024]{1,0:T(8,128)(2,1)S(1)} %bitcast.15), channel_id=1, source_target_pairs={{0,3},{1,4},{2,5},{3,6},{4,7},{5,0},{6,1},{7,2},{8,13},{9,14},{10,... | collective-permute-start | bytes 786440 | tf_op jit(solution)/shard_map/ppermute | solution.py:285
  23.4 5.5 %collective-permute-start = (bf16[128,1024]{1,0:T(8,128)(2,1)S(1)}, bf16[128,1024]{1,0:T(8,128)(2,1)S(1)}, u32[]{:S(2)}, u32[]{:S(2)}) collective-permute-start(bf16[128,1024]{1,0:T(8,128)(2,1)S(1)} %bitcast.16), channel_id=1, source_target_pairs={{0,1},{1,2},{2,3},{3,4},{4,5},{5,6},{6,7},{7,0},{8,15},{9,8},{10,9... | collective-permute-start | bytes 786440 | tf_op jit(solution)/shard_map/ppermute | solution.py:285
  28.9 0.0 copy-start.3
  28.9 0.0 copy-start.4
  28.9 0.0 copy-start.7
  28.9 0.0 copy-done.8
  28.9 0.6 copy-done.3
  29.5 0.0 copy-done.4
  29.5 0.0 copy-done.7
  29.6 0.0 copy-start.5
  29.6 0.0 copy-start.6
  29.6 4.9 %local.1 = (f32[512,384]{1,0:T(8,128)S(1)}, f32[8,128]{1,0:T(8,128)S(1)}) custom-call(bf16[512,1024]{1,0:T(8,128)(2,1)} %tokens_ref.5, bf16[1024,512]{1,0:T(8,128)(2,1)} %bitcast.31, s32[1,64]{1,0:T(1,128)S(1)} %bitcast.22, s32[1,64]{1,0:T(1,128)S(1)} %bitcast.24, s32[1,64]{1,0:T(1,128)S(1)} %bitcast.27, s32[1,64]{1,0:T(1,128)S(1)} %bitcast.28, s32[1]{0:T(128)} %bitcast.1.me_ref), custom_call_target="tpu_custom_call" | custom-call | flops 1073741824 | bytes 16777216 | tf_op jit(solution)/shard_map/local/pallas_call | solution.py:293
  34.5 0.0 copy-start.9
  34.5 0.9 %copy-done.9 = f32[512,384]{1,0:T(8,128)} copy-done((f32[512,384]{1,0:T(8,128)}, f32[512,384]{1,0:T(8,128)S(1)}, u32[]{:S(2)}) %copy-start.9) | copy-done | bytes 786456
  35.4 0.0 all-to-all-done
  35.4 0.0 copy-done.5
  35.4 0.0 copy-done.6
  35.4 2.3 %history.1 = bf16[1024,128]{1,0:T(8,128)(2,1)} custom-call(f32[8,128]{1,0:T(8,128)S(1)} %get-tuple-element.12.info_ref, bf16[1024,128]{1,0:T(8,128)(2,1)S(1)} %bitcast.19, bf16[1024,128]{1,0:T(8,128)(2,1)S(1)} %bitcast.25, bf16[1024,128]{1,0:T(8,128)(2,1)S(1)} %bitcast.26), custom_call_target="tpu_custom_call" | custom-call | flops 1073741824 | bytes 67108864 | tf_op jit(solution)/shard_map/history/pallas_call | solution.py:311
  37.7 10.3 %all-to-all-start.1 = ((bf16[64,16,128]{2,1,0:T(8,128)(2,1)}), bf16[64,16,128]{2,1,0:T(8,128)(2,1)S(1)}, u32[]{:S(2)}, u32[]{:S(2)}) async-start(bf16[64,16,128]{2,1,0:T(8,128)(2,1)} %bitcast.11), calls=%async_computation.1 | async-start | bytes 524288 | tf_op jit(solution)/shard_map/all_to_all | solution.py:334
  48.1 0.0 collective-permute-done.1
  48.1 0.0 collective-permute-done
  48.1 0.0 copy-start.10
  48.1 2.1 %collective-permute-start.3 = (bf16[256,1024]{1,0:T(8,128)(2,1)S(1)}, bf16[256,1024]{1,0:T(8,128)(2,1)S(1)}, u32[]{:S(2)}, u32[]{:S(2)}) collective-permute-start(bf16[256,1024]{1,0:T(8,128)(2,1)S(1)} %constant_dynamic-update-slice_fusion.next_ref), channel_id=1, source_target_pairs={{0,8},{8,0},{16,24},{24,16},{32,40},{40,32},{48,56},{56,48},{64,72... | collective-permute-start | bytes 1572872 | tf_op jit(solution)/shard_map/ppermute | solution.py:288
  50.2 0.0 copy-done.10
  50.2 3.4 %collective-permute-start.2 = (bf16[256,1024]{1,0:T(8,128)(2,1)S(1)}, bf16[256,1024]{1,0:T(8,128)(2,1)S(1)}, u32[]{:S(2)}, u32[]{:S(2)}) collective-permute-start(bf16[256,1024]{1,0:T(8,128)(2,1)S(1)} %constant_dynamic-update-slice_fusion.next_ref), channel_id=1, source_target_pairs={{0,1},{1,2},{2,3},{3,4},{4,5},{5,6},{6,7},{7,0},{8,15},{9,8},{10,9... | collective-permute-start | bytes 1572872 | tf_op jit(solution)/shard_map/ppermute | solution.py:285
  53.6 2.1 %collective-permute-start.4 = (bf16[128,1024]{1,0:T(8,128)(2,1)}, bf16[128,1024]{1,0:T(8,128)(2,1)S(1)}, u32[]{:S(2)}, u32[]{:S(2)}) collective-permute-start(bf16[128,1024]{1,0:T(8,128)(2,1)} %copy-done.10), channel_id=1, source_target_pairs={{0,9},{1,10},{2,11},{3,12},{4,13},{5,14},{6,15},{7,8},{8,7},{9,0},... | collective-permute-start | bytes 786440 | tf_op jit(solution)/shard_map/ppermute | solution.py:285
  55.8 3.9 %all-to-all-done.1 = bf16[64,16,128]{2,1,0:T(8,128)(2,1)S(1)} async-done(((bf16[64,16,128]{2,1,0:T(8,128)(2,1)}), bf16[64,16,128]{2,1,0:T(8,128)(2,1)S(1)}, u32[]{:S(2)}, u32[]{:S(2)}) %all-to-all-start.1) | async-done | bytes 262176 | tf_op jit(solution)/shard_map/all_to_all | solution.py:334
  59.6 0.0 copy-start
  59.6 2.3 %gate.1 = bf16[512,128]{1,0:T(8,128)(2,1)S(1)} custom-call(bf16[1024,128]{1,0:T(8,128)(2,1)S(1)} %bitcast.18, f32[512,384]{1,0:T(8,128)} %copy-done.9), custom_call_target="tpu_custom_call" | custom-call | flops 1073741824 | bytes 67108864 | tf_op jit(solution)/shard_map/gate/pallas_call | solution.py:337
  61.9 0.0 copy-start.2
  61.9 0.6 copy-done.2
  62.6 4.6 %all-to-all-start.2 = ((bf16[8,64,128]{2,1,0:T(8,128)(2,1)}), bf16[8,64,128]{2,1,0:T(8,128)(2,1)S(1)}, u32[]{:S(2)}, u32[]{:S(2)}) async-start(bf16[8,64,128]{2,1,0:T(8,128)(2,1)} %bitcast.20), calls=%async_computation.2 | async-start | bytes 262144 | tf_op jit(solution)/shard_map/all_to_all | solution.py:353
  67.2 0.0 collective-permute-done.4.two_ref
  67.2 0.0 collective-permute-done.3.other_ref
  67.2 0.0 collective-permute-done.2.last_ref
  67.2 9.3 %all-to-all-done.2.gated_ref = bf16[8,64,128]{2,1,0:T(8,128)(2,1)S(1)} async-done(((bf16[8,64,128]{2,1,0:T(8,128)(2,1)}), bf16[8,64,128]{2,1,0:T(8,128)(2,1)S(1)}, u32[]{:S(2)}, u32[]{:S(2)}) %all-to-all-start.2) | async-done | bytes 131104 | tf_op jit(solution)/shard_map/all_to_all | solution.py:353
  76.5 0.0 copy-done
  76.5 1.3 %output.1 = bf16[64,1024]{1,0:T(8,128)(2,1)} custom-call(s32[1]{0:T(128)} %bitcast.group_ref, s32[1]{0:T(128)} %bitcast.1.me_ref, bf16[512,1024]{1,0:T(8,128)(2,1)S(1)} %copy-done, bf16[8,64,128]{2,1,0:T(8,128)(2,1)S(1)} %all-to-all-done.2.gated_ref, bf16[128,1024]{1,0:T(8,128)(2,1)S(1)} %bitcast.17, ...), custom_call_target="tpu_custom_call" | custom-call | tf_op jit(solution)/shard_map/output/pallas_call | solution.py:356
  (2 shorter events, 0.0 us)
Async XLA Ops:
  4.5 11.0 %copy-start.1 = (bf16[1,128,1024]{2,1,0:T(8,128)(2,1)S(1)}, bf16[1,128,1024]{2,1,0:T(8,128)(2,1)}, u32[]{:S(2)}) copy-start(bf16[1,128,1024]{2,1,0:T(8,128)(2,1)} %param.11) | copy-start | bytes 786436
  4.5 24.4 %copy-start.8 = (s32[64]{0:T(128)S(1)}, s32[64]{0:T(128)}, u32[]{:S(2)}) copy-start(s32[64]{0:T(128)} %param.17) | copy-start | bytes 772
  4.5 30.9 %all-to-all-start = ((bf16[64,16,128]{2,1,0:T(8,128)(2,1)}), bf16[64,16,128]{2,1,0:T(8,128)(2,1)S(1)}, u32[]{:S(2)}, u32[]{:S(2)}) async-start(bf16[64,16,128]{2,1,0:T(8,128)(2,1)} %bitcast.29), calls=%async_computation | async-start | bytes 524288 | tf_op jit(solution)/shard_map/all_to_all | solution.py:277
  15.5 32.6 %collective-permute-start.1 = (bf16[128,1024]{1,0:T(8,128)(2,1)S(1)}, bf16[128,1024]{1,0:T(8,128)(2,1)S(1)}, u32[]{:S(2)}, u32[]{:S(2)}) collective-permute-start(bf16[128,1024]{1,0:T(8,128)(2,1)S(1)} %bitcast.15), channel_id=1, source_target_pairs={{0,3},{1,4},{2,5},{3,6},{4,7},{5,0},{6,1},{7,2},{8,13},{9,14},{10,... | collective-permute-start | bytes 786440 | tf_op jit(solution)/shard_map/ppermute | solution.py:285
  23.4 24.7 %collective-permute-start = (bf16[128,1024]{1,0:T(8,128)(2,1)S(1)}, bf16[128,1024]{1,0:T(8,128)(2,1)S(1)}, u32[]{:S(2)}, u32[]{:S(2)}) collective-permute-start(bf16[128,1024]{1,0:T(8,128)(2,1)S(1)} %bitcast.16), channel_id=1, source_target_pairs={{0,1},{1,2},{2,3},{3,4},{4,5},{5,6},{6,7},{7,0},{8,15},{9,8},{10,9... | collective-permute-start | bytes 786440 | tf_op jit(solution)/shard_map/ppermute | solution.py:285
  28.9 0.7 copy-start.3
  28.9 0.7 copy-start.4
  28.9 0.7 copy-start.7
  29.6 5.8 %copy-start.5 = (bf16[1,1024,1,128]{3,1,2,0:T(8,128)(2,1)S(1)}, bf16[1,1024,1,128]{3,1,2,0:T(8,128)(2,1)}, u32[]{:S(2)}) copy-start(bf16[1,1024,1,128]{3,1,2,0:T(8,128)(2,1)} %param.12) | copy-start | bytes 786436
  29.6 5.8 %copy-start.6 = (bf16[1,1024,1,128]{3,1,2,0:T(8,128)(2,1)S(1)}, bf16[1,1024,1,128]{3,1,2,0:T(8,128)(2,1)}, u32[]{:S(2)}) copy-start(bf16[1,1024,1,128]{3,1,2,0:T(8,128)(2,1)} %param.13) | copy-start | bytes 786436
  34.5 0.9 %copy-start.9 = (f32[512,384]{1,0:T(8,128)}, f32[512,384]{1,0:T(8,128)S(1)}, u32[]{:S(2)}) copy-start(f32[512,384]{1,0:T(8,128)S(1)} %get-tuple-element.13.mine_ref) | copy-start | bytes 2359300
  37.7 21.9 %all-to-all-start.1 = ((bf16[64,16,128]{2,1,0:T(8,128)(2,1)}), bf16[64,16,128]{2,1,0:T(8,128)(2,1)S(1)}, u32[]{:S(2)}, u32[]{:S(2)}) async-start(bf16[64,16,128]{2,1,0:T(8,128)(2,1)} %bitcast.11), calls=%async_computation.1 | async-start | bytes 524288 | tf_op jit(solution)/shard_map/all_to_all | solution.py:334
  48.1 2.1 %copy-start.10 = (bf16[128,1024]{1,0:T(8,128)(2,1)}, bf16[128,1024]{1,0:T(8,128)(2,1)S(1)}, u32[]{:S(2)}) copy-start(bf16[128,1024]{1,0:T(8,128)(2,1)S(1)} %collective-permute-done) | copy-start | bytes 786436
  48.1 19.0 %collective-permute-start.3 = (bf16[256,1024]{1,0:T(8,128)(2,1)S(1)}, bf16[256,1024]{1,0:T(8,128)(2,1)S(1)}, u32[]{:S(2)}, u32[]{:S(2)}) collective-permute-start(bf16[256,1024]{1,0:T(8,128)(2,1)S(1)} %constant_dynamic-update-slice_fusion.next_ref), channel_id=1, source_target_pairs={{0,8},{8,0},{16,24},{24,16},{32,40},{40,32},{48,56},{56,48},{64,72... | collective-permute-start | bytes 1572872 | tf_op jit(solution)/shard_map/ppermute | solution.py:288
  50.2 17.0 %collective-permute-start.2 = (bf16[256,1024]{1,0:T(8,128)(2,1)S(1)}, bf16[256,1024]{1,0:T(8,128)(2,1)S(1)}, u32[]{:S(2)}, u32[]{:S(2)}) collective-permute-start(bf16[256,1024]{1,0:T(8,128)(2,1)S(1)} %constant_dynamic-update-slice_fusion.next_ref), channel_id=1, source_target_pairs={{0,1},{1,2},{2,3},{3,4},{4,5},{5,6},{6,7},{7,0},{8,15},{9,8},{10,9... | collective-permute-start | bytes 1572872 | tf_op jit(solution)/shard_map/ppermute | solution.py:285
  53.6 13.5 %collective-permute-start.4 = (bf16[128,1024]{1,0:T(8,128)(2,1)}, bf16[128,1024]{1,0:T(8,128)(2,1)S(1)}, u32[]{:S(2)}, u32[]{:S(2)}) collective-permute-start(bf16[128,1024]{1,0:T(8,128)(2,1)} %copy-done.10), channel_id=1, source_target_pairs={{0,9},{1,10},{2,11},{3,12},{4,13},{5,14},{6,15},{7,8},{8,7},{9,0},... | collective-permute-start | bytes 786440 | tf_op jit(solution)/shard_map/ppermute | solution.py:285
  59.6 16.9 %copy-start = (bf16[512,1024]{1,0:T(8,128)(2,1)S(1)}, bf16[512,1024]{1,0:T(8,128)(2,1)}, u32[]{:S(2)}) copy-start(bf16[512,1024]{1,0:T(8,128)(2,1)} %tokens_ref.5) | copy-start | bytes 3145732
  61.9 0.7 copy-start.2
  62.6 13.9 %all-to-all-start.2 = ((bf16[8,64,128]{2,1,0:T(8,128)(2,1)}), bf16[8,64,128]{2,1,0:T(8,128)(2,1)S(1)}, u32[]{:S(2)}, u32[]{:S(2)}) async-start(bf16[8,64,128]{2,1,0:T(8,128)(2,1)} %bitcast.20), calls=%async_computation.2 | async-start | bytes 262144 | tf_op jit(solution)/shard_map/all_to_all | solution.py:353

commit v11 on v9

--- a/solution.py
+++ b/solution.py
@@ -266,9 +266,6 @@
     def swapped(piece):
         return lax.ppermute(piece, "replica", [(r, r ^ 1) for r in range(replicas)])
 
-    w_own = after(w_out.reshape(head_dim, model_width), sent)
-    next_one = passed(w_own, 1)
-    next_three = passed(w_own, 3)
     mine, info = pl.pallas_call(
         functools.partial(local_kernel, capacity, cands),
         in_specs=[VMEM] * 6 + [SMEM],
@@ -279,6 +276,9 @@
         cost_estimate=pl.CostEstimate(flops=1 << 30, bytes_accessed=16 << 20, transcendentals=1 << 18),
         name="local",
     )(tokens, w_flat, slots, after(named, sent), counts, lengths, my_index)
+    w_own = after(w_out.reshape(head_dim, model_width), mine)
+    next_one = passed(w_own, 1)
+    next_three = passed(w_own, 3)
     block = min(256, slot_rows)
     answers = pl.pallas_call(
         functools.partial(history_kernel, block),

time: 77.5 us -> 77.3 us (level)
  waiting for transfers between devices: 13.2 us -> 12.3 us
    all_to_all x1, waiting for transfers between devices: 3.85 us -> 2.93 us  [on_device(): lax.all_to_all(answers.reshape(replicas, capacity * cands, head_dim), 're...]
    unnamed x27 -> x23, local copies, waits for them, and re-layouts: 4.67 us -> 4.98 us
  transfers between devices with their start and end apart: 8 -> 8, of which waited for: 2 -> 2; matrix products, arithmetic and copies ran while one was open for 0% -> 1% of each run, Pallas kernels for 8% -> 9%
where the time goes in v11:
time: 77.3 us; the launch traced here: 76.6 us
  starting transfers between devices  46.7 us (60%)
  Pallas kernels  12.4 us (16%)
  waiting for transfers between devices  12.3 us (16%)
  local copies, waits for them, and re-layouts  5 us (6%)
    ppermute x4, starting transfers between devices, passed(): return lax.ppermute(piece, ('replica', 'tensor'), pairs)  18.9 us
    all_to_all x1, starting transfers between devices, on_device(): lax.all_to_all(sent.reshape(replicas, capacity * cands, head_dim), 'repli...  10.8 us
    all_to_all x1, starting transfers between devices, on_device(): lax.all_to_all(answers.reshape(replicas, capacity * cands, head_dim), 're...  10.3 us
    all_to_all x1, waiting for transfers between devices, on_device(): lax.all_to_all(gated.reshape(groups, share, head_dim), 'tensor', split_ax...  9.34 us
    unnamed x23, local copies, waits for them, and re-layouts  4.98 us
    all_to_all x1, starting transfers between devices, on_device(): lax.all_to_all(gated.reshape(groups, share, head_dim), 'tensor', split_ax...  4.58 us
    pallas_call x1, Pallas kernels, on_device(): pl.pallas_call(functools.partial(send_kernel, capacity, cands, chunks), i...  4.45 us
    all_to_all x1, waiting for transfers between devices, on_device(): lax.all_to_all(answers.reshape(replicas, capacity * cands, head_dim), 're...  2.93 us
  transfers between devices with their start and end apart: 8, of which 2 were waited for; matrix products, arithmetic and copies ran while one was open for 1% of the time, Pallas kernels for 9%

profile of v11, /device:TPU:6, one launch (start us, length us, event | category | flops | bytes accessed | tf_op | source)
XLA Modules:
  0.0 76.6 jit_solution(828825537165505067)
XLA Ops:
  0.0 4.4 %send.1 = bf16[1024,128]{1,0:T(8,128)(2,1)} custom-call(bf16[512,1024]{1,0:T(8,128)(2,1)} %tokens_ref.5, bf16[1024,512]{1,0:T(8,128)(2,1)} %bitcast.15, s32[1,64]{1,0:T(1,128)} %bitcast.22, s32[1,64]{1,0:T(1,128)} %bitcast.24), custom_call_target="tpu_custom_call" | custom-call | tf_op jit(solution)/shard_map/send/pallas_call | solution.py:239
  4.5 0.0 copy-start.9
  4.5 10.8 %all-to-all-start = ((bf16[64,16,128]{2,1,0:T(8,128)(2,1)}), bf16[64,16,128]{2,1,0:T(8,128)(2,1)S(1)}, u32[]{:S(2)}, u32[]{:S(2)}) async-start(bf16[64,16,128]{2,1,0:T(8,128)(2,1)} %bitcast.30), calls=%async_computation | async-start | bytes 524288 | tf_op jit(solution)/shard_map/all_to_all | solution.py:256
  15.3 0.0 copy-start.4
  15.3 0.0 copy-start.5
  15.3 0.0 copy-start.8
  15.3 0.0 copy-done.9
  15.3 0.6 copy-done.4
  16.0 0.0 copy-done.5
  16.0 0.0 copy-done.8
  16.0 0.0 copy-start
  16.0 1.2 %copy-done = bf16[512,1024]{1,0:T(8,128)(2,1)S(1)} copy-done((bf16[512,1024]{1,0:T(8,128)(2,1)S(1)}, bf16[512,1024]{1,0:T(8,128)(2,1)}, u32[]{:S(2)}) %copy-start) | copy-done | bytes 1048600
  17.2 0.0 copy-start.2
  17.2 1.2 %copy-done.2 = bf16[1024,1,512]{2,0,1:T(8,128)(2,1)S(1)} copy-done((bf16[1024,1,512]{2,0,1:T(8,128)(2,1)S(1)}, bf16[1024,1,512]{2,0,1:T(8,128)(2,1)}, u32[]{:S(2)}) %copy-start.2) | copy-done | bytes 1048600
  18.4 0.0 copy-start.3
  18.4 0.0 copy-start.6
  18.4 0.0 copy-start.7
  18.4 1.6 %local.1 = (f32[512,384]{1,0:T(8,128)S(1)}, f32[8,128]{1,0:T(8,128)S(1)}) custom-call(bf16[512,1024]{1,0:T(8,128)(2,1)S(1)} %copy-done, bf16[1024,512]{1,0:T(8,128)(2,1)S(1)} %bitcast.16, s32[1,64]{1,0:T(1,128)S(1)} %bitcast.23, s32[1,64]{1,0:T(1,128)S(1)} %bitcast.25, s32[1,64]{1,0:T(1,128)S(1)} %bitcast.28, s32[1,64]{1,0:T(1,128)S(1)} %bitcast.29, ...), custom_call_target="tpu_custom_call" | custom-call | flops 1073741824 | bytes 16777216 | tf_op jit(solution)/shard_map/local/pallas_call | solution.py:269
  20.0 0.0 copy-start.10
  20.0 0.9 %copy-done.10 = f32[512,384]{1,0:T(8,128)} copy-done((f32[512,384]{1,0:T(8,128)}, f32[512,384]{1,0:T(8,128)S(1)}, u32[]{:S(2)}) %copy-start.10) | copy-done | bytes 786456
  20.9 0.0 copy-done.3
  20.9 7.9 %collective-permute-start.1 = (bf16[128,1024]{1,0:T(8,128)(2,1)S(1)}, bf16[128,1024]{1,0:T(8,128)(2,1)S(1)}, u32[]{:S(2)}, u32[]{:S(2)}) collective-permute-start(bf16[128,1024]{1,0:T(8,128)(2,1)S(1)} %bitcast.17), channel_id=1, source_target_pairs={{0,3},{1,4},{2,5},{3,6},{4,7},{5,0},{6,1},{7,2},{8,13},{9,14},{10,... | collective-permute-start | bytes 786440 | tf_op jit(solution)/shard_map/ppermute | solution.py:264
  28.8 5.5 %collective-permute-start = (bf16[128,1024]{1,0:T(8,128)(2,1)S(1)}, bf16[128,1024]{1,0:T(8,128)(2,1)}, u32[]{:S(2)}, u32[]{:S(2)}) collective-permute-start(bf16[128,1024]{1,0:T(8,128)(2,1)S(1)} %bitcast.18), channel_id=1, source_target_pairs={{0,1},{1,2},{2,3},{3,4},{4,5},{5,6},{6,7},{7,0},{8,15},{9,8},{10,9... | collective-permute-start | bytes 786440 | tf_op jit(solution)/shard_map/ppermute | solution.py:264
  34.3 0.0 all-to-all-done
  34.3 0.0 copy-done.6
  34.3 0.0 copy-done.7
  34.3 2.3 %history.1 = bf16[1024,128]{1,0:T(8,128)(2,1)} custom-call(f32[8,128]{1,0:T(8,128)S(1)} %get-tuple-element.12.info_ref, bf16[1024,128]{1,0:T(8,128)(2,1)S(1)} %bitcast.21, bf16[1024,128]{1,0:T(8,128)(2,1)S(1)} %bitcast.26, bf16[1024,128]{1,0:T(8,128)(2,1)S(1)} %bitcast.27), custom_call_target="tpu_custom_call" | custom-call | flops 1073741824 | bytes 67108864 | tf_op jit(solution)/shard_map/history/pallas_call | solution.py:283
  36.6 10.3 %all-to-all-start.1 = ((bf16[64,16,128]{2,1,0:T(8,128)(2,1)}), bf16[64,16,128]{2,1,0:T(8,128)(2,1)S(1)}, u32[]{:S(2)}, u32[]{:S(2)}) async-start(bf16[64,16,128]{2,1,0:T(8,128)(2,1)} %bitcast.11), calls=%async_computation.1 | async-start | bytes 524288 | tf_op jit(solution)/shard_map/all_to_all | solution.py:306
  47.0 0.0 collective-permute-done.1
  47.0 0.0 collective-permute-done
  47.0 1.0 %constant_dynamic-update-slice_fusion.1 = bf16[256,1024]{1,0:T(8,128)(2,1)S(1)} fusion(bf16[128,1024]{1,0:T(8,128)(2,1)} %collective-permute-done), kind=kLoop, calls=%fused_computation.1 | loop fusion | bytes 524288
  48.0 2.1 %collective-permute-start.3 = (bf16[256,1024]{1,0:T(8,128)(2,1)S(1)}, bf16[256,1024]{1,0:T(8,128)(2,1)S(1)}, u32[]{:S(2)}, u32[]{:S(2)}) collective-permute-start(bf16[256,1024]{1,0:T(8,128)(2,1)S(1)} %constant_dynamic-update-slice_fusion.next_ref), channel_id=1, source_target_pairs={{0,8},{8,0},{16,24},{24,16},{32,40},{40,32},{48,56},{56,48},{64,72... | collective-permute-start | bytes 1572872 | tf_op jit(solution)/shard_map/ppermute | solution.py:267
  50.1 3.4 %collective-permute-start.2 = (bf16[256,1024]{1,0:T(8,128)(2,1)S(1)}, bf16[256,1024]{1,0:T(8,128)(2,1)S(1)}, u32[]{:S(2)}, u32[]{:S(2)}) collective-permute-start(bf16[256,1024]{1,0:T(8,128)(2,1)S(1)} %constant_dynamic-update-slice_fusion.next_ref), channel_id=1, source_target_pairs={{0,1},{1,2},{2,3},{3,4},{4,5},{5,6},{6,7},{7,0},{8,15},{9,8},{10,9... | collective-permute-start | bytes 1572872 | tf_op jit(solution)/shard_map/ppermute | solution.py:264
  53.5 2.1 %collective-permute-start.4 = (bf16[128,1024]{1,0:T(8,128)(2,1)}, bf16[128,1024]{1,0:T(8,128)(2,1)S(1)}, u32[]{:S(2)}, u32[]{:S(2)}) collective-permute-start(bf16[128,1024]{1,0:T(8,128)(2,1)} %collective-permute-done), channel_id=1, source_target_pairs={{0,9},{1,10},{2,11},{3,12},{4,13},{5,14},{6,15},{7,8},{8,7},{9,0},... | collective-permute-start | bytes 786440 | tf_op jit(solution)/shard_map/ppermute | solution.py:264
  55.6 2.9 %all-to-all-done.1 = bf16[64,16,128]{2,1,0:T(8,128)(2,1)S(1)} async-done(((bf16[64,16,128]{2,1,0:T(8,128)(2,1)}), bf16[64,16,128]{2,1,0:T(8,128)(2,1)S(1)}, u32[]{:S(2)}, u32[]{:S(2)}) %all-to-all-start.1) | async-done | bytes 262176 | tf_op jit(solution)/shard_map/all_to_all | solution.py:306
  58.6 0.0 copy-start.1
  58.6 2.8 %gate.1 = bf16[512,128]{1,0:T(8,128)(2,1)} custom-call(bf16[1024,128]{1,0:T(8,128)(2,1)S(1)} %bitcast.20, f32[512,384]{1,0:T(8,128)} %copy-done.10), custom_call_target="tpu_custom_call" | custom-call | flops 1073741824 | bytes 67108864 | tf_op jit(solution)/shard_map/gate/pallas_call | solution.py:309
  61.4 4.6 %all-to-all-start.2 = ((bf16[8,64,128]{2,1,0:T(8,128)(2,1)}), bf16[8,64,128]{2,1,0:T(8,128)(2,1)S(1)}, u32[]{:S(2)}, u32[]{:S(2)}) async-start(bf16[8,64,128]{2,1,0:T(8,128)(2,1)} %bitcast.13), calls=%async_computation.2 | async-start | bytes 262144 | tf_op jit(solution)/shard_map/all_to_all | solution.py:325
  65.9 0.0 collective-permute-done.4.two_ref
  65.9 0.0 collective-permute-done.3.other_ref
  66.0 0.0 collective-permute-done.2.last_ref
  66.0 9.3 %all-to-all-done.2.gated_ref = bf16[8,64,128]{2,1,0:T(8,128)(2,1)S(1)} async-done(((bf16[8,64,128]{2,1,0:T(8,128)(2,1)}), bf16[8,64,128]{2,1,0:T(8,128)(2,1)S(1)}, u32[]{:S(2)}, u32[]{:S(2)}) %all-to-all-start.2) | async-done | bytes 131104 | tf_op jit(solution)/shard_map/all_to_all | solution.py:325
  75.3 0.0 copy-done.1
  75.3 1.3 %output.1 = bf16[64,1024]{1,0:T(8,128)(2,1)} custom-call(s32[1]{0:T(128)} %bitcast.group_ref, s32[1]{0:T(128)} %bitcast.1.me_ref, bf16[512,1024]{1,0:T(8,128)(2,1)S(1)} %copy-done.1, bf16[8,64,128]{2,1,0:T(8,128)(2,1)S(1)} %all-to-all-done.2.gated_ref, bf16[128,1024]{1,0:T(8,128)(2,1)S(1)} %bitcast.19, ...), custom_call_target="tpu_custom_call" | custom-call | tf_op jit(solution)/shard_map/output/pallas_call | solution.py:328
  (1 shorter events, 0.0 us)
Async XLA Ops:
  4.5 10.9 %copy-start.9 = (s32[64]{0:T(128)S(1)}, s32[64]{0:T(128)}, u32[]{:S(2)}) copy-start(s32[64]{0:T(128)} %param.17) | copy-start | bytes 772
  4.5 29.8 %all-to-all-start = ((bf16[64,16,128]{2,1,0:T(8,128)(2,1)}), bf16[64,16,128]{2,1,0:T(8,128)(2,1)S(1)}, u32[]{:S(2)}, u32[]{:S(2)}) async-start(bf16[64,16,128]{2,1,0:T(8,128)(2,1)} %bitcast.30), calls=%async_computation | async-start | bytes 524288 | tf_op jit(solution)/shard_map/all_to_all | solution.py:256
  15.3 0.7 copy-start.4
  15.3 0.7 copy-start.5
  15.3 0.7 copy-start.8
  16.0 1.2 %copy-start = (bf16[512,1024]{1,0:T(8,128)(2,1)S(1)}, bf16[512,1024]{1,0:T(8,128)(2,1)}, u32[]{:S(2)}) copy-start(bf16[512,1024]{1,0:T(8,128)(2,1)} %tokens_ref.5) | copy-start | bytes 3145732
  17.2 1.2 %copy-start.2 = (bf16[1024,1,512]{2,0,1:T(8,128)(2,1)S(1)}, bf16[1024,1,512]{2,0,1:T(8,128)(2,1)}, u32[]{:S(2)}) copy-start(bf16[1024,1,512]{2,0,1:T(8,128)(2,1)} %param.10) | copy-start | bytes 3145732
  18.4 2.5 %copy-start.3 = (bf16[1,128,1024]{2,1,0:T(8,128)(2,1)S(1)}, bf16[1,128,1024]{2,1,0:T(8,128)(2,1)}, u32[]{:S(2)}) copy-start(bf16[1,128,1024]{2,1,0:T(8,128)(2,1)} %param.11) | copy-start | bytes 786436
  18.4 15.9 %copy-start.6 = (bf16[1,1024,1,128]{3,1,2,0:T(8,128)(2,1)S(1)}, bf16[1,1024,1,128]{3,1,2,0:T(8,128)(2,1)}, u32[]{:S(2)}) copy-start(bf16[1,1024,1,128]{3,1,2,0:T(8,128)(2,1)} %param.12) | copy-start | bytes 786436
  18.4 15.9 %copy-start.7 = (bf16[1,1024,1,128]{3,1,2,0:T(8,128)(2,1)S(1)}, bf16[1,1024,1,128]{3,1,2,0:T(8,128)(2,1)}, u32[]{:S(2)}) copy-start(bf16[1,1024,1,128]{3,1,2,0:T(8,128)(2,1)} %param.13) | copy-start | bytes 786436
  20.0 0.9 %copy-start.10 = (f32[512,384]{1,0:T(8,128)}, f32[512,384]{1,0:T(8,128)S(1)}, u32[]{:S(2)}) copy-start(f32[512,384]{1,0:T(8,128)S(1)} %get-tuple-element.13.mine_ref) | copy-start | bytes 2359300
  20.9 26.1 %collective-permute-start.1 = (bf16[128,1024]{1,0:T(8,128)(2,1)S(1)}, bf16[128,1024]{1,0:T(8,128)(2,1)S(1)}, u32[]{:S(2)}, u32[]{:S(2)}) collective-permute-start(bf16[128,1024]{1,0:T(8,128)(2,1)S(1)} %bitcast.17), channel_id=1, source_target_pairs={{0,3},{1,4},{2,5},{3,6},{4,7},{5,0},{6,1},{7,2},{8,13},{9,14},{10,... | collective-permute-start | bytes 786440 | tf_op jit(solution)/shard_map/ppermute | solution.py:264
  28.8 18.2 %collective-permute-start = (bf16[128,1024]{1,0:T(8,128)(2,1)S(1)}, bf16[128,1024]{1,0:T(8,128)(2,1)}, u32[]{:S(2)}, u32[]{:S(2)}) collective-permute-start(bf16[128,1024]{1,0:T(8,128)(2,1)S(1)} %bitcast.18), channel_id=1, source_target_pairs={{0,1},{1,2},{2,3},{3,4},{4,5},{5,6},{6,7},{7,0},{8,15},{9,8},{10,9... | collective-permute-start | bytes 786440 | tf_op jit(solution)/shard_map/ppermute | solution.py:264
  36.6 21.9 %all-to-all-start.1 = ((bf16[64,16,128]{2,1,0:T(8,128)(2,1)}), bf16[64,16,128]{2,1,0:T(8,128)(2,1)S(1)}, u32[]{:S(2)}, u32[]{:S(2)}) async-start(bf16[64,16,128]{2,1,0:T(8,128)(2,1)} %bitcast.11), calls=%async_computation.1 | async-start | bytes 524288 | tf_op jit(solution)/shard_map/all_to_all | solution.py:306
  48.0 17.9 %collective-permute-start.3 = (bf16[256,1024]{1,0:T(8,128)(2,1)S(1)}, bf16[256,1024]{1,0:T(8,128)(2,1)S(1)}, u32[]{:S(2)}, u32[]{:S(2)}) collective-permute-start(bf16[256,1024]{1,0:T(8,128)(2,1)S(1)} %constant_dynamic-update-slice_fusion.next_ref), channel_id=1, source_target_pairs={{0,8},{8,0},{16,24},{24,16},{32,40},{40,32},{48,56},{56,48},{64,72... | collective-permute-start | bytes 1572872 | tf_op jit(solution)/shard_map/ppermute | solution.py:267
  50.1 15.9 %collective-permute-start.2 = (bf16[256,1024]{1,0:T(8,128)(2,1)S(1)}, bf16[256,1024]{1,0:T(8,128)(2,1)S(1)}, u32[]{:S(2)}, u32[]{:S(2)}) collective-permute-start(bf16[256,1024]{1,0:T(8,128)(2,1)S(1)} %constant_dynamic-update-slice_fusion.next_ref), channel_id=1, source_target_pairs={{0,1},{1,2},{2,3},{3,4},{4,5},{5,6},{6,7},{7,0},{8,15},{9,8},{10,9... | collective-permute-start | bytes 1572872 | tf_op jit(solution)/shard_map/ppermute | solution.py:264
  53.5 12.5 %collective-permute-start.4 = (bf16[128,1024]{1,0:T(8,128)(2,1)}, bf16[128,1024]{1,0:T(8,128)(2,1)S(1)}, u32[]{:S(2)}, u32[]{:S(2)}) collective-permute-start(bf16[128,1024]{1,0:T(8,128)(2,1)} %collective-permute-done), channel_id=1, source_target_pairs={{0,9},{1,10},{2,11},{3,12},{4,13},{5,14},{6,15},{7,8},{8,7},{9,0},... | collective-permute-start | bytes 786440 | tf_op jit(solution)/shard_map/ppermute | solution.py:264
  58.6 16.8 %copy-start.1 = (bf16[512,1024]{1,0:T(8,128)(2,1)S(1)}, bf16[512,1024]{1,0:T(8,128)(2,1)}, u32[]{:S(2)}) copy-start(bf16[512,1024]{1,0:T(8,128)(2,1)} %tokens_ref.5) | copy-start | bytes 3145732
  61.4 14.0 %all-to-all-start.2 = ((bf16[8,64,128]{2,1,0:T(8,128)(2,1)}), bf16[8,64,128]{2,1,0:T(8,128)(2,1)S(1)}, u32[]{:S(2)}, u32[]{:S(2)}) async-start(bf16[8,64,128]{2,1,0:T(8,128)(2,1)} %bitcast.13), calls=%async_computation.2 | async-start | bytes 262144 | tf_op jit(solution)/shard_map/all_to_all | solution.py:325

commit v12 on v11

--- a/solution.py
+++ b/solution.py
@@ -169,7 +169,7 @@
 
 
 def output_kernel(
-    group_ref, me_ref, tokens_ref, gated_ref, own_ref, next_ref, last_ref, other_ref, two_ref,
+    group_ref, me_ref, tokens_ref, gated_ref, own_ref, next_ref, last_ref, other_ref, three_ref,
     out_ref, tokens, result, sems,
 ):
     groups, share, head_dim = gated_ref.shape
@@ -180,10 +180,10 @@
     sign = jnp.where(me_ref[0] % 2 == 0, -1, 1)
     total = jnp.zeros(result.shape, f32)
     for heads, weight in (
-        ((1, 3), next_ref[...]),
-        ((2, 4), last_ref[...]),
-        ((-1, -3), other_ref[...]),
-        ((0, -2), jnp.concatenate([own_ref[...], two_ref[...]], axis=0)),
+        ((1, 2), next_ref[...]),
+        ((3, 4), last_ref[...]),
+        ((-1, -2), other_ref[...]),
+        ((0, -3), jnp.concatenate([own_ref[...], three_ref[...]], axis=0)),
     ):
         rows = jnp.concatenate([gated_ref[lax.rem(group + sign * head + groups, groups)] for head in heads], axis=1)
         total = total + jnp.dot(rows, weight, preferred_element_type=f32)
@@ -278,7 +278,7 @@
     )(tokens, w_flat, slots, after(named, sent), counts, lengths, my_index)
     w_own = after(w_out.reshape(head_dim, model_width), mine)
     next_one = passed(w_own, 1)
-    next_three = passed(w_own, 3)
+    next_two = passed(w_own, 2)
     block = min(256, slot_rows)
     answers = pl.pallas_call(
         functools.partial(history_kernel, block),
@@ -298,11 +298,11 @@
         cache_keys.reshape(history, head_dim),
         cache_values.reshape(history, head_dim),
     )
-    next_one, next_three = after((next_one, next_three), answers)
-    nexts = jnp.concatenate([next_one, next_three], axis=0)
-    lasts = passed(nexts, 1)
+    next_one, next_two = after((next_one, next_two), answers)
+    nexts = jnp.concatenate([next_one, next_two], axis=0)
+    lasts = passed(nexts, 2)
     others = swapped(nexts)
-    other_two = passed(next_one, 1, flip=1)
+    other_three = passed(next_two, 1, flip=1)
     returned = lax.all_to_all(
         answers.reshape(replicas, capacity * cands, head_dim), "replica", split_axis=0, concat_axis=0, tiled=True
     )
@@ -337,7 +337,7 @@
         ],
         compiler_params=roomy,
         name="output",
-    )(group_index, my_index, tokens, heads, w_own, nexts, lasts, others, other_two)
+    )(group_index, my_index, tokens, heads, w_own, nexts, lasts, others, other_three)
 
 
 def solution(mesh):

time: 77.3 us -> 76.9 us (level)
  waiting for transfers between devices: 12.3 us -> 11.3 us
    all_to_all x1, waiting for transfers between devices: 9.34 us -> 4.98 us  [on_device(): lax.all_to_all(gated.reshape(groups, share, head_dim), 'tensor', split_ax...]
    ppermute x4, waiting for transfers between devices: 0.01 us -> 4.03 us  [passed(): return lax.ppermute(piece, ('replica', 'tensor'), pairs)]
    ppermute x4, starting transfers between devices: 18.9 us -> 16.6 us  [passed(): return lax.ppermute(piece, ('replica', 'tensor'), pairs)]
    all_to_all x1, starting transfers between devices: 10.3 us -> 12.6 us  [on_device(): lax.all_to_all(answers.reshape(replicas, capacity * cands, head_dim), 're...]
    unnamed x23, local copies, waits for them, and re-layouts: 4.98 us -> 4.03 us
    concatenate x1, local copies, waits for them, and re-layouts: 0.02 us -> 0.97 us  [on_device(): nexts = jnp.concatenate([next_one, next_two], axis=0)]
    all_to_all x1, starting transfers between devices: 4.58 us -> 5.38 us  [on_device(): lax.all_to_all(gated.reshape(groups, share, head_dim), 'tensor', split_ax...]
  transfers between devices with their start and end apart: 8 -> 8, of which waited for: 2 -> 3; matrix products, arithmetic and copies ran while one was open for 1% -> 1% of each run, Pallas kernels for 9% -> 9%
where the time goes in v12:
time: 76.9 us; the launch traced here: 76.3 us
  starting transfers between devices  47.4 us (62%)
  Pallas kernels  12.4 us (16%)
  waiting for transfers between devices  11.3 us (15%)
  local copies, waits for them, and re-layouts  5 us (7%)
    ppermute x4, starting transfers between devices, passed(): return lax.ppermute(piece, ('replica', 'tensor'), pairs)  16.6 us
    all_to_all x1, starting transfers between devices, on_device(): lax.all_to_all(answers.reshape(replicas, capacity * cands, head_dim), 're...  12.6 us
    all_to_all x1, starting transfers between devices, on_device(): lax.all_to_all(sent.reshape(replicas, capacity * cands, head_dim), 'repli...  10.8 us
    all_to_all x1, starting transfers between devices, on_device(): lax.all_to_all(gated.reshape(groups, share, head_dim), 'tensor', split_ax...  5.38 us
    all_to_all x1, waiting for transfers between devices, on_device(): lax.all_to_all(gated.reshape(groups, share, head_dim), 'tensor', split_ax...  4.98 us
    pallas_call x1, Pallas kernels, on_device(): pl.pallas_call(functools.partial(send_kernel, capacity, cands, chunks), i...  4.45 us
    ppermute x4, waiting for transfers between devices, passed(): return lax.ppermute(piece, ('replica', 'tensor'), pairs)  4.03 us
    unnamed x23, local copies, waits for them, and re-layouts  4.03 us
  transfers between devices with their start and end apart: 8, of which 3 were waited for; matrix products, arithmetic and copies ran while one was open for 1% of the time, Pallas kernels for 9%

profile of v12, /device:TPU:6, one launch (start us, length us, event | category | flops | bytes accessed | tf_op | source)
XLA Modules:
  0.0 76.3 jit_solution(1978609132855790462)
XLA Ops:
  0.0 4.4 %send.1 = bf16[1024,128]{1,0:T(8,128)(2,1)} custom-call(bf16[512,1024]{1,0:T(8,128)(2,1)} %tokens_ref.5, bf16[1024,512]{1,0:T(8,128)(2,1)} %bitcast.15, s32[1,64]{1,0:T(1,128)} %bitcast.22, s32[1,64]{1,0:T(1,128)} %bitcast.24), custom_call_target="tpu_custom_call" | custom-call | tf_op jit(solution)/shard_map/send/pallas_call | solution.py:239
  4.5 0.0 copy-start.9
  4.5 10.8 %all-to-all-start = ((bf16[64,16,128]{2,1,0:T(8,128)(2,1)}), bf16[64,16,128]{2,1,0:T(8,128)(2,1)S(1)}, u32[]{:S(2)}, u32[]{:S(2)}) async-start(bf16[64,16,128]{2,1,0:T(8,128)(2,1)} %bitcast.30), calls=%async_computation | async-start | bytes 524288 | tf_op jit(solution)/shard_map/all_to_all | solution.py:256
  15.3 0.0 copy-start.4
  15.3 0.0 copy-start.5
  15.3 0.0 copy-start.8
  15.3 0.0 copy-done.9
  15.3 0.6 copy-done.4
  16.0 0.0 copy-done.5
  16.0 0.0 copy-done.8
  16.0 0.0 copy-start
  16.0 1.2 %copy-done = bf16[512,1024]{1,0:T(8,128)(2,1)S(1)} copy-done((bf16[512,1024]{1,0:T(8,128)(2,1)S(1)}, bf16[512,1024]{1,0:T(8,128)(2,1)}, u32[]{:S(2)}) %copy-start) | copy-done | bytes 1048600
  17.2 0.0 copy-start.2
  17.2 1.2 %copy-done.2 = bf16[1024,1,512]{2,0,1:T(8,128)(2,1)S(1)} copy-done((bf16[1024,1,512]{2,0,1:T(8,128)(2,1)S(1)}, bf16[1024,1,512]{2,0,1:T(8,128)(2,1)}, u32[]{:S(2)}) %copy-start.2) | copy-done | bytes 1048600
  18.4 0.0 copy-start.3
  18.4 0.0 copy-start.6
  18.4 0.0 copy-start.7
  18.4 1.6 %local.1 = (f32[512,384]{1,0:T(8,128)S(1)}, f32[8,128]{1,0:T(8,128)S(1)}) custom-call(bf16[512,1024]{1,0:T(8,128)(2,1)S(1)} %copy-done, bf16[1024,512]{1,0:T(8,128)(2,1)S(1)} %bitcast.16, s32[1,64]{1,0:T(1,128)S(1)} %bitcast.23, s32[1,64]{1,0:T(1,128)S(1)} %bitcast.25, s32[1,64]{1,0:T(1,128)S(1)} %bitcast.28, s32[1,64]{1,0:T(1,128)S(1)} %bitcast.29, ...), custom_call_target="tpu_custom_call" | custom-call | flops 1073741824 | bytes 16777216 | tf_op jit(solution)/shard_map/local/pallas_call | solution.py:269
  20.0 0.0 copy-start.10
  20.0 0.9 %copy-done.10 = f32[512,384]{1,0:T(8,128)} copy-done((f32[512,384]{1,0:T(8,128)}, f32[512,384]{1,0:T(8,128)S(1)}, u32[]{:S(2)}) %copy-start.10) | copy-done | bytes 786456
  20.9 0.0 copy-done.3
  20.9 6.1 %collective-permute-start.1 = (bf16[128,1024]{1,0:T(8,128)(2,1)S(1)}, bf16[128,1024]{1,0:T(8,128)(2,1)}, u32[]{:S(2)}, u32[]{:S(2)}) collective-permute-start(bf16[128,1024]{1,0:T(8,128)(2,1)S(1)} %bitcast.17), channel_id=1, source_target_pairs={{0,2},{1,3},{2,4},{3,5},{4,6},{5,7},{6,0},{7,1},{8,14},{9,15},{10,... | collective-permute-start | bytes 786440 | tf_op jit(solution)/shard_map/ppermute | solution.py:264
  27.0 4.3 %collective-permute-start = (bf16[128,1024]{1,0:T(8,128)(2,1)S(1)}, bf16[128,1024]{1,0:T(8,128)(2,1)S(1)}, u32[]{:S(2)}, u32[]{:S(2)}) collective-permute-start(bf16[128,1024]{1,0:T(8,128)(2,1)S(1)} %bitcast.18), channel_id=1, source_target_pairs={{0,1},{1,2},{2,3},{3,4},{4,5},{5,6},{6,7},{7,0},{8,15},{9,8},{10,9... | collective-permute-start | bytes 786440 | tf_op jit(solution)/shard_map/ppermute | solution.py:264
  31.3 0.0 all-to-all-done
  31.3 0.0 copy-done.6
  31.3 0.0 copy-done.7
  31.3 2.3 %history.1 = bf16[1024,128]{1,0:T(8,128)(2,1)} custom-call(f32[8,128]{1,0:T(8,128)S(1)} %get-tuple-element.12.info_ref, bf16[1024,128]{1,0:T(8,128)(2,1)S(1)} %bitcast.21, bf16[1024,128]{1,0:T(8,128)(2,1)S(1)} %bitcast.26, bf16[1024,128]{1,0:T(8,128)(2,1)S(1)} %bitcast.27), custom_call_target="tpu_custom_call" | custom-call | flops 1073741824 | bytes 67108864 | tf_op jit(solution)/shard_map/history/pallas_call | solution.py:283
  33.6 12.6 %all-to-all-start.1 = ((bf16[64,16,128]{2,1,0:T(8,128)(2,1)}), bf16[64,16,128]{2,1,0:T(8,128)(2,1)S(1)}, u32[]{:S(2)}, u32[]{:S(2)}) async-start(bf16[64,16,128]{2,1,0:T(8,128)(2,1)} %bitcast.11), calls=%async_computation.1 | async-start | bytes 524288 | tf_op jit(solution)/shard_map/all_to_all | solution.py:306
  46.2 0.0 collective-permute-done.1
  46.2 0.0 collective-permute-done
  46.2 1.0 %constant_dynamic-update-slice_fusion.next_ref = bf16[256,1024]{1,0:T(8,128)(2,1)S(1)} fusion(bf16[256,1024]{1,0:T(8,128)(2,1)S(1)} %constant_dynamic-update-slice_fusion.1, bf16[128,1024]{1,0:T(8,128)(2,1)} %collective-permute-done.1), kind=kLoop, calls=%fused_computation | loop fusion | bytes 524288 | tf_op jit(solution)/shard_map/concatenate | solution.py:302
  47.2 2.1 %collective-permute-start.3 = (bf16[256,1024]{1,0:T(8,128)(2,1)S(1)}, bf16[256,1024]{1,0:T(8,128)(2,1)S(1)}, u32[]{:S(2)}, u32[]{:S(2)}) collective-permute-start(bf16[256,1024]{1,0:T(8,128)(2,1)S(1)} %constant_dynamic-update-slice_fusion.next_ref), channel_id=1, source_target_pairs={{0,8},{8,0},{16,24},{24,16},{32,40},{40,32},{48,56},{56,48},{64,72... | collective-permute-start | bytes 1572872 | tf_op jit(solution)/shard_map/ppermute | solution.py:267
  49.3 4.3 %collective-permute-start.2 = (bf16[256,1024]{1,0:T(8,128)(2,1)S(1)}, bf16[256,1024]{1,0:T(8,128)(2,1)S(1)}, u32[]{:S(2)}, u32[]{:S(2)}) collective-permute-start(bf16[256,1024]{1,0:T(8,128)(2,1)S(1)} %constant_dynamic-update-slice_fusion.next_ref), channel_id=1, source_target_pairs={{0,2},{1,3},{2,4},{3,5},{4,6},{5,7},{6,0},{7,1},{8,14},{9,15},{10,... | collective-permute-start | bytes 1572872 | tf_op jit(solution)/shard_map/ppermute | solution.py:264
  53.6 1.9 %collective-permute-start.4 = (bf16[128,1024]{1,0:T(8,128)(2,1)}, bf16[128,1024]{1,0:T(8,128)(2,1)S(1)}, u32[]{:S(2)}, u32[]{:S(2)}) collective-permute-start(bf16[128,1024]{1,0:T(8,128)(2,1)} %collective-permute-done.1), channel_id=1, source_target_pairs={{0,9},{1,10},{2,11},{3,12},{4,13},{5,14},{6,15},{7,8},{8,7},{9,0},... | collective-permute-start | bytes 786440 | tf_op jit(solution)/shard_map/ppermute | solution.py:264
  55.5 2.2 %all-to-all-done.1 = bf16[64,16,128]{2,1,0:T(8,128)(2,1)S(1)} async-done(((bf16[64,16,128]{2,1,0:T(8,128)(2,1)}), bf16[64,16,128]{2,1,0:T(8,128)(2,1)S(1)}, u32[]{:S(2)}, u32[]{:S(2)}) %all-to-all-start.1) | async-done | bytes 262176 | tf_op jit(solution)/shard_map/all_to_all | solution.py:306
  57.8 0.0 copy-start.1
  57.8 2.8 %gate.1 = bf16[512,128]{1,0:T(8,128)(2,1)} custom-call(bf16[1024,128]{1,0:T(8,128)(2,1)S(1)} %bitcast.20, f32[512,384]{1,0:T(8,128)} %copy-done.10), custom_call_target="tpu_custom_call" | custom-call | flops 1073741824 | bytes 67108864 | tf_op jit(solution)/shard_map/gate/pallas_call | solution.py:309
  60.6 5.4 %all-to-all-start.2 = ((bf16[8,64,128]{2,1,0:T(8,128)(2,1)}), bf16[8,64,128]{2,1,0:T(8,128)(2,1)S(1)}, u32[]{:S(2)}, u32[]{:S(2)}) async-start(bf16[8,64,128]{2,1,0:T(8,128)(2,1)} %bitcast.13), calls=%async_computation.2 | async-start | bytes 262144 | tf_op jit(solution)/shard_map/all_to_all | solution.py:325
  65.9 4.0 %collective-permute-done.4.three_ref = bf16[128,1024]{1,0:T(8,128)(2,1)S(1)} collective-permute-done((bf16[128,1024]{1,0:T(8,128)(2,1)}, bf16[128,1024]{1,0:T(8,128)(2,1)S(1)}, u32[]{:S(2)}, u32[]{:S(2)}) %collective-permute-start.4) | collective-permute-done | bytes 262176 | tf_op jit(solution)/shard_map/ppermute | solution.py:264
  70.0 0.0 collective-permute-done.3.other_ref
  70.0 0.0 collective-permute-done.2.last_ref
  70.0 5.0 %all-to-all-done.2.gated_ref = bf16[8,64,128]{2,1,0:T(8,128)(2,1)S(1)} async-done(((bf16[8,64,128]{2,1,0:T(8,128)(2,1)}), bf16[8,64,128]{2,1,0:T(8,128)(2,1)S(1)}, u32[]{:S(2)}, u32[]{:S(2)}) %all-to-all-start.2) | async-done | bytes 131104 | tf_op jit(solution)/shard_map/all_to_all | solution.py:325
  75.0 0.0 copy-done.1
  75.0 1.3 %output.1 = bf16[64,1024]{1,0:T(8,128)(2,1)} custom-call(s32[1]{0:T(128)} %bitcast.group_ref, s32[1]{0:T(128)} %bitcast.1.me_ref, bf16[512,1024]{1,0:T(8,128)(2,1)S(1)} %copy-done.1, bf16[8,64,128]{2,1,0:T(8,128)(2,1)S(1)} %all-to-all-done.2.gated_ref, bf16[128,1024]{1,0:T(8,128)(2,1)S(1)} %bitcast.19, ...), custom_call_target="tpu_custom_call" | custom-call | tf_op jit(solution)/shard_map/output/pallas_call | solution.py:328
  (1 shorter events, 0.0 us)
Async XLA Ops:
  4.5 10.9 %copy-start.9 = (s32[64]{0:T(128)S(1)}, s32[64]{0:T(128)}, u32[]{:S(2)}) copy-start(s32[64]{0:T(128)} %param.17) | copy-start | bytes 772
  4.5 26.8 %all-to-all-start = ((bf16[64,16,128]{2,1,0:T(8,128)(2,1)}), bf16[64,16,128]{2,1,0:T(8,128)(2,1)S(1)}, u32[]{:S(2)}, u32[]{:S(2)}) async-start(bf16[64,16,128]{2,1,0:T(8,128)(2,1)} %bitcast.30), calls=%async_computation | async-start | bytes 524288 | tf_op jit(solution)/shard_map/all_to_all | solution.py:256
  15.3 0.7 copy-start.4
  15.3 0.7 copy-start.5
  15.3 0.7 copy-start.8
  16.0 1.2 %copy-start = (bf16[512,1024]{1,0:T(8,128)(2,1)S(1)}, bf16[512,1024]{1,0:T(8,128)(2,1)}, u32[]{:S(2)}) copy-start(bf16[512,1024]{1,0:T(8,128)(2,1)} %tokens_ref.5) | copy-start | bytes 3145732
  17.2 1.2 %copy-start.2 = (bf16[1024,1,512]{2,0,1:T(8,128)(2,1)S(1)}, bf16[1024,1,512]{2,0,1:T(8,128)(2,1)}, u32[]{:S(2)}) copy-start(bf16[1024,1,512]{2,0,1:T(8,128)(2,1)} %param.10) | copy-start | bytes 3145732
  18.4 2.5 %copy-start.3 = (bf16[1,128,1024]{2,1,0:T(8,128)(2,1)S(1)}, bf16[1,128,1024]{2,1,0:T(8,128)(2,1)}, u32[]{:S(2)}) copy-start(bf16[1,128,1024]{2,1,0:T(8,128)(2,1)} %param.11) | copy-start | bytes 786436
  18.4 12.9 %copy-start.6 = (bf16[1,1024,1,128]{3,1,2,0:T(8,128)(2,1)S(1)}, bf16[1,1024,1,128]{3,1,2,0:T(8,128)(2,1)}, u32[]{:S(2)}) copy-start(bf16[1,1024,1,128]{3,1,2,0:T(8,128)(2,1)} %param.12) | copy-start | bytes 786436
  18.4 12.9 %copy-start.7 = (bf16[1,1024,1,128]{3,1,2,0:T(8,128)(2,1)S(1)}, bf16[1,1024,1,128]{3,1,2,0:T(8,128)(2,1)}, u32[]{:S(2)}) copy-start(bf16[1,1024,1,128]{3,1,2,0:T(8,128)(2,1)} %param.13) | copy-start | bytes 786436
  20.0 0.9 %copy-start.10 = (f32[512,384]{1,0:T(8,128)}, f32[512,384]{1,0:T(8,128)S(1)}, u32[]{:S(2)}) copy-start(f32[512,384]{1,0:T(8,128)S(1)} %get-tuple-element.13.mine_ref) | copy-start | bytes 2359300
  20.9 25.3 %collective-permute-start.1 = (bf16[128,1024]{1,0:T(8,128)(2,1)S(1)}, bf16[128,1024]{1,0:T(8,128)(2,1)}, u32[]{:S(2)}, u32[]{:S(2)}) collective-permute-start(bf16[128,1024]{1,0:T(8,128)(2,1)S(1)} %bitcast.17), channel_id=1, source_target_pairs={{0,2},{1,3},{2,4},{3,5},{4,6},{5,7},{6,0},{7,1},{8,14},{9,15},{10,... | collective-permute-start | bytes 786440 | tf_op jit(solution)/shard_map/ppermute | solution.py:264
  27.0 19.2 %collective-permute-start = (bf16[128,1024]{1,0:T(8,128)(2,1)S(1)}, bf16[128,1024]{1,0:T(8,128)(2,1)S(1)}, u32[]{:S(2)}, u32[]{:S(2)}) collective-permute-start(bf16[128,1024]{1,0:T(8,128)(2,1)S(1)} %bitcast.18), channel_id=1, source_target_pairs={{0,1},{1,2},{2,3},{3,4},{4,5},{5,6},{6,7},{7,0},{8,15},{9,8},{10,9... | collective-permute-start | bytes 786440 | tf_op jit(solution)/shard_map/ppermute | solution.py:264
  33.6 24.1 %all-to-all-start.1 = ((bf16[64,16,128]{2,1,0:T(8,128)(2,1)}), bf16[64,16,128]{2,1,0:T(8,128)(2,1)S(1)}, u32[]{:S(2)}, u32[]{:S(2)}) async-start(bf16[64,16,128]{2,1,0:T(8,128)(2,1)} %bitcast.11), calls=%async_computation.1 | async-start | bytes 524288 | tf_op jit(solution)/shard_map/all_to_all | solution.py:306
  47.2 22.8 %collective-permute-start.3 = (bf16[256,1024]{1,0:T(8,128)(2,1)S(1)}, bf16[256,1024]{1,0:T(8,128)(2,1)S(1)}, u32[]{:S(2)}, u32[]{:S(2)}) collective-permute-start(bf16[256,1024]{1,0:T(8,128)(2,1)S(1)} %constant_dynamic-update-slice_fusion.next_ref), channel_id=1, source_target_pairs={{0,8},{8,0},{16,24},{24,16},{32,40},{40,32},{48,56},{56,48},{64,72... | collective-permute-start | bytes 1572872 | tf_op jit(solution)/shard_map/ppermute | solution.py:267
  49.3 20.7 %collective-permute-start.2 = (bf16[256,1024]{1,0:T(8,128)(2,1)S(1)}, bf16[256,1024]{1,0:T(8,128)(2,1)S(1)}, u32[]{:S(2)}, u32[]{:S(2)}) collective-permute-start(bf16[256,1024]{1,0:T(8,128)(2,1)S(1)} %constant_dynamic-update-slice_fusion.next_ref), channel_id=1, source_target_pairs={{0,2},{1,3},{2,4},{3,5},{4,6},{5,7},{6,0},{7,1},{8,14},{9,15},{10,... | collective-permute-start | bytes 1572872 | tf_op jit(solution)/shard_map/ppermute | solution.py:264
  53.6 16.4 %collective-permute-start.4 = (bf16[128,1024]{1,0:T(8,128)(2,1)}, bf16[128,1024]{1,0:T(8,128)(2,1)S(1)}, u32[]{:S(2)}, u32[]{:S(2)}) collective-permute-start(bf16[128,1024]{1,0:T(8,128)(2,1)} %collective-permute-done.1), channel_id=1, source_target_pairs={{0,9},{1,10},{2,11},{3,12},{4,13},{5,14},{6,15},{7,8},{8,7},{9,0},... | collective-permute-start | bytes 786440 | tf_op jit(solution)/shard_map/ppermute | solution.py:264
  57.8 17.2 %copy-start.1 = (bf16[512,1024]{1,0:T(8,128)(2,1)S(1)}, bf16[512,1024]{1,0:T(8,128)(2,1)}, u32[]{:S(2)}) copy-start(bf16[512,1024]{1,0:T(8,128)(2,1)} %tokens_ref.5) | copy-start | bytes 3145732
  60.6 14.4 %all-to-all-start.2 = ((bf16[8,64,128]{2,1,0:T(8,128)(2,1)}), bf16[8,64,128]{2,1,0:T(8,128)(2,1)S(1)}, u32[]{:S(2)}, u32[]{:S(2)}) async-start(bf16[8,64,128]{2,1,0:T(8,128)(2,1)} %bitcast.13), calls=%async_computation.2 | async-start | bytes 262144 | tf_op jit(solution)/shard_map/all_to_all | solution.py:325
